TPU v7x, 32 devices: a whole 2x2x4 slice. The times are simulated.
32 devices in a mesh: hi: 4 (over x, core), lo: 8 (over z, y).
Axes of the slice: x: 2, y: 2, z: 4, core: 2. Of those that a mesh axis runs over, the one named last changes fastest.
Arguments:
- design: float32 [65536, 512], P(('hi', 'lo')), may hold values from -40 to 40
- signs: int32 [65536], P(('hi', 'lo')), may hold values from 0 to 1
- samples: int32 [4096], P(('hi', 'lo')), may hold values from 0 to 65535, as said below
Outputs:
- sketch: float32 [4096, 512], P(('hi', 'lo'))
- gram: float32 [512, 512], P(('hi', 'lo'))
Inputs may be any that keep to these rules, and one draw needn't show every extreme that they name: `samples`: row indices into the whole design. Among the 128 entries owned by one device, at most 8 fall in the rows of any one device (rows p * 2048 to (p + 1) * 2048 - 1 for device p, devices in hi+lo order), and in every draw one device supplies exactly 8 to every owner. Likewise, among one owner's entries at most 8 have a local row (index modulo 2048) in any one range s * 64 to (s + 1) * 64 - 1, and for every owner one such range holds exactly 8.
All inputs are finite; a program needn't handle non-finite values.
Results may differ from a plain program's by a relative error of at most 0.00011.
Values sent between devices are 32-bit elements; how exact they have to be, the bound alone decides.
No kernel may reach another device: no remote copies, remote signals or barrier semaphores. Data moves between devices by JAX's collectives and lax.ppermute only.
A program may use at most 64 MiB of HBM per device.

v0:
```python
import math

import jax
import jax.numpy as jnp
from jax import lax
from jax.sharding import PartitionSpec as P


def from_partner(block, axis, stride):
    count = lax.axis_size(axis)
    route = []
    for low in range(count):
        high = low | 1 << stride
        if high != low and high < count:
            route += [(low, high), (high, low)]
    return lax.ppermute(block, axis, route)


def hadamard(order):
    row_ids = lax.broadcasted_iota(jnp.int32, (order, order), 0)
    col_ids = lax.broadcasted_iota(jnp.int32, (order, order), 1)
    common = row_ids & col_ids
    parity = jnp.zeros_like(common)
    for bit_number in range(max(order.bit_length() - 1, 1)):
        parity = parity ^ common >> bit_number & 1
    return (1 - 2 * parity).astype(jnp.float32)


def slot_rows(wanted, values, capacity):
    ranking = jnp.cumsum(wanted.astype(jnp.int32), axis=1) - 1
    slot_ids = jnp.arange(capacity, dtype=jnp.int32)
    picked = wanted[:, None, :] & (ranking[:, None, :] == slot_ids[None, :, None])
    which_row = jnp.sum(jnp.where(picked, values[:, None, :], 0), axis=2)
    filled = jnp.any(picked, axis=2)
    return (which_row, filled)


def slot_of(groups, capacity):
    positions = jnp.arange(groups.shape[0], dtype=jnp.int32)
    same_group = groups[:, None] == groups[None, :]
    earlier = jnp.sum(
        (same_group & (positions[None, :] < positions[:, None])).astype(jnp.int32), axis=1
    )
    return groups * capacity + earlier


def per_device(design, signs, samples):
    row_count = design.shape[0]
    col_count = design.shape[1]
    devices = lax.axis_size(("hi", "lo"))
    samp_count = samples.shape[0]
    capacity = max(2, 2 * samp_count // devices)
    own_index = lax.axis_index(("hi", "lo"))
    scale = 1.0 / math.sqrt(row_count * devices)
    every = lax.all_gather(samples, ("hi", "lo"), axis=0, tiled=True).reshape(devices, samp_count)
    source = every // row_count
    local_row = every % row_count
    flipped = design * (2 * signs - 1).astype(jnp.float32)[:, None]
    mixed = jnp.dot(
        hadamard(row_count),
        flipped,
        precision=lax.Precision.HIGHEST,
        preferred_element_type=jnp.float32,
    )
    for bit_number in range(lax.axis_size("lo").bit_length() - 1):
        partner = from_partner(mixed, "lo", bit_number)
        upper = lax.axis_index("lo") >> bit_number & 1
        mixed = jnp.where(upper == 1, partner - mixed, mixed + partner)
    for bit_number in range(lax.axis_size("hi").bit_length() - 1):
        partner = from_partner(mixed, "hi", bit_number)
        upper = lax.axis_index("hi") >> bit_number & 1
        mixed = jnp.where(upper == 1, partner - mixed, mixed + partner)
    mixed = mixed * scale
    which_row, filled = slot_rows(source == own_index, local_row, capacity)
    outgoing = jnp.where(filled[:, :, None], mixed[which_row], 0.0)
    arrived = lax.all_to_all(outgoing, ("hi", "lo"), split_axis=0, concat_axis=0, tiled=True)
    flat_index = slot_of(samples // row_count, capacity)
    sketch = arrived.reshape(devices * capacity, col_count)[flat_index]
    inverse_total = 1.0 / (samp_count * devices)
    product = lax.dot_general(
        sketch,
        sketch,
        (((0,), (0,)), ((), ())),
        precision=lax.Precision.HIGHEST,
        preferred_element_type=jnp.float32,
    )
    gram = lax.psum_scatter(product * inverse_total, ("hi", "lo"), scatter_dimension=0, tiled=True)
    return (sketch, gram)


def solution(mesh):
    placed = (P(("hi", "lo"), None), P(("hi", "lo")), P(("hi", "lo")))
    return jax.shard_map(
        per_device,
        mesh=mesh,
        in_specs=placed,
        out_specs=(P(("hi", "lo"), None), P(("hi", "lo"), None)),
        check_vma=False,
    )
```

profile of v0, /device:TPU:0, one launch (start us, length us, event | category | flops | bytes accessed | tf_op | source)
XLA Modules:
  0.0 926.8 jit_solution(10566649431912508214)
XLA Ops:
  7.2 0.7 add_convert_fusion
  7.9 2.5 fusion.79
  10.4 247.3 %fusion = f32[2048,512]{1,0:T(8,128)} fusion(f32[2048,512]{1,0:T(8,128)S(1)} %fusion.79), kind=kOutput, calls=%fused_computation.2 | convolution fusion | flops 25920798720 | bytes 8388608 | tf_op jit(solution)/shard_map/dot_general | solution.py:59
  257.7 3.0 collective-permute-start
  260.6 90.9 %collective-permute-done = f32[2048,512]{1,0:T(8,128)} collective-permute-done((f32[2048,512]{1,0:T(8,128)}, f32[2048,512]{1,0:T(8,128)}, u32[]{:S(2)}, u32[]{:S(2)}) %collective-permute-start) | collective-permute-done | bytes 4194336 | tf_op jit(solution)/shard_map/ppermute | solution.py:16
  351.5 6.5 add_select_fusion.3
  358.0 1.8 collective-permute-start.1
  359.8 90.3 %collective-permute-done.1 = f32[2048,512]{1,0:T(8,128)} collective-permute-done((f32[2048,512]{1,0:T(8,128)}, f32[2048,512]{1,0:T(8,128)}, u32[]{:S(2)}, u32[]{:S(2)}) %collective-permute-start.1) | collective-permute-done | bytes 4194336 | tf_op jit(solution)/shard_map/ppermute | solution.py:16
  450.1 6.5 add_select_fusion.2
  456.5 2.5 collective-permute-start.2
  459.0 179.4 %collective-permute-done.2 = f32[2048,512]{1,0:T(8,128)} collective-permute-done((f32[2048,512]{1,0:T(8,128)}, f32[2048,512]{1,0:T(8,128)}, u32[]{:S(2)}, u32[]{:S(2)}) %collective-permute-start.2) | collective-permute-done | bytes 4194336 | tf_op jit(solution)/shard_map/ppermute | solution.py:16
  638.5 6.5 add_select_fusion.1
  644.9 0.0 collective-permute-start.3
  644.9 0.0 copy-start.1
  644.9 7.5 collective-permute-done.3
  652.4 6.5 add_select_fusion
  658.9 1.1 collective-permute-start.4
  660.0 0.0 copy-done.1
  660.0 66.8 %all-gather = s32[32,1,128]{2,1,0:T(1,128)S(1)} all-gather(s32[1,1,128]{2,1,0:T(1,128)S(1)} %bitcast.15), channel_id=1, replica_groups=mesh['hi'=4,'lo'=8] {'hi','lo'}, dimensions={0}, use_global_device_ids=true | all-gather | bytes 16896 | tf_op jit(solution)/shard_map/all_gather | solution.py:55
  726.8 0.3 reduce_window_sum.11
  727.2 0.6 select_reduce_fusion
  727.8 0.1 reshape.117
  727.9 0.6 fusion.53
  728.5 23.3 %collective-permute-done.4 = f32[2048,512]{1,0:T(8,128)} collective-permute-done((f32[2048,512]{1,0:T(8,128)}, f32[2048,512]{1,0:T(8,128)}, u32[]{:S(2)}, u32[]{:S(2)}) %collective-permute-start.4) | collective-permute-done | bytes 4194336 | tf_op jit(solution)/shard_map/ppermute | solution.py:16
  751.9 6.5 select_multiply_fusion
  758.3 3.4 gather_fusion
  761.7 0.9 bitcast_select_fusion
  762.6 5.3 all-to-all-start
  767.9 0.0 reduce-scatter.2.cloned.1.call-start
  768.0 0.2 convert_reduce_fusion
  768.2 16.1 %all-to-all-done = f32[32,8,512]{2,1,0:T(8,128)S(1)} async-done(((f32[32,8,512]{2,1,0:T(8,128)}), f32[32,8,512]{2,1,0:T(8,128)S(1)}, u32[]{:S(2)}, u32[]{:S(2)}) %all-to-all-start) | async-done | bytes 524320 | tf_op jit(solution)/shard_map/all_to_all | solution.py:76
  784.3 0.8 gather_fusion.1
  785.1 0.0 copy-start
  785.1 2.0 convolution_multiply_fusion
  787.1 0.0 reduce-scatter.2.cloned.1.call-update
  787.1 132.8 %reduce-scatter.2.cloned.1.call-done = f32[16,512]{1,0:T(8,128)} async-done(((f32[512,512]{1,0:T(8,128)}), f32[16,512]{1,0:T(8,128)}) %reduce-scatter.2.cloned.1.call-update) | async-done | bytes 32784 | tf_op jit(solution)/shard_map/reduce_scatter | solution.py:87
  919.9 0.0 copy-done
  (8 shorter events, 0.1 us)
Async XLA Ops:
  257.7 93.8 %collective-permute-start = (f32[2048,512]{1,0:T(8,128)}, f32[2048,512]{1,0:T(8,128)}, u32[]{:S(2)}, u32[]{:S(2)}) collective-permute-start(f32[2048,512]{1,0:T(8,128)} %fusion), channel_id=1, source_target_pairs={{0,1},{1,0},{2,3},{3,2},{4,5},{5,4},{6,7},{7,6},{8,9},{9,8},{10,11... | collective-permute-start | bytes 12582920 | tf_op jit(solution)/shard_map/ppermute | solution.py:16
  358.0 92.1 %collective-permute-start.1 = (f32[2048,512]{1,0:T(8,128)}, f32[2048,512]{1,0:T(8,128)}, u32[]{:S(2)}, u32[]{:S(2)}) collective-permute-start(f32[2048,512]{1,0:T(8,128)} %add_select_fusion.3), channel_id=1, source_target_pairs={{0,2},{2,0},{1,3},{3,1},{4,6},{6,4},{5,7},{7,5},{8,10},{10,8},{9,1... | collective-permute-start | bytes 12582920 | tf_op jit(solution)/shard_map/ppermute | solution.py:16
  456.5 181.9 %collective-permute-start.2 = (f32[2048,512]{1,0:T(8,128)}, f32[2048,512]{1,0:T(8,128)}, u32[]{:S(2)}, u32[]{:S(2)}) collective-permute-start(f32[2048,512]{1,0:T(8,128)} %add_select_fusion.2), channel_id=1, source_target_pairs={{0,4},{4,0},{1,5},{5,1},{2,6},{6,2},{3,7},{7,3},{8,12},{12,8},{9,1... | collective-permute-start | bytes 12582920 | tf_op jit(solution)/shard_map/ppermute | solution.py:16
  644.9 7.5 collective-permute-start.3
  644.9 15.1 %copy-start.1 = (s32[128]{0:T(128)S(1)}, s32[128]{0:T(128)}, u32[]{:S(2)}) copy-start(s32[128]{0:T(128)} %param.5) | copy-start | bytes 1540
  658.9 92.9 %collective-permute-start.4 = (f32[2048,512]{1,0:T(8,128)}, f32[2048,512]{1,0:T(8,128)}, u32[]{:S(2)}, u32[]{:S(2)}) collective-permute-start(f32[2048,512]{1,0:T(8,128)} %add_select_fusion), channel_id=1, source_target_pairs={{0,16},{16,0},{8,24},{24,8},{1,17},{17,1},{9,25},{25,9},{2,18},{18... | collective-permute-start | bytes 12582920 | tf_op jit(solution)/shard_map/ppermute | solution.py:16
  762.6 21.7 %all-to-all-start = ((f32[32,8,512]{2,1,0:T(8,128)}), f32[32,8,512]{2,1,0:T(8,128)S(1)}, u32[]{:S(2)}, u32[]{:S(2)}) async-start(f32[32,8,512]{2,1,0:T(8,128)} %bitcast_select_fusion), calls=%async_computation | async-start | bytes 1048576 | tf_op jit(solution)/shard_map/all_to_all | solution.py:76
  767.9 152.0 %reduce-scatter.2.cloned.1.call-start = ((), (), s32[]{:S(2)}) async-start(), calls=%async_computation.2 | async-start | bytes 1081344 | tf_op jit(solution)/shard_map/reduce_scatter | solution.py:87
  785.1 134.9 %copy-start = (f32[128,512]{1,0:T(8,128)}, f32[128,512]{1,0:T(8,128)S(1)}, u32[]{:S(2)}) copy-start(f32[128,512]{1,0:T(8,128)S(1)} %gather_fusion.1) | copy-start | bytes 786436
Sparse Core Ops, SparseCore 0:
  787.2 132.6 reduce-scatter.1
where the time goes:
time: 927 us
  waiting for transfers between devices  540 us (58%)
  matrix products  249 us (27%)
  blocking collectives  66.8 us (7%)
  other arithmetic  38.3 us (4%)
  between operations  14.1 us (2%)
  starting transfers between devices  13.7 us (1%)
    ppermute x5, waiting for transfers between devices, from_partner(): return lax.ppermute(block, axis, route)  391 us
    dot_general x1, matrix products, per_device(): jnp.dot(hadamard(row_count), flipped, precision=lax.Precision.HIGHEST, pr...  247 us
    reduce_scatter x1, waiting for transfers between devices, per_device(): lax.psum_scatter(product * inverse_total, ('hi', 'lo'), scatter_dimension...  133 us
    all_gather x1, blocking collectives, per_device(): lax.all_gather(samples, ('hi', 'lo'), axis=0, tiled=True)  66.8 us
    select_n x4, other arithmetic, per_device(): mixed = jnp.where(upper == 1, partner - mixed, mixed + partner)  25.9 us
  transfers between devices with their start and end apart: 7, of which 7 were waited for; matrix products, arithmetic and copies ran while one was open for 0% of the time, Pallas kernels for 0%

commit v1 on v0

v1 whole, which is shorter than its diff:
```python
import functools
import math

import jax
import jax.numpy as jnp
from jax import lax
from jax.experimental import pallas as pl
from jax.experimental.pallas import tpu as pltpu
from jax.sharding import Mesh, PartitionSpec as P

VMEM = pl.BlockSpec(memory_space=pltpu.VMEM)
SMEM = pl.BlockSpec(memory_space=pltpu.SMEM)
LIMIT = pltpu.CompilerParams(vmem_limit_bytes=48 * 1024 * 1024)
BLOCK = 256
LANES = 128


def walsh(values):
    half = 1
    while half < len(values):
        out = list(values)
        for i in range(len(values)):
            if not i & half:
                out[i] = values[i] + values[i | half]
                out[i | half] = values[i] - values[i | half]
        values = out
        half *= 2
    return values


def transform_kernel(own_ref, oth_ref, own_sign_ref, oth_sign_ref, mixed_ref, part_ref):
    rows, cols = own_ref.shape
    blocks, tiles = rows // BLOCK, cols // LANES
    common = lax.broadcasted_iota(jnp.int32, (BLOCK, BLOCK), 0) & lax.broadcasted_iota(
        jnp.int32, (BLOCK, BLOCK), 1
    )
    for shift in (4, 2, 1):
        common = common ^ (common >> shift)
    had = (1 - 2 * (common & 1)).astype(jnp.float32)

    for which, (ref, sign_ref) in enumerate(((own_ref, own_sign_ref), (oth_ref, oth_sign_ref))):

        def one_block(b, carry, ref=ref, sign_ref=sign_ref, which=which):
            left = (had * sign_ref[pl.ds(b, 1), :]).astype(jnp.bfloat16)
            full = ref[pl.ds(pl.multiple_of(b * BLOCK, BLOCK), BLOCK), :]
            high = full.astype(jnp.bfloat16)
            low = (full - high.astype(jnp.float32)).astype(jnp.bfloat16)
            part_ref[which, b] = jnp.dot(
                left, high, preferred_element_type=jnp.float32
            ) + jnp.dot(left, low, preferred_element_type=jnp.float32)
            return carry

        lax.fori_loop(0, blocks, one_block, 0)

    def one_chunk(chunk, carry):
        start = pl.multiple_of(chunk * 8, 8)
        for tile in range(tiles):
            lanes = slice(tile * LANES, (tile + 1) * LANES)
            own = walsh([part_ref[0, b, pl.ds(start, 8), lanes] for b in range(blocks)])
            oth = walsh([part_ref[1, b, pl.ds(start, 8), lanes] for b in range(blocks)])
            for b in range(blocks):
                both = (own[b] + oth[b], own[b] - oth[b])
                for core in range(2):
                    for negative in range(2):
                        row = (negative * 2 + core) * rows + b * BLOCK + start
                        mixed_ref[pl.ds(row * tiles + tile, 8, stride=tiles), :] = (
                            -both[core] if negative else both[core]
                        )
        return carry

    lax.fori_loop(0, BLOCK // 8, one_chunk, 0)


def transform(own, oth, own_sign, oth_sign):
    rows, cols = own.shape
    return pl.pallas_call(
        transform_kernel,
        out_shape=jax.ShapeDtypeStruct((4 * rows * cols // LANES, LANES), jnp.float32),
        in_specs=[VMEM] * 4,
        out_specs=VMEM,
        scratch_shapes=[pltpu.VMEM((2, rows // BLOCK, BLOCK, cols), jnp.float32)],
        compiler_params=LIMIT,
        cost_estimate=pl.CostEstimate(
            flops=4 * rows * BLOCK * cols * 2, bytes_accessed=6 * rows * cols * 4, transcendentals=0
        ),
    )(own, oth, own_sign, oth_sign)


def gather_kernel(plans, tiles, code_ref, mixed_ref, *out_refs):
    for out_ref, (starts, count) in zip(out_refs, plans):
        for place, start in enumerate(starts):

            def one(i, carry, out_ref=out_ref, place=place, start=start, count=count):
                code = code_ref[start + i]
                out_ref[pl.ds((place * count + i) * tiles, tiles), :] = mixed_ref[
                    pl.ds(pl.multiple_of(code * tiles, tiles), tiles), :
                ]
                return carry

            lax.fori_loop(0, count, one, 0, unroll=4)


def gather(plans, tiles, code, mixed):
    total = sum(len(starts) * count for starts, count in plans)
    return pl.pallas_call(
        functools.partial(gather_kernel, plans, tiles),
        out_shape=[
            jax.ShapeDtypeStruct((len(starts) * count * tiles, LANES), jnp.float32)
            for starts, count in plans
        ],
        in_specs=[SMEM, VMEM],
        out_specs=[VMEM] * len(plans),
        compiler_params=LIMIT,
        cost_estimate=pl.CostEstimate(
            flops=0, bytes_accessed=8 * total * tiles * LANES, transcendentals=0
        ),
    )(code, mixed)


def gram_kernel(scale, inverse_total, core_ref, own_ref, oth_ref, sketch_ref, gram_ref, both_ref):
    samp, cols = sketch_ref.shape
    tiles = cols // LANES
    for tile in range(tiles):
        lanes = slice(tile * LANES, (tile + 1) * LANES)
        mine = own_ref[pl.ds(tile, samp, stride=tiles), :] * scale
        sketch_ref[:, lanes] = mine
        both_ref[:samp, lanes] = mine
        both_ref[samp:, lanes] = oth_ref[pl.ds(tile, samp, stride=tiles), :] * scale
    rows = gram_ref.shape[0]
    width = cols * rows // cols // 2
    for upper in range(2):
        start = pl.multiple_of(upper * (cols // 2) + core_ref[0] * width, LANES)
        gram_ref[upper * width : (upper + 1) * width, :] = (
            lax.dot_general(
                both_ref[:, pl.ds(start, width)],
                both_ref[...],
                (((0,), (0,)), ((), ())),
                precision=lax.Precision.HIGHEST,
                preferred_element_type=jnp.float32,
            )
            * inverse_total
        )


def swap(block, bit):
    return lax.ppermute(block, bit, [(0, 1), (1, 0)])


def per_device(bits, design, signs, samples):
    rows, cols = design.shape
    samp = samples.shape[0]
    tiles = cols // LANES
    devices = 2 ** len(bits)
    high, core, low = bits[0], bits[1], bits[:1:-1]
    steps = [high, *low]
    own_index = lax.axis_index(tuple(bits))
    core_bit = len(low)

    oth_design = swap(design, core)
    oth_signs = swap(signs, core)
    listed = samples
    for bit in steps:
        listed = jnp.concatenate([listed, swap(listed, bit)])

    sign_rows = [(2 * s - 1).astype(jnp.float32).reshape(rows // BLOCK, BLOCK) for s in (signs, oth_signs)]
    mixed = transform(design, oth_design, *sign_rows)

    source = listed // rows
    parity = source & own_index
    shift = 1
    while shift < devices:
        parity = parity ^ (parity >> shift)
        shift *= 2
    code = ((parity & 1) * 2 + (source >> core_bit & 1)) * rows + listed % rows

    third = (samp // 3 + 2) // 2 * 2
    counts = [third, third, samp - 2 * third]
    owners = devices // 2
    orders = []
    for part in range(3):
        order = [(part + i) % 3 for i in range(3)]
        orders.append(order + list(range(3, len(steps))))

    def starts(part, first):
        order = orders[part]
        found = []
        for place in range(owners // 2):
            owner = first << order[0]
            for level, bit in enumerate(order[1:]):
                owner |= (place >> (len(order) - 2 - level) & 1) << bit
            found.append(owner * samp + sum(counts[:part]))
        return found, counts[part]

    sent = [gather([starts(part, 1)], tiles, code, mixed)[0] for part in range(3)]
    arrived = [swap(sent[part], steps[part]) for part in range(3)]
    held = gather([starts(part, 0) for part in range(3)], tiles, code, mixed)
    for level in range(1, 3):
        sends, keeps = [], []
        for part in range(3):
            half = held[part].shape[0] // 2
            keeps.append(held[part][:half] + arrived[part][:half])
            sends.append(held[part][half:] + arrived[part][half:])
        arrived = [swap(sends[part], steps[orders[part][level]]) for part in range(3)]
        held = keeps
    pieces = [held[part] + arrived[part] for part in range(3)]
    pieces = [p.reshape(-1, counts[i] * tiles, LANES) for i, p in enumerate(pieces)]
    whole = jnp.concatenate(pieces, axis=1)
    for level in range(3, len(steps)):
        half = whole.shape[0] // 2
        whole = whole[:half] + swap(whole[half:], steps[level])
    own_sum = whole[0]
    oth_sum = swap(own_sum, core)

    half_rows = cols // 2
    sketch, product = pl.pallas_call(
        functools.partial(gram_kernel, 1.0 / math.sqrt(rows * devices), 1.0 / (samp * devices)),
        out_shape=[
            jax.ShapeDtypeStruct((samp, cols), jnp.float32),
            jax.ShapeDtypeStruct((half_rows, cols), jnp.float32),
        ],
        in_specs=[SMEM, VMEM, VMEM],
        out_specs=[VMEM, VMEM],
        scratch_shapes=[pltpu.VMEM((2 * samp, cols), jnp.float32)],
        compiler_params=LIMIT,
    )(lax.axis_index(core).astype(jnp.int32).reshape(1), own_sum, oth_sum)

    gathered = lax.all_to_all(product, (high, *reversed(low)), split_axis=0, concat_axis=0, tiled=True)
    gram = jnp.sum(gathered.reshape(owners, cols // devices, cols), axis=0)
    return sketch, gram


def solution(mesh):
    width = [size.bit_length() - 1 for size in mesh.devices.shape]
    bits = [f"{axis}{i}" for axis, w in zip(mesh.axis_names, width) for i in reversed(range(w))]
    split = Mesh(mesh.devices.reshape((2,) * len(bits)), tuple(bits))
    every = tuple(bits)
    return jax.shard_map(
        functools.partial(per_device, bits),
        mesh=split,
        in_specs=(P(every, None), P(every), P(every)),
        out_specs=(P(every, None), P(every, None)),
        check_vma=False,
    )
```

time: 927 us -> 129 us (0.14)
  waiting for transfers between devices: 540 us -> 31.7 us
  matrix products: 249 us -> 0 us
  blocking collectives: 66.8 us -> 21.4 us
  Pallas kernels: 0 us -> 44.6 us
  other arithmetic: 38.3 us -> 3.83 us
  between operations: 14.1 us -> 0.79 us
  starting transfers between devices: 13.7 us -> 23.1 us
    ppermute x5 -> x17, waiting for transfers between devices: 391 us -> 31.7 us  [swap(): return lax.ppermute(block, bit, [(0, 1), (1, 0)])]
    dot_general x2 -> x0, matrix products: 249 us -> none  [the longest x1 247 us: per_device(): jnp.dot(hadamard(row_count), flipped, precision=lax.Precision.HIGHEST, pr...]
    reduce_scatter x1 -> x0, waiting for transfers between devices: 133 us -> none  [per_device(): lax.psum_scatter(product * inverse_total, ('hi', 'lo'), scatter_dimension...]
    all_gather x1 -> x0, blocking collectives: 66.8 us -> none  [per_device(): lax.all_gather(samples, ('hi', 'lo'), axis=0, tiled=True)]
    pallas_call x0 -> x6, Pallas kernels: none -> 44.6 us  [the longest x4 27.7 us: gather(): pl.pallas_call(functools.partial(gather_kernel, plans, tiles), out_shape=...]
    select_n x9 -> x0, other arithmetic: 26.8 us -> none  [the longest x4 25.9 us: per_device(): mixed = jnp.where(upper == 1, partner - mixed, mixed + partner)]
    all_to_all x0 -> x1, blocking collectives: none -> 21.4 us  [per_device(): lax.all_to_all(product, (high, *reversed(low)), split_axis=0, concat_axis...]
    all_to_all x1 -> x0, waiting for transfers between devices: 16.1 us -> none  [per_device(): lax.all_to_all(outgoing, ('hi', 'lo'), split_axis=0, concat_axis=0, tiled...]
  transfers between devices with their start and end apart: 7 -> 17, of which waited for: 7 -> 11; matrix products, arithmetic and copies ran while one was open for 0% -> 3% of each run, Pallas kernels for 0% -> 17%
where the time goes in v1:
time: 129 us; the launch traced here: 128 us
  Pallas kernels  44.6 us (35%)
  waiting for transfers between devices  31.7 us (25%)
  starting transfers between devices  23.1 us (18%)
  blocking collectives  21.4 us (17%)
  other arithmetic  3.83 us (3%)
  local copies, waits for them, and re-layouts  2.89 us (2%)
    ppermute x17, waiting for transfers between devices, swap(): return lax.ppermute(block, bit, [(0, 1), (1, 0)])  31.7 us
    pallas_call x4, Pallas kernels, gather(): pl.pallas_call(functools.partial(gather_kernel, plans, tiles), out_shape=...  27.7 us
    ppermute x17, starting transfers between devices, swap(): return lax.ppermute(block, bit, [(0, 1), (1, 0)])  23.1 us
    all_to_all x1, blocking collectives, per_device(): lax.all_to_all(product, (high, *reversed(low)), split_axis=0, concat_axis...  21.4 us
    pallas_call x1, Pallas kernels, transform(): pl.pallas_call(transform_kernel, out_shape=jax.ShapeDtypeStruct((4 * rows...  16.1 us
    unnamed x6, local copies, waits for them, and re-layouts  2.86 us
  transfers between devices with their start and end apart: 17, of which 11 were waited for; matrix products, arithmetic and copies ran while one was open for 3% of the time, Pallas kernels for 17%

profile of v1, /device:TPU:0, one launch (start us, length us, event | category | flops | bytes accessed | tf_op | source)
XLA Modules:
  0.0 128.3 jit_solution(6873972164965705829)
XLA Ops:
  0.6 0.5 collective-permute-start.4
  1.1 2.6 %collective-permute-start = (s32[128]{0:T(128)}, s32[128]{0:T(128)S(1)}, u32[]{:S(2)}, u32[]{:S(2)}) collective-permute-start(s32[128]{0:T(128)} %param.5), channel_id=1, source_target_pairs={{0,16},{16,0},{1,17},{17,1},{2,18},{18,2},{3,19},{19,3},{4,20},{20... | collective-permute-start | bytes 1544 | tf_op jit(solution)/shard_map/ppermute | solution.py:146
  3.7 0.2 collective-permute-start.5
  3.9 0.7 add_convert_fusion.1
  4.6 0.7 constant_dynamic-update-slice_fusion.4
  5.2 0.1 collective-permute-done
  5.4 0.7 pad_add_fusion.2
  6.0 2.0 %collective-permute-start.1 = (s32[256]{0:T(256)S(1)}, s32[256]{0:T(256)S(1)}, u32[]{:S(2)}, u32[]{:S(2)}) collective-permute-start(s32[256]{0:T(256)S(1)} %pad_add_fusion.2), channel_id=1, source_target_pairs={{0,1},{1,0},{2,3},{3,2},{4,5},{5,4},{6,7},{7,6},{8,9},{9,8},{10,11... | collective-permute-start | bytes 3080 | tf_op jit(solution)/shard_map/ppermute | solution.py:146
  8.1 1.5 %collective-permute-done.1 = s32[256]{0:T(256)S(1)} collective-permute-done((s32[256]{0:T(256)S(1)}, s32[256]{0:T(256)S(1)}, u32[]{:S(2)}, u32[]{:S(2)}) %collective-permute-start.1) | collective-permute-done | bytes 1056 | tf_op jit(solution)/shard_map/ppermute | solution.py:146
  9.6 0.7 pad_add_fusion.1
  10.3 2.1 %collective-permute-start.2 = (s32[512]{0:T(512)S(1)}, s32[512]{0:T(512)S(1)}, u32[]{:S(2)}, u32[]{:S(2)}) collective-permute-start(s32[512]{0:T(512)S(1)} %pad_add_fusion.1), channel_id=1, source_target_pairs={{0,2},{2,0},{1,3},{3,1},{4,6},{6,4},{5,7},{7,5},{8,10},{10,8},{9,1... | collective-permute-start | bytes 6152 | tf_op jit(solution)/shard_map/ppermute | solution.py:146
  12.4 1.6 %collective-permute-done.2 = s32[512]{0:T(512)S(1)} collective-permute-done((s32[512]{0:T(512)S(1)}, s32[512]{0:T(512)S(1)}, u32[]{:S(2)}, u32[]{:S(2)}) %collective-permute-start.2) | collective-permute-done | bytes 2080 | tf_op jit(solution)/shard_map/ppermute | solution.py:146
  13.9 0.7 pad_add_fusion
  14.6 3.0 %collective-permute-start.3 = (s32[1024]{0:T(1024)S(1)}, s32[1024]{0:T(1024)S(1)}, u32[]{:S(2)}, u32[]{:S(2)}) collective-permute-start(s32[1024]{0:T(1024)S(1)} %pad_add_fusion), channel_id=1, source_target_pairs={{0,4},{4,0},{1,5},{5,1},{2,6},{6,2},{3,7},{7,3},{8,12},{12,8},{9,1... | collective-permute-start | bytes 12296 | tf_op jit(solution)/shard_map/ppermute | solution.py:146
  17.6 1.6 %collective-permute-done.3 = s32[1024]{0:T(1024)S(1)} collective-permute-done((s32[1024]{0:T(1024)S(1)}, s32[1024]{0:T(1024)S(1)}, u32[]{:S(2)}, u32[]{:S(2)}) %collective-permute-start.3) | collective-permute-done | bytes 4128 | tf_op jit(solution)/shard_map/ppermute | solution.py:146
  19.3 0.0 collective-permute-done.5
  19.3 0.0 collective-permute-done.4.oth_ref
  19.3 0.0 copy-start
  19.3 2.2 %copy-done = f32[2048,512]{1,0:T(8,128)S(1)} copy-done((f32[2048,512]{1,0:T(8,128)S(1)}, f32[2048,512]{1,0:T(8,128)}, u32[]{:S(2)}) %copy-start) | copy-done | bytes 4194328
  21.5 16.1 %shard_map.50.mixed_ref = f32[32768,128]{1,0:T(8,128)} custom-call(f32[2048,512]{1,0:T(8,128)S(1)} %copy-done, f32[2048,512]{1,0:T(8,128)} %collective-permute-done.4.oth_ref, f32[8,256]{1,0:T(8,128)S(1)} %reshape.27.own_sign_ref, f32[8,256]{1,0:T(8,128)S(1)} %reshape.28.oth_sign_ref), custom_call_target="tpu_custom_call" | custom-call | flops 2147483648 | bytes 25165824 | tf_op jit(solution)/shard_map/pallas_call | solution.py:76
  37.5 6.5 %shard_map.54 = f32[1280,128]{1,0:T(8,128)S(1)} custom-call(s32[2048]{0:T(1024)S(1)} %fusion.8.code_ref, f32[32768,128]{1,0:T(8,128)} %shard_map.50.mixed_ref), custom_call_target="tpu_custom_call" | custom-call | bytes 1310720 | tf_op jit(solution)/shard_map/pallas_call | solution.py:105
  44.0 2.0 %collective-permute-start.12 = (f32[1280,128]{1,0:T(8,128)S(1)}, f32[1280,128]{1,0:T(8,128)S(1)}, u32[]{:S(2)}, u32[]{:S(2)}) collective-permute-start(f32[1280,128]{1,0:T(8,128)S(1)} %shard_map.54), channel_id=1, source_target_pairs={{0,2},{2,0},{1,3},{3,1},{4,6},{6,4},{5,7},{7,5},{8,10},{10,8},{9,1... | collective-permute-start | bytes 1966088 | tf_op jit(solution)/shard_map/ppermute | solution.py:146
  46.0 6.6 %shard_map.52 = f32[1408,128]{1,0:T(8,128)S(1)} custom-call(s32[2048]{0:T(1024)S(1)} %fusion.8.code_ref, f32[32768,128]{1,0:T(8,128)} %shard_map.50.mixed_ref), custom_call_target="tpu_custom_call" | custom-call | bytes 1441792 | tf_op jit(solution)/shard_map/pallas_call | solution.py:105
  52.6 1.6 %collective-permute-start.6 = (f32[1408,128]{1,0:T(8,128)S(1)}, f32[1408,128]{1,0:T(8,128)S(1)}, u32[]{:S(2)}, u32[]{:S(2)}) collective-permute-start(f32[1408,128]{1,0:T(8,128)S(1)} %shard_map.52), channel_id=1, source_target_pairs={{0,16},{16,0},{1,17},{17,1},{2,18},{18,2},{3,19},{19,3},{4,20},{20... | collective-permute-start | bytes 2162696 | tf_op jit(solution)/shard_map/ppermute | solution.py:146
  54.1 6.6 %shard_map.53 = f32[1408,128]{1,0:T(8,128)S(1)} custom-call(s32[2048]{0:T(1024)S(1)} %fusion.8.code_ref, f32[32768,128]{1,0:T(8,128)} %shard_map.50.mixed_ref), custom_call_target="tpu_custom_call" | custom-call | bytes 1441792 | tf_op jit(solution)/shard_map/pallas_call | solution.py:105
  60.7 1.6 %collective-permute-start.9 = (f32[1408,128]{1,0:T(8,128)S(1)}, f32[1408,128]{1,0:T(8,128)S(1)}, u32[]{:S(2)}, u32[]{:S(2)}) collective-permute-start(f32[1408,128]{1,0:T(8,128)S(1)} %shard_map.53), channel_id=1, source_target_pairs={{0,1},{1,0},{2,3},{3,2},{4,5},{5,4},{6,7},{7,6},{8,9},{9,8},{10,11... | collective-permute-start | bytes 2162696 | tf_op jit(solution)/shard_map/ppermute | solution.py:146
  62.3 8.1 %shard_map.51 = (f32[1408,128]{1,0:T(8,128)S(1)}, f32[1408,128]{1,0:T(8,128)S(1)}, f32[1280,128]{1,0:T(8,128)S(1)}) custom-call(s32[2048]{0:T(1024)S(1)} %fusion.8.code_ref, f32[32768,128]{1,0:T(8,128)} %shard_map.50.mixed_ref), custom_call_target="tpu_custom_call" | custom-call | bytes 4194304 | tf_op jit(solution)/shard_map/pallas_call | solution.py:105
  70.4 0.0 collective-permute-done.12
  70.4 0.1 slice_add_fusion.5
  70.4 0.6 collective-permute-start.13
  71.0 0.0 collective-permute-done.6
  71.0 0.1 slice_add_fusion.3
  71.1 0.6 collective-permute-start.7
  71.7 7.5 %collective-permute-done.9 = f32[1408,128]{1,0:T(8,128)S(1)} collective-permute-done((f32[1408,128]{1,0:T(8,128)S(1)}, f32[1408,128]{1,0:T(8,128)S(1)}, u32[]{:S(2)}, u32[]{:S(2)}) %collective-permute-start.9) | collective-permute-done | bytes 720928 | tf_op jit(solution)/shard_map/ppermute | solution.py:146
  79.2 0.1 slice_add_fusion.1
  79.3 0.5 collective-permute-start.10
  79.8 0.0 collective-permute-done.13
  79.8 2.1 %collective-permute-start.14 = (f32[320,128]{1,0:T(8,128)S(1)}, f32[320,128]{1,0:T(8,128)S(1)}, u32[]{:S(2)}, u32[]{:S(2)}) collective-permute-start(f32[320,128]{1,0:T(8,128)S(1)} %slice_add_fusion.11), channel_id=1, source_target_pairs={{0,1},{1,0},{2,3},{3,2},{4,5},{5,4},{6,7},{7,6},{8,9},{9,8},{10,11... | collective-permute-start | bytes 491528 | tf_op jit(solution)/shard_map/ppermute | solution.py:146
  81.9 1.7 %collective-permute-done.7 = f32[704,128]{1,0:T(8,128)S(1)} collective-permute-done((f32[704,128]{1,0:T(8,128)S(1)}, f32[704,128]{1,0:T(8,128)S(1)}, u32[]{:S(2)}, u32[]{:S(2)}) %collective-permute-start.7) | collective-permute-done | bytes 360480 | tf_op jit(solution)/shard_map/ppermute | solution.py:146
  83.6 0.5 collective-permute-start.8
  84.1 5.0 %collective-permute-done.10 = f32[704,128]{1,0:T(8,128)S(1)} collective-permute-done((f32[704,128]{1,0:T(8,128)S(1)}, f32[704,128]{1,0:T(8,128)S(1)}, u32[]{:S(2)}, u32[]{:S(2)}) %collective-permute-start.10) | collective-permute-done | bytes 360480 | tf_op jit(solution)/shard_map/ppermute | solution.py:146
  89.1 0.6 collective-permute-start.11
  89.8 0.0 collective-permute-done.14
  89.8 1.7 %collective-permute-done.8 = f32[352,128]{1,0:T(8,128)S(1)} collective-permute-done((f32[352,128]{1,0:T(8,128)S(1)}, f32[352,128]{1,0:T(8,128)S(1)}, u32[]{:S(2)}, u32[]{:S(2)}) %collective-permute-start.8) | collective-permute-done | bytes 180256 | tf_op jit(solution)/shard_map/ppermute | solution.py:146
  91.6 3.1 %collective-permute-done.11 = f32[352,128]{1,0:T(8,128)S(1)} collective-permute-done((f32[352,128]{1,0:T(8,128)S(1)}, f32[352,128]{1,0:T(8,128)S(1)}, u32[]{:S(2)}, u32[]{:S(2)}) %collective-permute-start.11) | collective-permute-done | bytes 180256 | tf_op jit(solution)/shard_map/ppermute | solution.py:146
  94.8 2.6 %collective-permute-start.15 = (f32[1,512,128]{2,1,0:T(8,128)S(1)}, f32[1,512,128]{2,1,0:T(8,128)S(1)}, u32[]{:S(2)}, u32[]{:S(2)}) collective-permute-start(f32[1,512,128]{2,1,0:T(8,128)S(1)} %slice.123), channel_id=1, source_target_pairs={{0,4},{4,0},{1,5},{5,1},{2,6},{6,2},{3,7},{7,3},{8,12},{12,8},{9,1... | collective-permute-start | bytes 786440 | tf_op jit(solution)/shard_map/ppermute | solution.py:146
  97.4 6.4 %collective-permute-done.15 = f32[1,512,128]{2,1,0:T(8,128)S(1)} collective-permute-done((f32[1,512,128]{2,1,0:T(8,128)S(1)}, f32[1,512,128]{2,1,0:T(8,128)S(1)}, u32[]{:S(2)}, u32[]{:S(2)}) %collective-permute-start.15) | collective-permute-done | bytes 262176 | tf_op jit(solution)/shard_map/ppermute | solution.py:146
  103.8 0.1 collective-permute-start.16
  103.9 1.5 %collective-permute-done.16.oth_ref = f32[512,128]{1,0:T(8,128)S(1)} collective-permute-done((f32[512,128]{1,0:T(8,128)S(1)}, f32[512,128]{1,0:T(8,128)S(1)}, u32[]{:S(2)}, u32[]{:S(2)}) %collective-permute-start.16) | collective-permute-done | bytes 262176 | tf_op jit(solution)/shard_map/ppermute | solution.py:146
  105.4 0.9 shard_map.55
  106.3 21.4 %all_to_all.9 = f32[16,16,512]{2,1,0:T(8,128)S(1)} all-to-all(f32[16,16,512]{2,1,0:T(8,128)S(1)} %bitcast.7), channel_id=1, replica_groups=mesh['hi1'=2,'hi0'=2,'lo2'=2,'lo1'=2,'lo0'=2] {'hi1','lo2','lo1','lo0'}, dimensions={0} | all-to-all | bytes 1048576 | tf_op jit(solution)/shard_map/all_to_all | solution.py:227
  127.7 0.6 reduce_sum.9
  (18 shorter events, 0.3 us)
Async XLA Ops:
  0.6 18.7 %collective-permute-start.4 = (f32[2048,512]{1,0:T(8,128)}, f32[2048,512]{1,0:T(8,128)}, u32[]{:S(2)}, u32[]{:S(2)}) collective-permute-start(f32[2048,512]{1,0:T(8,128)} %own_ref.1), channel_id=1, source_target_pairs={{0,8},{8,0},{1,9},{9,1},{2,10},{10,2},{3,11},{11,3},{4,12},{12,4},... | collective-permute-start | bytes 12582920 | tf_op jit(solution)/shard_map/ppermute | solution.py:146
  1.1 4.2 %collective-permute-start = (s32[128]{0:T(128)}, s32[128]{0:T(128)S(1)}, u32[]{:S(2)}, u32[]{:S(2)}) collective-permute-start(s32[128]{0:T(128)} %param.5), channel_id=1, source_target_pairs={{0,16},{16,0},{1,17},{17,1},{2,18},{18,2},{3,19},{19,3},{4,20},{20... | collective-permute-start | bytes 1544 | tf_op jit(solution)/shard_map/ppermute | solution.py:146
  3.7 15.5 %collective-permute-start.5 = (s32[2048]{0:T(1024)}, s32[2048]{0:T(1024)S(1)}, u32[]{:S(2)}, u32[]{:S(2)}) collective-permute-start(s32[2048]{0:T(1024)} %param.4), channel_id=1, source_target_pairs={{0,8},{8,0},{1,9},{9,1},{2,10},{10,2},{3,11},{11,3},{4,12},{12,4},... | collective-permute-start | bytes 24584 | tf_op jit(solution)/shard_map/ppermute | solution.py:146
  6.0 3.6 %collective-permute-start.1 = (s32[256]{0:T(256)S(1)}, s32[256]{0:T(256)S(1)}, u32[]{:S(2)}, u32[]{:S(2)}) collective-permute-start(s32[256]{0:T(256)S(1)} %pad_add_fusion.2), channel_id=1, source_target_pairs={{0,1},{1,0},{2,3},{3,2},{4,5},{5,4},{6,7},{7,6},{8,9},{9,8},{10,11... | collective-permute-start | bytes 3080 | tf_op jit(solution)/shard_map/ppermute | solution.py:146
  10.3 3.6 %collective-permute-start.2 = (s32[512]{0:T(512)S(1)}, s32[512]{0:T(512)S(1)}, u32[]{:S(2)}, u32[]{:S(2)}) collective-permute-start(s32[512]{0:T(512)S(1)} %pad_add_fusion.1), channel_id=1, source_target_pairs={{0,2},{2,0},{1,3},{3,1},{4,6},{6,4},{5,7},{7,5},{8,10},{10,8},{9,1... | collective-permute-start | bytes 6152 | tf_op jit(solution)/shard_map/ppermute | solution.py:146
  14.6 4.6 %collective-permute-start.3 = (s32[1024]{0:T(1024)S(1)}, s32[1024]{0:T(1024)S(1)}, u32[]{:S(2)}, u32[]{:S(2)}) collective-permute-start(s32[1024]{0:T(1024)S(1)} %pad_add_fusion), channel_id=1, source_target_pairs={{0,4},{4,0},{1,5},{5,1},{2,6},{6,2},{3,7},{7,3},{8,12},{12,8},{9,1... | collective-permute-start | bytes 12296 | tf_op jit(solution)/shard_map/ppermute | solution.py:146
  19.3 2.2 %copy-start = (f32[2048,512]{1,0:T(8,128)S(1)}, f32[2048,512]{1,0:T(8,128)}, u32[]{:S(2)}) copy-start(f32[2048,512]{1,0:T(8,128)} %own_ref.1) | copy-start | bytes 12582916
  44.0 26.3 %collective-permute-start.12 = (f32[1280,128]{1,0:T(8,128)S(1)}, f32[1280,128]{1,0:T(8,128)S(1)}, u32[]{:S(2)}, u32[]{:S(2)}) collective-permute-start(f32[1280,128]{1,0:T(8,128)S(1)} %shard_map.54), channel_id=1, source_target_pairs={{0,2},{2,0},{1,3},{3,1},{4,6},{6,4},{5,7},{7,5},{8,10},{10,8},{9,1... | collective-permute-start | bytes 1966088 | tf_op jit(solution)/shard_map/ppermute | solution.py:146
  52.6 18.5 %collective-permute-start.6 = (f32[1408,128]{1,0:T(8,128)S(1)}, f32[1408,128]{1,0:T(8,128)S(1)}, u32[]{:S(2)}, u32[]{:S(2)}) collective-permute-start(f32[1408,128]{1,0:T(8,128)S(1)} %shard_map.52), channel_id=1, source_target_pairs={{0,16},{16,0},{1,17},{17,1},{2,18},{18,2},{3,19},{19,3},{4,20},{20... | collective-permute-start | bytes 2162696 | tf_op jit(solution)/shard_map/ppermute | solution.py:146
  60.7 18.5 %collective-permute-start.9 = (f32[1408,128]{1,0:T(8,128)S(1)}, f32[1408,128]{1,0:T(8,128)S(1)}, u32[]{:S(2)}, u32[]{:S(2)}) collective-permute-start(f32[1408,128]{1,0:T(8,128)S(1)} %shard_map.53), channel_id=1, source_target_pairs={{0,1},{1,0},{2,3},{3,2},{4,5},{5,4},{6,7},{7,6},{8,9},{9,8},{10,11... | collective-permute-start | bytes 2162696 | tf_op jit(solution)/shard_map/ppermute | solution.py:146
  70.4 9.4 %collective-permute-start.13 = (f32[640,128]{1,0:T(8,128)S(1)}, f32[640,128]{1,0:T(8,128)S(1)}, u32[]{:S(2)}, u32[]{:S(2)}) collective-permute-start(f32[640,128]{1,0:T(8,128)S(1)} %get-tuple-element.17), channel_id=1, source_target_pairs={{0,16},{16,0},{1,17},{17,1},{2,18},{18,2},{3,19},{19,3},{4,20},{20... | collective-permute-start | bytes 983048 | tf_op jit(solution)/shard_map/ppermute | solution.py:146
  71.1 12.5 %collective-permute-start.7 = (f32[704,128]{1,0:T(8,128)S(1)}, f32[704,128]{1,0:T(8,128)S(1)}, u32[]{:S(2)}, u32[]{:S(2)}) collective-permute-start(f32[704,128]{1,0:T(8,128)S(1)} %get-tuple-element.13), channel_id=1, source_target_pairs={{0,1},{1,0},{2,3},{3,2},{4,5},{5,4},{6,7},{7,6},{8,9},{9,8},{10,11... | collective-permute-start | bytes 1081352 | tf_op jit(solution)/shard_map/ppermute | solution.py:146
  79.3 9.8 %collective-permute-start.10 = (f32[704,128]{1,0:T(8,128)S(1)}, f32[704,128]{1,0:T(8,128)S(1)}, u32[]{:S(2)}, u32[]{:S(2)}) collective-permute-start(f32[704,128]{1,0:T(8,128)S(1)} %get-tuple-element.15), channel_id=1, source_target_pairs={{0,2},{2,0},{1,3},{3,1},{4,6},{6,4},{5,7},{7,5},{8,10},{10,8},{9,1... | collective-permute-start | bytes 1081352 | tf_op jit(solution)/shard_map/ppermute | solution.py:146
  79.8 9.9 %collective-permute-start.14 = (f32[320,128]{1,0:T(8,128)S(1)}, f32[320,128]{1,0:T(8,128)S(1)}, u32[]{:S(2)}, u32[]{:S(2)}) collective-permute-start(f32[320,128]{1,0:T(8,128)S(1)} %slice_add_fusion.11), channel_id=1, source_target_pairs={{0,1},{1,0},{2,3},{3,2},{4,5},{5,4},{6,7},{7,6},{8,9},{9,8},{10,11... | collective-permute-start | bytes 491528 | tf_op jit(solution)/shard_map/ppermute | solution.py:146
  83.6 7.9 %collective-permute-start.8 = (f32[352,128]{1,0:T(8,128)S(1)}, f32[352,128]{1,0:T(8,128)S(1)}, u32[]{:S(2)}, u32[]{:S(2)}) collective-permute-start(f32[352,128]{1,0:T(8,128)S(1)} %slice_add_fusion.9), channel_id=1, source_target_pairs={{0,2},{2,0},{1,3},{3,1},{4,6},{6,4},{5,7},{7,5},{8,10},{10,8},{9,1... | collective-permute-start | bytes 540680 | tf_op jit(solution)/shard_map/ppermute | solution.py:146
  89.1 5.6 %collective-permute-start.11 = (f32[352,128]{1,0:T(8,128)S(1)}, f32[352,128]{1,0:T(8,128)S(1)}, u32[]{:S(2)}, u32[]{:S(2)}) collective-permute-start(f32[352,128]{1,0:T(8,128)S(1)} %slice_add_fusion.7), channel_id=1, source_target_pairs={{0,16},{16,0},{1,17},{17,1},{2,18},{18,2},{3,19},{19,3},{4,20},{20... | collective-permute-start | bytes 540680 | tf_op jit(solution)/shard_map/ppermute | solution.py:146
  94.8 9.0 %collective-permute-start.15 = (f32[1,512,128]{2,1,0:T(8,128)S(1)}, f32[1,512,128]{2,1,0:T(8,128)S(1)}, u32[]{:S(2)}, u32[]{:S(2)}) collective-permute-start(f32[1,512,128]{2,1,0:T(8,128)S(1)} %slice.123), channel_id=1, source_target_pairs={{0,4},{4,0},{1,5},{5,1},{2,6},{6,2},{3,7},{7,3},{8,12},{12,8},{9,1... | collective-permute-start | bytes 786440 | tf_op jit(solution)/shard_map/ppermute | solution.py:146
  103.8 1.6 %collective-permute-start.16 = (f32[512,128]{1,0:T(8,128)S(1)}, f32[512,128]{1,0:T(8,128)S(1)}, u32[]{:S(2)}, u32[]{:S(2)}) collective-permute-start(f32[512,128]{1,0:T(8,128)S(1)} %fusion.own_ref), channel_id=1, source_target_pairs={{0,8},{8,0},{1,9},{9,1},{2,10},{10,2},{3,11},{11,3},{4,12},{12,4},... | collective-permute-start | bytes 786440 | tf_op jit(solution)/shard_map/ppermute | solution.py:146

commit v2 on v1

v2 whole, which is shorter than its diff:
```python
import functools
import math

import jax
import jax.numpy as jnp
from jax import lax
from jax.experimental import pallas as pl
from jax.experimental.pallas import tpu as pltpu
from jax.sharding import Mesh, PartitionSpec as P

HBM = pl.BlockSpec(memory_space=pltpu.HBM)
VMEM = pl.BlockSpec(memory_space=pltpu.VMEM)
SMEM = pl.BlockSpec(memory_space=pltpu.SMEM)
BLOCK = 256
LANES = 128
BATCH = 16
GROUPS = 1
NEGATIVE = 1 << 30


def limit(mib):
    return pltpu.CompilerParams(vmem_limit_bytes=mib * 1024 * 1024)


def cost(flops, moved):
    return pl.CostEstimate(flops=flops, bytes_accessed=moved, transcendentals=0)


def walsh(values):
    half = 1
    while half < len(values):
        out = list(values)
        for i in range(len(values)):
            if not i & half:
                out[i] = values[i] + values[i | half]
                out[i | half] = values[i] - values[i | half]
        values = out
        half *= 2
    return values


def transform_kernel(own_ref, oth_ref, own_sign_ref, oth_sign_ref, table_ref, held_ref, part_ref, sems):
    blocks, cols = part_ref.shape[1], part_ref.shape[3]
    tiles = cols // LANES
    copies = [
        pltpu.make_async_copy(
            ref.at[pl.ds(b * BLOCK, BLOCK)], held_ref.at[core, b], sems.at[core, b]
        )
        for core, ref in enumerate((own_ref, oth_ref))
        for b in range(blocks)
    ]
    for copy in copies:
        copy.start()
    common = lax.broadcasted_iota(jnp.int32, (BLOCK, BLOCK), 0) & lax.broadcasted_iota(
        jnp.int32, (BLOCK, BLOCK), 1
    )
    for shift in (4, 2, 1):
        common = common ^ (common >> shift)
    had = (1 - 2 * (common & 1)).astype(jnp.float32)
    for core, sign_ref in enumerate((own_sign_ref, oth_sign_ref)):
        for b in range(blocks):
            copies[core * blocks + b].wait()
            left = (had * sign_ref[b : b + 1, :]).astype(jnp.bfloat16)
            full = held_ref[core, b]
            high = full.astype(jnp.bfloat16)
            low = (full - high.astype(jnp.float32)).astype(jnp.bfloat16)
            part_ref[core, b] = jnp.dot(
                jnp.concatenate([left, left], axis=1),
                jnp.concatenate([high, low], axis=0),
                preferred_element_type=jnp.float32,
            )

    def one_chunk(chunk, carry):
        start = pl.multiple_of(chunk * 8, 8)
        for tile in range(tiles):
            lanes = slice(tile * LANES, (tile + 1) * LANES)
            own = walsh([part_ref[0, b, pl.ds(start, 8), lanes] for b in range(blocks)])
            oth = walsh([part_ref[1, b, pl.ds(start, 8), lanes] for b in range(blocks)])
            for b in range(blocks):
                for core, value in enumerate((own[b] + oth[b], own[b] - oth[b])):
                    row = (core * blocks + b) * BLOCK + start
                    table_ref[pl.ds(row * tiles + tile, 8, stride=tiles), :] = value
        return carry

    lax.fori_loop(0, BLOCK // 8, one_chunk, 0)


def transform(own, oth, own_sign, oth_sign):
    count, cols = own.shape
    blocks = count // BLOCK
    return pl.pallas_call(
        transform_kernel,
        out_shape=jax.ShapeDtypeStruct((2 * count * cols // LANES, LANES), jnp.float32),
        in_specs=[HBM, HBM, VMEM, VMEM],
        out_specs=VMEM,
        scratch_shapes=[
            pltpu.VMEM((2, blocks, BLOCK, cols), jnp.float32),
            pltpu.VMEM((2, blocks, BLOCK, cols), jnp.float32),
            pltpu.SemaphoreType.DMA((2, blocks)),
        ],
        compiler_params=limit(20),
        cost_estimate=cost(8 * count * BLOCK * cols, 16 * count * cols),
    )(own, oth, own_sign, oth_sign)


def gather_kernel(plans, tiles, code_ref, table_ref, *out_refs):
    for out_ref, (starts, count) in zip(out_refs, plans):

        def copy(first, base, number, out_ref=out_ref):
            rows = []
            for i in range(number):
                code = code_ref[first + i]
                at = pl.multiple_of(code & (NEGATIVE - 1), tiles)
                row = table_ref[pl.ds(at, tiles), :]
                rows.append(jnp.where(code >= NEGATIVE, -row, row))
            for i, row in enumerate(rows):
                out_ref[pl.ds(pl.multiple_of((base + i) * tiles, tiles), tiles), :] = row

        for place, start in enumerate(starts):
            whole = count // BATCH

            def batch(step, carry, start=start, place=place, count=count, copy=copy):
                copy(start + step * BATCH, place * count + step * BATCH, BATCH)
                return carry

            lax.fori_loop(0, whole, batch, 0)
            if count % BATCH:
                copy(start + whole * BATCH, place * count + whole * BATCH, count % BATCH)


def gather(plans, tiles, code, table):
    total = sum(len(starts) * count for starts, count in plans)
    return pl.pallas_call(
        functools.partial(gather_kernel, plans, tiles),
        out_shape=[
            jax.ShapeDtypeStruct((len(starts) * count * tiles, LANES), jnp.float32)
            for starts, count in plans
        ],
        in_specs=[SMEM, VMEM],
        out_specs=[VMEM] * len(plans),
        compiler_params=limit(4),
        cost_estimate=cost(0, 8 * total * tiles * LANES),
    )(code, table)


def gram_kernel(scale, inverse_total, core_ref, *refs):
    sums, (sketch_ref, gram_ref, both_ref) = refs[:-3], refs[-3:]
    samp, cols = sketch_ref.shape
    tiles = cols // LANES
    for tile in range(tiles):
        lanes = slice(tile * LANES, (tile + 1) * LANES)
        at = 0
        for ref in sums:
            count = ref.shape[0] // tiles
            both_ref[at : at + count, lanes] = ref[pl.ds(tile, count, stride=tiles), :] * scale
            at += count
    sketch_ref[...] = both_ref[:samp, :]
    width = gram_ref.shape[0] // 2
    for upper in range(2):
        start = pl.multiple_of(upper * (cols // 2) + core_ref[0] * width, LANES)
        gram_ref[upper * width : (upper + 1) * width, :] = (
            lax.dot_general(
                both_ref[:, pl.ds(start, width)],
                both_ref[...],
                (((0,), (0,)), ((), ())),
                precision=lax.Precision.HIGHEST,
                preferred_element_type=jnp.float32,
            )
            * inverse_total
        )


def swap(block, bit):
    return lax.ppermute(block, bit, [(0, 1), (1, 0)])


def exclusive(block, place, axis):
    while block.shape[axis] > 1:
        half = block.shape[axis] // 2
        upper = lax.slice_in_dim(block, half, 2 * half, axis=axis)
        lower = lax.slice_in_dim(block, 0, half, axis=axis)
        block = jnp.where(place & half == half, upper, lower)
    return jnp.squeeze(block, axis)


def reduce_pairs(block, axes):
    own = lax.axis_index(axes)
    total = exclusive(block, own, 0)
    for flip in (3, 2, 1):
        route = [(i, i ^ flip) for i in range(4)]
        total += lax.ppermute(exclusive(block, own ^ flip, 0), axes, route)
    return total


def reduce_gram(block, high, low):
    first, rest = low[0], low[1:]
    block = block.reshape(2, -1, 2, *block.shape[2:])
    block = jnp.moveaxis(block, 2, 1).reshape(4, -1, *block.shape[3:])
    block = reduce_pairs(block, (high, first))
    while rest:
        if len(rest) >= 2:
            block = reduce_pairs(block.reshape(4, -1, *block.shape[1:]), (rest[-1], rest[-2]))
            rest = rest[:-2]
        else:
            last = rest[-1]
            own = lax.axis_index(last)
            block = block.reshape(2, -1, *block.shape[1:])
            block = exclusive(block, own, 0) + swap(exclusive(block, 1 - own, 0), last)
            rest = rest[:-1]
    return block[0]


def per_device(bits, design, signs, samples):
    rows, cols = design.shape
    samp = samples.shape[0]
    tiles = cols // LANES
    devices = 2 ** len(bits)
    high, core, low = bits[0], bits[1], bits[:1:-1]
    steps = [high, *low]
    own_index = lax.axis_index(tuple(bits))
    core_bit = len(low)

    oth_design = swap(design, core)
    oth_signs = swap(signs, core)
    sign_rows = [(2 * s - 1).astype(jnp.float32).reshape(rows // BLOCK, BLOCK) for s in (signs, oth_signs)]
    listed = lax.optimization_barrier(samples ^ (own_index >> len(bits)))
    for bit in steps[:-1]:
        listed = jnp.concatenate([listed, swap(listed, bit)])
    listed, oth_design = lax.optimization_barrier((listed, oth_design))
    listed = jnp.concatenate([listed, swap(listed, steps[-1])])
    mixed = transform(design, oth_design, *sign_rows)

    source = listed // rows
    parity = source & own_index
    shift = 1
    while shift < devices:
        parity = parity ^ (parity >> shift)
        shift *= 2
    code = ((source >> core_bit & 1) * rows + listed % rows) * tiles + (parity & 1) * NEGATIVE

    owners = devices // 2
    groups = GROUPS
    group_samp = samp // groups
    third = (group_samp // 3 + 2) // 2 * 2
    counts = [third, third, group_samp - 2 * third] * groups
    orders = []
    for part in range(3):
        order = [(part + i) % 3 for i in range(3)]
        orders.append(order + list(range(3, len(steps))))

    def plan(piece, first):
        order = orders[piece % 3]
        found = []
        for place in range(owners // 2):
            owner = first << order[0]
            for level, bit in enumerate(order[1:]):
                owner |= (place >> (len(order) - 2 - level) & 1) << bit
            found.append(owner * samp + sum(counts[:piece]))
        return found, counts[piece]

    arrived, held = [], []
    for piece in range(3 * groups):
        sent = gather([plan(piece, 1)], tiles, code, mixed)[0]
        arrived.append(swap(sent, steps[piece % 3]))
    for group in range(groups):
        held += gather([plan(group * 3 + part, 0) for part in range(3)], tiles, code, mixed)
    own_sums, oth_sums = [], []
    for group in range(groups):
        pieces = range(group * 3, group * 3 + 3)
        for level in range(1, 3):
            for piece in pieces:
                half = held[piece].shape[0] // 2
                send = held[piece][half:] + arrived[piece][half:]
                held[piece] = held[piece][:half] + arrived[piece][:half]
                arrived[piece] = swap(send, steps[orders[piece % 3][level]])
        whole = jnp.concatenate(
            [(held[i] + arrived[i]).reshape(-1, counts[i] * tiles, LANES) for i in pieces], axis=1
        )
        for level in range(3, len(steps)):
            half = whole.shape[0] // 2
            whole = whole[:half] + swap(whole[half:], steps[level])
        own_sums.append(whole[0])
        oth_sums.append(swap(whole[0], core))

    half_rows = cols // 2
    sketch, product = pl.pallas_call(
        functools.partial(gram_kernel, 1.0 / math.sqrt(rows * devices), 1.0 / (samp * devices)),
        out_shape=[
            jax.ShapeDtypeStruct((samp, cols), jnp.float32),
            jax.ShapeDtypeStruct((half_rows, cols), jnp.float32),
        ],
        in_specs=[SMEM] + [VMEM] * (2 * groups),
        out_specs=[VMEM, VMEM],
        scratch_shapes=[pltpu.VMEM((2 * samp, cols), jnp.float32)],
        compiler_params=limit(8),
        cost_estimate=cost(24 * samp * samp * cols, 16 * samp * cols),
    )(lax.axis_index(core).astype(jnp.int32).reshape(1), *own_sums, *oth_sums)

    gram = reduce_gram(product.reshape(2, 2 ** len(low), -1, cols), high, low)
    return sketch, gram


def solution(mesh):
    width = [size.bit_length() - 1 for size in mesh.devices.shape]
    bits = [f"{axis}{i}" for axis, w in zip(mesh.axis_names, width) for i in reversed(range(w))]
    split = Mesh(mesh.devices.reshape((2,) * len(bits)), tuple(bits))
    every = tuple(bits)
    return jax.shard_map(
        functools.partial(per_device, bits),
        mesh=split,
        in_specs=(P(every, None), P(every), P(every)),
        out_specs=(P(every, None), P(every, None)),
        check_vma=False,
    )
```

time: 129 us -> 95.7 us (0.74)
  Pallas kernels: 44.6 us -> 15.4 us
  blocking collectives: 21.4 us -> 0 us
  waiting for transfers between devices: 31.7 us -> 44.3 us
  starting transfers between devices: 23.1 us -> 29.8 us
    all_to_all x1 -> x0, blocking collectives: 21.4 us -> none  [per_device(): lax.all_to_all(product, (high, *reversed(low)), split_axis=0, concat_axis...]
    pallas_call x4, Pallas kernels: 27.7 us -> 6.87 us  [gather(): pl.pallas_call(functools.partial(gather_kernel, plans, tiles), out_shape=...]
    pallas_call x1, Pallas kernels: 16.1 us -> 7.22 us  [transform(): pl.pallas_call(transform_kernel, out_shape=jax.ShapeDtypeStruct((2 * coun...]
    ppermute x0 -> x6, starting transfers between devices: none -> 8.12 us  [reduce_pairs(): total += lax.ppermute(exclusive(block, own ^ flip, 0), axes, route)]
    ppermute x0 -> x6, waiting for transfers between devices: none -> 7.48 us  [reduce_pairs(): total += lax.ppermute(exclusive(block, own ^ flip, 0), axes, route)]
    ppermute x17, waiting for transfers between devices: 31.7 us -> 36.9 us  [swap(): return lax.ppermute(block, bit, [(0, 1), (1, 0)])]
    concatenate x3, other arithmetic: 1.99 us -> 0.02 us  [per_device(): listed = jnp.concatenate([listed, swap(listed, bit)])]
    ppermute x17, starting transfers between devices: 23.1 us -> 21.7 us  [swap(): return lax.ppermute(block, bit, [(0, 1), (1, 0)])]
  transfers between devices with their start and end apart: 17 -> 23, of which waited for: 11 -> 17; matrix products, arithmetic and copies ran while one was open for 3% -> 2% of each run, Pallas kernels for 17% -> 13%
where the time goes in v2:
time: 95.7 us; the launch traced here: 95.5 us
  waiting for transfers between devices  44.3 us (46%)
  starting transfers between devices  29.8 us (31%)
  Pallas kernels  15.4 us (16%)
  other arithmetic  2.75 us (3%)
  local copies, waits for them, and re-layouts  2.26 us (2%)
    ppermute x17, waiting for transfers between devices, swap(): return lax.ppermute(block, bit, [(0, 1), (1, 0)])  36.9 us
    ppermute x17, starting transfers between devices, swap(): return lax.ppermute(block, bit, [(0, 1), (1, 0)])  21.7 us
    ppermute x6, starting transfers between devices, reduce_pairs(): total += lax.ppermute(exclusive(block, own ^ flip, 0), axes, route)  8.12 us
    ppermute x6, waiting for transfers between devices, reduce_pairs(): total += lax.ppermute(exclusive(block, own ^ flip, 0), axes, route)  7.48 us
    pallas_call x1, Pallas kernels, transform(): pl.pallas_call(transform_kernel, out_shape=jax.ShapeDtypeStruct((2 * coun...  7.22 us
    pallas_call x4, Pallas kernels, gather(): pl.pallas_call(functools.partial(gather_kernel, plans, tiles), out_shape=...  6.87 us
    unnamed x3, local copies, waits for them, and re-layouts  2.19 us
  transfers between devices with their start and end apart: 23, of which 17 were waited for; matrix products, arithmetic and copies ran while one was open for 2% of the time, Pallas kernels for 13%

profile of v2, /device:TPU:0, one launch (start us, length us, event | category | flops | bytes accessed | tf_op | source)
XLA Modules:
  0.0 95.5 jit_solution(8366119429116957078)
XLA Ops:
  0.6 0.5 collective-permute-start.3
  1.1 0.7 broadcast_xor_fusion
  1.8 2.5 %collective-permute-start = (s32[128]{0:T(128)S(1)}, s32[128]{0:T(128)S(1)}, u32[]{:S(2)}, u32[]{:S(2)}) collective-permute-start(s32[128]{0:T(128)S(1)} %broadcast_xor_fusion), channel_id=1, source_target_pairs={{0,16},{16,0},{1,17},{17,1},{2,18},{18,2},{3,19},{19,3},{4,20},{20... | collective-permute-start | bytes 1544 | tf_op jit(solution)/shard_map/ppermute | solution.py:174
  4.3 1.5 %collective-permute-done = s32[128]{0:T(128)S(1)} collective-permute-done((s32[128]{0:T(128)S(1)}, s32[128]{0:T(128)S(1)}, u32[]{:S(2)}, u32[]{:S(2)}) %collective-permute-start) | collective-permute-done | bytes 544 | tf_op jit(solution)/shard_map/ppermute | solution.py:174
  5.9 2.1 %collective-permute-start.1 = (s32[256]{0:T(256)S(1)}, s32[256]{0:T(256)S(1)}, u32[]{:S(2)}, u32[]{:S(2)}) collective-permute-start(s32[256]{0:T(256)S(1)} %pad_add_fusion.2), channel_id=1, source_target_pairs={{0,1},{1,0},{2,3},{3,2},{4,5},{5,4},{6,7},{7,6},{8,9},{9,8},{10,11... | collective-permute-start | bytes 3080 | tf_op jit(solution)/shard_map/ppermute | solution.py:174
  7.9 0.0 collective-permute-start.5
  7.9 1.5 %collective-permute-done.1 = s32[256]{0:T(256)S(1)} collective-permute-done((s32[256]{0:T(256)S(1)}, s32[256]{0:T(256)S(1)}, u32[]{:S(2)}, u32[]{:S(2)}) %collective-permute-start.1) | collective-permute-done | bytes 1056 | tf_op jit(solution)/shard_map/ppermute | solution.py:174
  9.5 2.1 %collective-permute-start.2 = (s32[512]{0:T(512)S(1)}, s32[512]{0:T(512)S(1)}, u32[]{:S(2)}, u32[]{:S(2)}) collective-permute-start(s32[512]{0:T(512)S(1)} %pad_add_fusion.1), channel_id=1, source_target_pairs={{0,2},{2,0},{1,3},{3,1},{4,6},{6,4},{5,7},{7,5},{8,10},{10,8},{9,1... | collective-permute-start | bytes 6152 | tf_op jit(solution)/shard_map/ppermute | solution.py:174
  11.5 0.7 add_convert_fusion.1
  12.2 0.9 collective-permute-done.2
  13.1 0.0 collective-permute-done.5
  13.1 0.0 collective-permute-done.3.oth_ref
  13.2 3.1 %collective-permute-start.4 = (s32[1024]{0:T(1024)S(1)}, s32[1024]{0:T(1024)S(1)}, u32[]{:S(2)}, u32[]{:S(2)}) collective-permute-start(s32[1024]{0:T(1024)S(1)} %pad_add_fusion), channel_id=1, source_target_pairs={{0,4},{4,0},{1,5},{5,1},{2,6},{6,2},{3,7},{7,3},{8,12},{12,8},{9,1... | collective-permute-start | bytes 12296 | tf_op jit(solution)/shard_map/ppermute | solution.py:174
  16.3 0.0 copy-start
  16.3 2.2 %copy-done = f32[2048,512]{1,0:T(8,128)S(1)} copy-done((f32[2048,512]{1,0:T(8,128)S(1)}, f32[2048,512]{1,0:T(8,128)}, u32[]{:S(2)}) %copy-start) | copy-done | bytes 4194328
  18.5 7.2 %shard_map.50.table_ref = f32[16384,128]{1,0:T(8,128)S(1)} custom-call(f32[2048,512]{1,0:T(8,128)S(1)} %copy-done, f32[2048,512]{1,0:T(8,128)} %collective-permute-done.3.oth_ref, f32[8,256]{1,0:T(8,128)S(1)} %reshape.89.own_sign_ref, f32[8,256]{1,0:T(8,128)S(1)} %reshape.90.oth_sign_ref), custom_call_target="tpu_custom_call" | custom-call | flops 2147483648 | bytes 16777216 | tf_op jit(solution)/shard_map/pallas_call | solution.py:91
  25.7 0.0 collective-permute-done.4
  25.8 1.3 %shard_map.54 = f32[1280,128]{1,0:T(8,128)S(1)} custom-call(s32[2048]{0:T(1024)S(1)} %fusion.17.code_ref, f32[16384,128]{1,0:T(8,128)S(1)} %shard_map.50.table_ref), custom_call_target="tpu_custom_call" | custom-call | bytes 1310720 | tf_op jit(solution)/shard_map/pallas_call | solution.py:133
  27.1 1.6 %collective-permute-start.12 = (f32[1280,128]{1,0:T(8,128)S(1)}, f32[1280,128]{1,0:T(8,128)S(1)}, u32[]{:S(2)}, u32[]{:S(2)}) collective-permute-start(f32[1280,128]{1,0:T(8,128)S(1)} %shard_map.54), channel_id=1, source_target_pairs={{0,2},{2,0},{1,3},{3,1},{4,6},{6,4},{5,7},{7,5},{8,10},{10,8},{9,1... | collective-permute-start | bytes 1966088 | tf_op jit(solution)/shard_map/ppermute | solution.py:174
  28.7 1.4 %shard_map.52 = f32[1408,128]{1,0:T(8,128)S(1)} custom-call(s32[2048]{0:T(1024)S(1)} %fusion.17.code_ref, f32[16384,128]{1,0:T(8,128)S(1)} %shard_map.50.table_ref), custom_call_target="tpu_custom_call" | custom-call | bytes 1441792 | tf_op jit(solution)/shard_map/pallas_call | solution.py:133
  30.1 1.5 %collective-permute-start.6 = (f32[1408,128]{1,0:T(8,128)S(1)}, f32[1408,128]{1,0:T(8,128)S(1)}, u32[]{:S(2)}, u32[]{:S(2)}) collective-permute-start(f32[1408,128]{1,0:T(8,128)S(1)} %shard_map.52), channel_id=1, source_target_pairs={{0,16},{16,0},{1,17},{17,1},{2,18},{18,2},{3,19},{19,3},{4,20},{20... | collective-permute-start | bytes 2162696 | tf_op jit(solution)/shard_map/ppermute | solution.py:174
  31.7 1.4 %shard_map.53 = f32[1408,128]{1,0:T(8,128)S(1)} custom-call(s32[2048]{0:T(1024)S(1)} %fusion.17.code_ref, f32[16384,128]{1,0:T(8,128)S(1)} %shard_map.50.table_ref), custom_call_target="tpu_custom_call" | custom-call | bytes 1441792 | tf_op jit(solution)/shard_map/pallas_call | solution.py:133
  33.1 1.6 %collective-permute-start.9 = (f32[1408,128]{1,0:T(8,128)S(1)}, f32[1408,128]{1,0:T(8,128)S(1)}, u32[]{:S(2)}, u32[]{:S(2)}) collective-permute-start(f32[1408,128]{1,0:T(8,128)S(1)} %shard_map.53), channel_id=1, source_target_pairs={{0,1},{1,0},{2,3},{3,2},{4,5},{5,4},{6,7},{7,6},{8,9},{9,8},{10,11... | collective-permute-start | bytes 2162696 | tf_op jit(solution)/shard_map/ppermute | solution.py:174
  34.6 2.8 %shard_map.51 = (f32[1408,128]{1,0:T(8,128)S(1)}, f32[1408,128]{1,0:T(8,128)S(1)}, f32[1280,128]{1,0:T(8,128)S(1)}) custom-call(s32[2048]{0:T(1024)S(1)} %fusion.17.code_ref, f32[16384,128]{1,0:T(8,128)S(1)} %shard_map.50.table_ref), custom_call_target="tpu_custom_call" | custom-call | bytes 4194304 | tf_op jit(solution)/shard_map/pallas_call | solution.py:133
  37.4 3.5 %collective-permute-done.12 = f32[1280,128]{1,0:T(8,128)S(1)} collective-permute-done((f32[1280,128]{1,0:T(8,128)S(1)}, f32[1280,128]{1,0:T(8,128)S(1)}, u32[]{:S(2)}, u32[]{:S(2)}) %collective-permute-start.12) | collective-permute-done | bytes 655392 | tf_op jit(solution)/shard_map/ppermute | solution.py:174
  40.9 0.1 slice_add_fusion.5
  41.0 1.6 %collective-permute-start.13 = (f32[640,128]{1,0:T(8,128)S(1)}, f32[640,128]{1,0:T(8,128)S(1)}, u32[]{:S(2)}, u32[]{:S(2)}) collective-permute-start(f32[640,128]{1,0:T(8,128)S(1)} %get-tuple-element.21), channel_id=1, source_target_pairs={{0,16},{16,0},{1,17},{17,1},{2,18},{18,2},{3,19},{19,3},{4,20},{20... | collective-permute-start | bytes 983048 | tf_op jit(solution)/shard_map/ppermute | solution.py:174
  42.5 6.0 %collective-permute-done.6 = f32[1408,128]{1,0:T(8,128)S(1)} collective-permute-done((f32[1408,128]{1,0:T(8,128)S(1)}, f32[1408,128]{1,0:T(8,128)S(1)}, u32[]{:S(2)}, u32[]{:S(2)}) %collective-permute-start.6) | collective-permute-done | bytes 720928 | tf_op jit(solution)/shard_map/ppermute | solution.py:174
  48.6 0.1 slice_add_fusion.3
  48.6 1.2 %collective-permute-start.7 = (f32[704,128]{1,0:T(8,128)S(1)}, f32[704,128]{1,0:T(8,128)S(1)}, u32[]{:S(2)}, u32[]{:S(2)}) collective-permute-start(f32[704,128]{1,0:T(8,128)S(1)} %get-tuple-element.17), channel_id=1, source_target_pairs={{0,1},{1,0},{2,3},{3,2},{4,5},{5,4},{6,7},{7,6},{8,9},{9,8},{10,11... | collective-permute-start | bytes 1081352 | tf_op jit(solution)/shard_map/ppermute | solution.py:174
  49.9 1.8 %collective-permute-done.9 = f32[1408,128]{1,0:T(8,128)S(1)} collective-permute-done((f32[1408,128]{1,0:T(8,128)S(1)}, f32[1408,128]{1,0:T(8,128)S(1)}, u32[]{:S(2)}, u32[]{:S(2)}) %collective-permute-start.9) | collective-permute-done | bytes 720928 | tf_op jit(solution)/shard_map/ppermute | solution.py:174
  51.7 0.1 slice_add_fusion.1
  51.8 0.6 collective-permute-start.10
  52.4 0.0 collective-permute-done.13
  52.4 1.5 %collective-permute-start.14 = (f32[320,128]{1,0:T(8,128)S(1)}, f32[320,128]{1,0:T(8,128)S(1)}, u32[]{:S(2)}, u32[]{:S(2)}) collective-permute-start(f32[320,128]{1,0:T(8,128)S(1)} %slice_add_fusion.11), channel_id=1, source_target_pairs={{0,1},{1,0},{2,3},{3,2},{4,5},{5,4},{6,7},{7,6},{8,9},{9,8},{10,11... | collective-permute-start | bytes 491528 | tf_op jit(solution)/shard_map/ppermute | solution.py:174
  53.9 3.3 %collective-permute-done.7 = f32[704,128]{1,0:T(8,128)S(1)} collective-permute-done((f32[704,128]{1,0:T(8,128)S(1)}, f32[704,128]{1,0:T(8,128)S(1)}, u32[]{:S(2)}, u32[]{:S(2)}) %collective-permute-start.7) | collective-permute-done | bytes 360480 | tf_op jit(solution)/shard_map/ppermute | solution.py:174
  57.2 0.5 collective-permute-start.8
  57.8 2.3 %collective-permute-done.10 = f32[704,128]{1,0:T(8,128)S(1)} collective-permute-done((f32[704,128]{1,0:T(8,128)S(1)}, f32[704,128]{1,0:T(8,128)S(1)}, u32[]{:S(2)}, u32[]{:S(2)}) %collective-permute-start.10) | collective-permute-done | bytes 360480 | tf_op jit(solution)/shard_map/ppermute | solution.py:174
  60.1 0.7 collective-permute-start.11
  60.8 0.0 collective-permute-done.14
  60.8 3.7 %collective-permute-done.8 = f32[352,128]{1,0:T(8,128)S(1)} collective-permute-done((f32[352,128]{1,0:T(8,128)S(1)}, f32[352,128]{1,0:T(8,128)S(1)}, u32[]{:S(2)}, u32[]{:S(2)}) %collective-permute-start.8) | collective-permute-done | bytes 180256 | tf_op jit(solution)/shard_map/ppermute | solution.py:174
  64.5 1.1 %collective-permute-done.11 = f32[352,128]{1,0:T(8,128)S(1)} collective-permute-done((f32[352,128]{1,0:T(8,128)S(1)}, f32[352,128]{1,0:T(8,128)S(1)}, u32[]{:S(2)}, u32[]{:S(2)}) %collective-permute-start.11) | collective-permute-done | bytes 180256 | tf_op jit(solution)/shard_map/ppermute | solution.py:174
  65.7 0.4 collective-permute-start.15
  66.1 9.7 %collective-permute-done.15 = f32[1,512,128]{2,1,0:T(8,128)S(1)} collective-permute-done((f32[1,512,128]{2,1,0:T(8,128)S(1)}, f32[1,512,128]{2,1,0:T(8,128)S(1)}, u32[]{:S(2)}, u32[]{:S(2)}) %collective-permute-start.15) | collective-permute-done | bytes 262176 | tf_op jit(solution)/shard_map/ppermute | solution.py:174
  75.9 0.1 collective-permute-start.16
  76.0 1.5 %collective-permute-done.16.refs_1_ = f32[512,128]{1,0:T(8,128)S(1)} collective-permute-done((f32[512,128]{1,0:T(8,128)S(1)}, f32[512,128]{1,0:T(8,128)S(1)}, u32[]{:S(2)}, u32[]{:S(2)}) %collective-permute-start.16) | collective-permute-done | bytes 262176 | tf_op jit(solution)/shard_map/ppermute | solution.py:174
  77.5 1.4 %shard_map.55 = (f32[128,512]{1,0:T(8,128)}, f32[256,512]{1,0:T(8,128)S(1)}) custom-call(s32[1]{0:T(128)} %bitcast.core_ref, f32[512,128]{1,0:T(8,128)S(1)} %fusion.refs_0_, f32[512,128]{1,0:T(8,128)S(1)} %collective-permute-done.16.refs_1_), custom_call_target="tpu_custom_call" | custom-call | flops 201326592 | bytes 1048576 | tf_op jit(solution)/shard_map/pallas_call | solution.py:286
  78.9 0.1 slice_select_fusion.3
  79.1 1.2 %collective-permute-start.17 = (f32[4,16,512]{2,1,0:T(8,128)S(1)}, f32[4,16,512]{2,1,0:T(8,128)S(1)}, u32[]{:S(2)}, u32[]{:S(2)}) collective-permute-start(f32[4,16,512]{2,1,0:T(8,128)S(1)} %fusion.6), channel_id=1, source_target_pairs={{0,17},{1,16},{16,1},{17,0},{2,19},{3,18},{18,3},{19,2},{4,21},{5,... | collective-permute-start | bytes 393224 | tf_op jit(solution)/shard_map/ppermute | solution.py:191
  80.3 1.2 %collective-permute-start.18 = (f32[4,16,512]{2,1,0:T(8,128)S(1)}, f32[4,16,512]{2,1,0:T(8,128)S(1)}, u32[]{:S(2)}, u32[]{:S(2)}) collective-permute-start(f32[4,16,512]{2,1,0:T(8,128)S(1)} %fusion.5), channel_id=1, source_target_pairs={{0,16},{1,17},{16,0},{17,1},{2,18},{3,19},{18,2},{19,3},{4,20},{5,... | collective-permute-start | bytes 393224 | tf_op jit(solution)/shard_map/ppermute | solution.py:191
  81.5 1.3 %collective-permute-start.19 = (f32[4,16,512]{2,1,0:T(8,128)S(1)}, f32[4,16,512]{2,1,0:T(8,128)S(1)}, u32[]{:S(2)}, u32[]{:S(2)}) collective-permute-start(f32[4,16,512]{2,1,0:T(8,128)S(1)} %fusion.4), channel_id=1, source_target_pairs={{0,1},{1,0},{16,17},{17,16},{2,3},{3,2},{18,19},{19,18},{4,5},{5,4... | collective-permute-start | bytes 393224 | tf_op jit(solution)/shard_map/ppermute | solution.py:191
  82.8 3.6 %collective-permute-done.17 = f32[4,16,512]{2,1,0:T(8,128)S(1)} collective-permute-done((f32[4,16,512]{2,1,0:T(8,128)S(1)}, f32[4,16,512]{2,1,0:T(8,128)S(1)}, u32[]{:S(2)}, u32[]{:S(2)}) %collective-permute-start.17) | collective-permute-done | bytes 131104 | tf_op jit(solution)/shard_map/ppermute | solution.py:191
  86.4 1.4 %collective-permute-done.18 = f32[4,16,512]{2,1,0:T(8,128)S(1)} collective-permute-done((f32[4,16,512]{2,1,0:T(8,128)S(1)}, f32[4,16,512]{2,1,0:T(8,128)S(1)}, u32[]{:S(2)}, u32[]{:S(2)}) %collective-permute-start.18) | collective-permute-done | bytes 131104 | tf_op jit(solution)/shard_map/ppermute | solution.py:191
  87.7 0.6 collective-permute-done.19
  88.5 0.4 collective-permute-start.20
  88.9 0.0 collective-permute-start.21
  89.0 4.0 %collective-permute-start.22 = (f32[1,16,512]{2,1,0:T(8,128)S(1)}, f32[1,16,512]{2,1,0:T(8,128)S(1)}, u32[]{:S(2)}, u32[]{:S(2)}) collective-permute-start(f32[1,16,512]{2,1,0:T(8,128)S(1)} %slice_select_fusion.12), channel_id=1, source_target_pairs={{0,2},{2,0},{4,6},{6,4},{1,3},{3,1},{5,7},{7,5},{8,10},{10,8},{12,... | collective-permute-start | bytes 98312 | tf_op jit(solution)/shard_map/ppermute | solution.py:191
  92.9 1.3 %collective-permute-done.20 = f32[1,16,512]{2,1,0:T(8,128)S(1)} collective-permute-done((f32[1,16,512]{2,1,0:T(8,128)S(1)}, f32[1,16,512]{2,1,0:T(8,128)S(1)}, u32[]{:S(2)}, u32[]{:S(2)}) %collective-permute-start.20) | collective-permute-done | bytes 32800 | tf_op jit(solution)/shard_map/ppermute | solution.py:191
  94.3 0.0 collective-permute-done.21
  94.3 0.6 collective-permute-done.22
  94.8 0.6 fusion.14
  (27 shorter events, 0.5 us)
Async XLA Ops:
  0.6 12.5 %collective-permute-start.3 = (f32[2048,512]{1,0:T(8,128)}, f32[2048,512]{1,0:T(8,128)}, u32[]{:S(2)}, u32[]{:S(2)}) collective-permute-start(f32[2048,512]{1,0:T(8,128)} %own_ref.1), channel_id=1, source_target_pairs={{0,8},{8,0},{1,9},{9,1},{2,10},{10,2},{3,11},{11,3},{4,12},{12,4},... | collective-permute-start | bytes 12582920 | tf_op jit(solution)/shard_map/ppermute | solution.py:174
  1.8 4.0 %collective-permute-start = (s32[128]{0:T(128)S(1)}, s32[128]{0:T(128)S(1)}, u32[]{:S(2)}, u32[]{:S(2)}) collective-permute-start(s32[128]{0:T(128)S(1)} %broadcast_xor_fusion), channel_id=1, source_target_pairs={{0,16},{16,0},{1,17},{17,1},{2,18},{18,2},{3,19},{19,3},{4,20},{20... | collective-permute-start | bytes 1544 | tf_op jit(solution)/shard_map/ppermute | solution.py:174
  5.9 3.6 %collective-permute-start.1 = (s32[256]{0:T(256)S(1)}, s32[256]{0:T(256)S(1)}, u32[]{:S(2)}, u32[]{:S(2)}) collective-permute-start(s32[256]{0:T(256)S(1)} %pad_add_fusion.2), channel_id=1, source_target_pairs={{0,1},{1,0},{2,3},{3,2},{4,5},{5,4},{6,7},{7,6},{8,9},{9,8},{10,11... | collective-permute-start | bytes 3080 | tf_op jit(solution)/shard_map/ppermute | solution.py:174
  7.9 5.2 %collective-permute-start.5 = (s32[2048]{0:T(1024)}, s32[2048]{0:T(1024)S(1)}, u32[]{:S(2)}, u32[]{:S(2)}) collective-permute-start(s32[2048]{0:T(1024)} %param.4), channel_id=1, source_target_pairs={{0,8},{8,0},{1,9},{9,1},{2,10},{10,2},{3,11},{11,3},{4,12},{12,4},... | collective-permute-start | bytes 24584 | tf_op jit(solution)/shard_map/ppermute | solution.py:174
  9.5 3.6 %collective-permute-start.2 = (s32[512]{0:T(512)S(1)}, s32[512]{0:T(512)S(1)}, u32[]{:S(2)}, u32[]{:S(2)}) collective-permute-start(s32[512]{0:T(512)S(1)} %pad_add_fusion.1), channel_id=1, source_target_pairs={{0,2},{2,0},{1,3},{3,1},{4,6},{6,4},{5,7},{7,5},{8,10},{10,8},{9,1... | collective-permute-start | bytes 6152 | tf_op jit(solution)/shard_map/ppermute | solution.py:174
  13.2 12.5 %collective-permute-start.4 = (s32[1024]{0:T(1024)S(1)}, s32[1024]{0:T(1024)S(1)}, u32[]{:S(2)}, u32[]{:S(2)}) collective-permute-start(s32[1024]{0:T(1024)S(1)} %pad_add_fusion), channel_id=1, source_target_pairs={{0,4},{4,0},{1,5},{5,1},{2,6},{6,2},{3,7},{7,3},{8,12},{12,8},{9,1... | collective-permute-start | bytes 12296 | tf_op jit(solution)/shard_map/ppermute | solution.py:174
  16.3 2.2 %copy-start = (f32[2048,512]{1,0:T(8,128)S(1)}, f32[2048,512]{1,0:T(8,128)}, u32[]{:S(2)}) copy-start(f32[2048,512]{1,0:T(8,128)} %own_ref.1) | copy-start | bytes 12582916
  27.1 13.8 %collective-permute-start.12 = (f32[1280,128]{1,0:T(8,128)S(1)}, f32[1280,128]{1,0:T(8,128)S(1)}, u32[]{:S(2)}, u32[]{:S(2)}) collective-permute-start(f32[1280,128]{1,0:T(8,128)S(1)} %shard_map.54), channel_id=1, source_target_pairs={{0,2},{2,0},{1,3},{3,1},{4,6},{6,4},{5,7},{7,5},{8,10},{10,8},{9,1... | collective-permute-start | bytes 1966088 | tf_op jit(solution)/shard_map/ppermute | solution.py:174
  30.1 18.4 %collective-permute-start.6 = (f32[1408,128]{1,0:T(8,128)S(1)}, f32[1408,128]{1,0:T(8,128)S(1)}, u32[]{:S(2)}, u32[]{:S(2)}) collective-permute-start(f32[1408,128]{1,0:T(8,128)S(1)} %shard_map.52), channel_id=1, source_target_pairs={{0,16},{16,0},{1,17},{17,1},{2,18},{18,2},{3,19},{19,3},{4,20},{20... | collective-permute-start | bytes 2162696 | tf_op jit(solution)/shard_map/ppermute | solution.py:174
  33.1 18.7 %collective-permute-start.9 = (f32[1408,128]{1,0:T(8,128)S(1)}, f32[1408,128]{1,0:T(8,128)S(1)}, u32[]{:S(2)}, u32[]{:S(2)}) collective-permute-start(f32[1408,128]{1,0:T(8,128)S(1)} %shard_map.53), channel_id=1, source_target_pairs={{0,1},{1,0},{2,3},{3,2},{4,5},{5,4},{6,7},{7,6},{8,9},{9,8},{10,11... | collective-permute-start | bytes 2162696 | tf_op jit(solution)/shard_map/ppermute | solution.py:174
  41.0 11.4 %collective-permute-start.13 = (f32[640,128]{1,0:T(8,128)S(1)}, f32[640,128]{1,0:T(8,128)S(1)}, u32[]{:S(2)}, u32[]{:S(2)}) collective-permute-start(f32[640,128]{1,0:T(8,128)S(1)} %get-tuple-element.21), channel_id=1, source_target_pairs={{0,16},{16,0},{1,17},{17,1},{2,18},{18,2},{3,19},{19,3},{4,20},{20... | collective-permute-start | bytes 983048 | tf_op jit(solution)/shard_map/ppermute | solution.py:174
  48.6 8.6 %collective-permute-start.7 = (f32[704,128]{1,0:T(8,128)S(1)}, f32[704,128]{1,0:T(8,128)S(1)}, u32[]{:S(2)}, u32[]{:S(2)}) collective-permute-start(f32[704,128]{1,0:T(8,128)S(1)} %get-tuple-element.17), channel_id=1, source_target_pairs={{0,1},{1,0},{2,3},{3,2},{4,5},{5,4},{6,7},{7,6},{8,9},{9,8},{10,11... | collective-permute-start | bytes 1081352 | tf_op jit(solution)/shard_map/ppermute | solution.py:174
  51.8 8.2 %collective-permute-start.10 = (f32[704,128]{1,0:T(8,128)S(1)}, f32[704,128]{1,0:T(8,128)S(1)}, u32[]{:S(2)}, u32[]{:S(2)}) collective-permute-start(f32[704,128]{1,0:T(8,128)S(1)} %get-tuple-element.19), channel_id=1, source_target_pairs={{0,2},{2,0},{1,3},{3,1},{4,6},{6,4},{5,7},{7,5},{8,10},{10,8},{9,1... | collective-permute-start | bytes 1081352 | tf_op jit(solution)/shard_map/ppermute | solution.py:174
  52.4 8.4 %collective-permute-start.14 = (f32[320,128]{1,0:T(8,128)S(1)}, f32[320,128]{1,0:T(8,128)S(1)}, u32[]{:S(2)}, u32[]{:S(2)}) collective-permute-start(f32[320,128]{1,0:T(8,128)S(1)} %slice_add_fusion.11), channel_id=1, source_target_pairs={{0,1},{1,0},{2,3},{3,2},{4,5},{5,4},{6,7},{7,6},{8,9},{9,8},{10,11... | collective-permute-start | bytes 491528 | tf_op jit(solution)/shard_map/ppermute | solution.py:174
  57.2 7.3 %collective-permute-start.8 = (f32[352,128]{1,0:T(8,128)S(1)}, f32[352,128]{1,0:T(8,128)S(1)}, u32[]{:S(2)}, u32[]{:S(2)}) collective-permute-start(f32[352,128]{1,0:T(8,128)S(1)} %slice_add_fusion.9), channel_id=1, source_target_pairs={{0,2},{2,0},{1,3},{3,1},{4,6},{6,4},{5,7},{7,5},{8,10},{10,8},{9,1... | collective-permute-start | bytes 540680 | tf_op jit(solution)/shard_map/ppermute | solution.py:174
  60.1 5.6 %collective-permute-start.11 = (f32[352,128]{1,0:T(8,128)S(1)}, f32[352,128]{1,0:T(8,128)S(1)}, u32[]{:S(2)}, u32[]{:S(2)}) collective-permute-start(f32[352,128]{1,0:T(8,128)S(1)} %slice_add_fusion.7), channel_id=1, source_target_pairs={{0,16},{16,0},{1,17},{17,1},{2,18},{18,2},{3,19},{19,3},{4,20},{20... | collective-permute-start | bytes 540680 | tf_op jit(solution)/shard_map/ppermute | solution.py:174
  65.7 10.1 %collective-permute-start.15 = (f32[1,512,128]{2,1,0:T(8,128)S(1)}, f32[1,512,128]{2,1,0:T(8,128)S(1)}, u32[]{:S(2)}, u32[]{:S(2)}) collective-permute-start(f32[1,512,128]{2,1,0:T(8,128)S(1)} %slice.235), channel_id=1, source_target_pairs={{0,4},{4,0},{1,5},{5,1},{2,6},{6,2},{3,7},{7,3},{8,12},{12,8},{9,1... | collective-permute-start | bytes 786440 | tf_op jit(solution)/shard_map/ppermute | solution.py:174
  75.9 1.6 %collective-permute-start.16 = (f32[512,128]{1,0:T(8,128)S(1)}, f32[512,128]{1,0:T(8,128)S(1)}, u32[]{:S(2)}, u32[]{:S(2)}) collective-permute-start(f32[512,128]{1,0:T(8,128)S(1)} %fusion.refs_0_), channel_id=1, source_target_pairs={{0,8},{8,0},{1,9},{9,1},{2,10},{10,2},{3,11},{11,3},{4,12},{12,4},... | collective-permute-start | bytes 786440 | tf_op jit(solution)/shard_map/ppermute | solution.py:174
  79.1 7.3 %collective-permute-start.17 = (f32[4,16,512]{2,1,0:T(8,128)S(1)}, f32[4,16,512]{2,1,0:T(8,128)S(1)}, u32[]{:S(2)}, u32[]{:S(2)}) collective-permute-start(f32[4,16,512]{2,1,0:T(8,128)S(1)} %fusion.6), channel_id=1, source_target_pairs={{0,17},{1,16},{16,1},{17,0},{2,19},{3,18},{18,3},{19,2},{4,21},{5,... | collective-permute-start | bytes 393224 | tf_op jit(solution)/shard_map/ppermute | solution.py:191
  80.3 7.4 %collective-permute-start.18 = (f32[4,16,512]{2,1,0:T(8,128)S(1)}, f32[4,16,512]{2,1,0:T(8,128)S(1)}, u32[]{:S(2)}, u32[]{:S(2)}) collective-permute-start(f32[4,16,512]{2,1,0:T(8,128)S(1)} %fusion.5), channel_id=1, source_target_pairs={{0,16},{1,17},{16,0},{17,1},{2,18},{3,19},{18,2},{19,3},{4,20},{5,... | collective-permute-start | bytes 393224 | tf_op jit(solution)/shard_map/ppermute | solution.py:191
  81.5 6.9 %collective-permute-start.19 = (f32[4,16,512]{2,1,0:T(8,128)S(1)}, f32[4,16,512]{2,1,0:T(8,128)S(1)}, u32[]{:S(2)}, u32[]{:S(2)}) collective-permute-start(f32[4,16,512]{2,1,0:T(8,128)S(1)} %fusion.4), channel_id=1, source_target_pairs={{0,1},{1,0},{16,17},{17,16},{2,3},{3,2},{18,19},{19,18},{4,5},{5,4... | collective-permute-start | bytes 393224 | tf_op jit(solution)/shard_map/ppermute | solution.py:191
  88.5 5.8 %collective-permute-start.20 = (f32[1,16,512]{2,1,0:T(8,128)S(1)}, f32[1,16,512]{2,1,0:T(8,128)S(1)}, u32[]{:S(2)}, u32[]{:S(2)}) collective-permute-start(f32[1,16,512]{2,1,0:T(8,128)S(1)} %slice_select_fusion.14), channel_id=1, source_target_pairs={{0,6},{2,4},{4,2},{6,0},{1,7},{3,5},{5,3},{7,1},{8,14},{10,12},{12... | collective-permute-start | bytes 98312 | tf_op jit(solution)/shard_map/ppermute | solution.py:191
  88.9 5.3 %collective-permute-start.21 = (f32[1,16,512]{2,1,0:T(8,128)S(1)}, f32[1,16,512]{2,1,0:T(8,128)S(1)}, u32[]{:S(2)}, u32[]{:S(2)}) collective-permute-start(f32[1,16,512]{2,1,0:T(8,128)S(1)} %slice_select_fusion.13), channel_id=1, source_target_pairs={{0,4},{2,6},{4,0},{6,2},{1,5},{3,7},{5,1},{7,3},{8,12},{10,14},{12... | collective-permute-start | bytes 98312 | tf_op jit(solution)/shard_map/ppermute | solution.py:191
  89.0 5.9 %collective-permute-start.22 = (f32[1,16,512]{2,1,0:T(8,128)S(1)}, f32[1,16,512]{2,1,0:T(8,128)S(1)}, u32[]{:S(2)}, u32[]{:S(2)}) collective-permute-start(f32[1,16,512]{2,1,0:T(8,128)S(1)} %slice_select_fusion.12), channel_id=1, source_target_pairs={{0,2},{2,0},{4,6},{6,4},{1,3},{3,1},{5,7},{7,5},{8,10},{10,8},{12,... | collective-permute-start | bytes 98312 | tf_op jit(solution)/shard_map/ppermute | solution.py:191

commit v3 on v2

--- a/solution.py
+++ b/solution.py
@@ -15,6 +15,7 @@
 LANES = 128
 BATCH = 16
 GROUPS = 1
+CHUNKS = 4
 NEGATIVE = 1 << 30
 
 
@@ -42,12 +43,15 @@
 def transform_kernel(own_ref, oth_ref, own_sign_ref, oth_sign_ref, table_ref, held_ref, part_ref, sems):
     blocks, cols = part_ref.shape[1], part_ref.shape[3]
     tiles = cols // LANES
+    chunk = blocks // CHUNKS
     copies = [
         pltpu.make_async_copy(
-            ref.at[pl.ds(b * BLOCK, BLOCK)], held_ref.at[core, b], sems.at[core, b]
+            ref.at[pl.ds(i * chunk * BLOCK, chunk * BLOCK)],
+            held_ref.at[core, pl.ds(i * chunk * BLOCK, chunk * BLOCK)],
+            sems.at[core, i],
         )
         for core, ref in enumerate((own_ref, oth_ref))
-        for b in range(blocks)
+        for i in range(CHUNKS)
     ]
     for copy in copies:
         copy.start()
@@ -59,9 +63,10 @@
     had = (1 - 2 * (common & 1)).astype(jnp.float32)
     for core, sign_ref in enumerate((own_sign_ref, oth_sign_ref)):
         for b in range(blocks):
-            copies[core * blocks + b].wait()
+            if b % chunk == 0:
+                copies[core * CHUNKS + b // chunk].wait()
             left = (had * sign_ref[b : b + 1, :]).astype(jnp.bfloat16)
-            full = held_ref[core, b]
+            full = held_ref[core, b * BLOCK : (b + 1) * BLOCK, :]
             high = full.astype(jnp.bfloat16)
             low = (full - high.astype(jnp.float32)).astype(jnp.bfloat16)
             part_ref[core, b] = jnp.dot(
@@ -94,13 +99,13 @@
         in_specs=[HBM, HBM, VMEM, VMEM],
         out_specs=VMEM,
         scratch_shapes=[
+            pltpu.VMEM((2, count, cols), jnp.float32),
             pltpu.VMEM((2, blocks, BLOCK, cols), jnp.float32),
-            pltpu.VMEM((2, blocks, BLOCK, cols), jnp.float32),
-            pltpu.SemaphoreType.DMA((2, blocks)),
+            pltpu.SemaphoreType.DMA((2, CHUNKS)),
         ],
-        compiler_params=limit(20),
+        compiler_params=limit(18),
         cost_estimate=cost(8 * count * BLOCK * cols, 16 * count * cols),
-    )(own, oth, own_sign, oth_sign)
+    )(*(pltpu.with_memory_space_constraint(x, pltpu.HBM) for x in (own, oth)), own_sign, oth_sign)
 
 
 def gather_kernel(plans, tiles, code_ref, table_ref, *out_refs):
@@ -223,11 +228,13 @@
     oth_design = swap(design, core)
     oth_signs = swap(signs, core)
     sign_rows = [(2 * s - 1).astype(jnp.float32).reshape(rows // BLOCK, BLOCK) for s in (signs, oth_signs)]
+    listing = steps
     listed = lax.optimization_barrier(samples ^ (own_index >> len(bits)))
-    for bit in steps[:-1]:
+    listed = jnp.concatenate([listed, swap(samples, listing[0])])
+    for bit in listing[1:-1]:
         listed = jnp.concatenate([listed, swap(listed, bit)])
     listed, oth_design = lax.optimization_barrier((listed, oth_design))
-    listed = jnp.concatenate([listed, swap(listed, steps[-1])])
+    listed = jnp.concatenate([listed, swap(listed, listing[-1])])
     mixed = transform(design, oth_design, *sign_rows)
 
     source = listed // rows
@@ -252,16 +259,17 @@
         order = orders[piece % 3]
         found = []
         for place in range(owners // 2):
-            owner = first << order[0]
+            owner = first << listing.index(steps[order[0]])
             for level, bit in enumerate(order[1:]):
-                owner |= (place >> (len(order) - 2 - level) & 1) << bit
+                owner |= (place >> (len(order) - 2 - level) & 1) << listing.index(steps[bit])
             found.append(owner * samp + sum(counts[:piece]))
         return found, counts[piece]
 
     arrived, held = [], []
-    for piece in range(3 * groups):
-        sent = gather([plan(piece, 1)], tiles, code, mixed)[0]
-        arrived.append(swap(sent, steps[piece % 3]))
+    for group in range(groups):
+        pieces = range(group * 3, group * 3 + 3)
+        sent = gather([plan(piece, 1) for piece in pieces], tiles, code, mixed)
+        arrived += [swap(rows_sent, steps[part]) for part, rows_sent in enumerate(sent)]
     for group in range(groups):
         held += gather([plan(group * 3 + part, 0) for part in range(3)], tiles, code, mixed)
     own_sums, oth_sums = [], []

time: 95.7 us -> 91 us (0.951)
  local copies, waits for them, and re-layouts: 2.26 us -> 0.07 us
  Pallas kernels: 15.4 us -> 13.4 us
    unnamed x3 -> x1, local copies, waits for them, and re-layouts: 2.19 us -> 0.01 us
    pallas_call x4 -> x2, Pallas kernels: 6.87 us -> 5.54 us  [gather(): pl.pallas_call(functools.partial(gather_kernel, plans, tiles), out_shape=...]
  transfers between devices with their start and end apart: 23 -> 23, of which waited for: 17 -> 17; matrix products, arithmetic and copies ran while one was open for 2% -> 2% of each run, Pallas kernels for 13% -> 10%
where the time goes in v3:
time: 91 us; the launch traced here: 90.8 us
  waiting for transfers between devices  44.3 us (49%)
  starting transfers between devices  29.2 us (32%)
  Pallas kernels  13.4 us (15%)
  other arithmetic  2.83 us (3%)
    ppermute x17, waiting for transfers between devices, swap(): return lax.ppermute(block, bit, [(0, 1), (1, 0)])  36.9 us
    ppermute x17, starting transfers between devices, swap(): return lax.ppermute(block, bit, [(0, 1), (1, 0)])  21.1 us
    ppermute x6, starting transfers between devices, reduce_pairs(): total += lax.ppermute(exclusive(block, own ^ flip, 0), axes, route)  8.12 us
    ppermute x6, waiting for transfers between devices, reduce_pairs(): total += lax.ppermute(exclusive(block, own ^ flip, 0), axes, route)  7.48 us
    pallas_call x1, Pallas kernels, transform(): pl.pallas_call(transform_kernel, out_shape=jax.ShapeDtypeStruct((2 * coun...  6.56 us
    pallas_call x2, Pallas kernels, gather(): pl.pallas_call(functools.partial(gather_kernel, plans, tiles), out_shape=...  5.54 us
  transfers between devices with their start and end apart: 23, of which 17 were waited for; matrix products, arithmetic and copies ran while one was open for 2% of the time, Pallas kernels for 10%

profile of v3, /device:TPU:0, one launch (start us, length us, event | category | flops | bytes accessed | tf_op | source)
XLA Modules:
  0.0 90.8 jit_solution(15567901654323234443)
XLA Ops:
  0.6 0.5 collective-permute-start.3
  1.1 2.6 %collective-permute-start = (s32[128]{0:T(128)}, s32[128]{0:T(128)S(1)}, u32[]{:S(2)}, u32[]{:S(2)}) collective-permute-start(s32[128]{0:T(128)} %param.5), channel_id=1, source_target_pairs={{0,16},{16,0},{1,17},{17,1},{2,18},{18,2},{3,19},{19,3},{4,20},{20... | collective-permute-start | bytes 1544 | tf_op jit(solution)/shard_map/ppermute | solution.py:179
  3.7 0.7 broadcast_xor_fusion
  4.4 1.0 %collective-permute-done = s32[128]{0:T(128)S(1)} collective-permute-done((s32[128]{0:T(128)}, s32[128]{0:T(128)S(1)}, u32[]{:S(2)}, u32[]{:S(2)}) %collective-permute-start) | collective-permute-done | bytes 544 | tf_op jit(solution)/shard_map/ppermute | solution.py:179
  5.4 2.0 %collective-permute-start.1 = (s32[256]{0:T(256)S(1)}, s32[256]{0:T(256)S(1)}, u32[]{:S(2)}, u32[]{:S(2)}) collective-permute-start(s32[256]{0:T(256)S(1)} %pad_add_fusion.2), channel_id=1, source_target_pairs={{0,1},{1,0},{2,3},{3,2},{4,5},{5,4},{6,7},{7,6},{8,9},{9,8},{10,11... | collective-permute-start | bytes 3080 | tf_op jit(solution)/shard_map/ppermute | solution.py:179
  7.4 0.0 collective-permute-start.5
  7.4 1.5 %collective-permute-done.1 = s32[256]{0:T(256)S(1)} collective-permute-done((s32[256]{0:T(256)S(1)}, s32[256]{0:T(256)S(1)}, u32[]{:S(2)}, u32[]{:S(2)}) %collective-permute-start.1) | collective-permute-done | bytes 1056 | tf_op jit(solution)/shard_map/ppermute | solution.py:179
  9.0 2.1 %collective-permute-start.2 = (s32[512]{0:T(512)S(1)}, s32[512]{0:T(512)S(1)}, u32[]{:S(2)}, u32[]{:S(2)}) collective-permute-start(s32[512]{0:T(512)S(1)} %pad_add_fusion.1), channel_id=1, source_target_pairs={{0,2},{2,0},{1,3},{3,1},{4,6},{6,4},{5,7},{7,5},{8,10},{10,8},{9,1... | collective-permute-start | bytes 6152 | tf_op jit(solution)/shard_map/ppermute | solution.py:179
  11.1 0.7 add_convert_fusion.1
  11.8 0.9 collective-permute-done.2
  12.6 0.0 collective-permute-done.5
  12.7 0.0 collective-permute-done.3.oth_ref
  12.7 3.1 %collective-permute-start.4 = (s32[1024]{0:T(1024)S(1)}, s32[1024]{0:T(1024)S(1)}, u32[]{:S(2)}, u32[]{:S(2)}) collective-permute-start(s32[1024]{0:T(1024)S(1)} %pad_add_fusion), channel_id=1, source_target_pairs={{0,4},{4,0},{1,5},{5,1},{2,6},{6,2},{3,7},{7,3},{8,12},{12,8},{9,1... | collective-permute-start | bytes 12296 | tf_op jit(solution)/shard_map/ppermute | solution.py:179
  15.8 6.6 %shard_map.50.table_ref = f32[16384,128]{1,0:T(8,128)S(1)} custom-call(f32[2048,512]{1,0:T(8,128)} %own_ref.1, f32[2048,512]{1,0:T(8,128)} %collective-permute-done.3.oth_ref, f32[8,256]{1,0:T(8,128)S(1)} %reshape.89.own_sign_ref, f32[8,256]{1,0:T(8,128)S(1)} %reshape.90.oth_sign_ref), custom_call_target="tpu_custom_call" | custom-call | flops 2147483648 | bytes 16777216 | tf_op jit(solution)/shard_map/pallas_call | solution.py:96
  22.4 0.0 collective-permute-done.4
  22.4 2.8 %shard_map.52 = (f32[1408,128]{1,0:T(8,128)S(1)}, f32[1408,128]{1,0:T(8,128)S(1)}, f32[1280,128]{1,0:T(8,128)S(1)}) custom-call(s32[2048]{0:T(1024)S(1)} %fusion.17.code_ref, f32[16384,128]{1,0:T(8,128)S(1)} %shard_map.50.table_ref), custom_call_target="tpu_custom_call" | custom-call | bytes 4194304 | tf_op jit(solution)/shard_map/pallas_call | solution.py:138
  25.2 1.6 %collective-permute-start.12 = (f32[1280,128]{1,0:T(8,128)S(1)}, f32[1280,128]{1,0:T(8,128)S(1)}, u32[]{:S(2)}, u32[]{:S(2)}) collective-permute-start(f32[1280,128]{1,0:T(8,128)S(1)} %get-tuple-element.19), channel_id=1, source_target_pairs={{0,2},{2,0},{1,3},{3,1},{4,6},{6,4},{5,7},{7,5},{8,10},{10,8},{9,1... | collective-permute-start | bytes 1966088 | tf_op jit(solution)/shard_map/ppermute | solution.py:179
  26.8 1.5 %collective-permute-start.6 = (f32[1408,128]{1,0:T(8,128)S(1)}, f32[1408,128]{1,0:T(8,128)S(1)}, u32[]{:S(2)}, u32[]{:S(2)}) collective-permute-start(f32[1408,128]{1,0:T(8,128)S(1)} %get-tuple-element.15), channel_id=1, source_target_pairs={{0,16},{16,0},{1,17},{17,1},{2,18},{18,2},{3,19},{19,3},{4,20},{20... | collective-permute-start | bytes 2162696 | tf_op jit(solution)/shard_map/ppermute | solution.py:179
  28.3 1.5 %collective-permute-start.9 = (f32[1408,128]{1,0:T(8,128)S(1)}, f32[1408,128]{1,0:T(8,128)S(1)}, u32[]{:S(2)}, u32[]{:S(2)}) collective-permute-start(f32[1408,128]{1,0:T(8,128)S(1)} %get-tuple-element.17), channel_id=1, source_target_pairs={{0,1},{1,0},{2,3},{3,2},{4,5},{5,4},{6,7},{7,6},{8,9},{9,8},{10,11... | collective-permute-start | bytes 2162696 | tf_op jit(solution)/shard_map/ppermute | solution.py:179
  29.8 2.8 %shard_map.51 = (f32[1408,128]{1,0:T(8,128)S(1)}, f32[1408,128]{1,0:T(8,128)S(1)}, f32[1280,128]{1,0:T(8,128)S(1)}) custom-call(s32[2048]{0:T(1024)S(1)} %fusion.17.code_ref, f32[16384,128]{1,0:T(8,128)S(1)} %shard_map.50.table_ref), custom_call_target="tpu_custom_call" | custom-call | bytes 4194304 | tf_op jit(solution)/shard_map/pallas_call | solution.py:138
  32.6 6.4 %collective-permute-done.12 = f32[1280,128]{1,0:T(8,128)S(1)} collective-permute-done((f32[1280,128]{1,0:T(8,128)S(1)}, f32[1280,128]{1,0:T(8,128)S(1)}, u32[]{:S(2)}, u32[]{:S(2)}) %collective-permute-start.12) | collective-permute-done | bytes 655392 | tf_op jit(solution)/shard_map/ppermute | solution.py:179
  39.0 0.1 slice_add_fusion.5
  39.1 1.5 %collective-permute-start.13 = (f32[640,128]{1,0:T(8,128)S(1)}, f32[640,128]{1,0:T(8,128)S(1)}, u32[]{:S(2)}, u32[]{:S(2)}) collective-permute-start(f32[640,128]{1,0:T(8,128)S(1)} %get-tuple-element.27), channel_id=1, source_target_pairs={{0,16},{16,0},{1,17},{17,1},{2,18},{18,2},{3,19},{19,3},{4,20},{20... | collective-permute-start | bytes 983048 | tf_op jit(solution)/shard_map/ppermute | solution.py:179
  40.6 4.6 %collective-permute-done.6 = f32[1408,128]{1,0:T(8,128)S(1)} collective-permute-done((f32[1408,128]{1,0:T(8,128)S(1)}, f32[1408,128]{1,0:T(8,128)S(1)}, u32[]{:S(2)}, u32[]{:S(2)}) %collective-permute-start.6) | collective-permute-done | bytes 720928 | tf_op jit(solution)/shard_map/ppermute | solution.py:179
  45.2 0.1 slice_add_fusion.3
  45.3 1.2 %collective-permute-start.7 = (f32[704,128]{1,0:T(8,128)S(1)}, f32[704,128]{1,0:T(8,128)S(1)}, u32[]{:S(2)}, u32[]{:S(2)}) collective-permute-start(f32[704,128]{1,0:T(8,128)S(1)} %get-tuple-element.23), channel_id=1, source_target_pairs={{0,1},{1,0},{2,3},{3,2},{4,5},{5,4},{6,7},{7,6},{8,9},{9,8},{10,11... | collective-permute-start | bytes 1081352 | tf_op jit(solution)/shard_map/ppermute | solution.py:179
  46.5 0.0 collective-permute-done.9
  46.5 0.1 slice_add_fusion.1
  46.6 0.1 collective-permute-start.10
  46.7 2.1 %collective-permute-done.13 = f32[640,128]{1,0:T(8,128)S(1)} collective-permute-done((f32[640,128]{1,0:T(8,128)S(1)}, f32[640,128]{1,0:T(8,128)S(1)}, u32[]{:S(2)}, u32[]{:S(2)}) %collective-permute-start.13) | collective-permute-done | bytes 327712 | tf_op jit(solution)/shard_map/ppermute | solution.py:179
  48.7 1.2 %collective-permute-start.14 = (f32[320,128]{1,0:T(8,128)S(1)}, f32[320,128]{1,0:T(8,128)S(1)}, u32[]{:S(2)}, u32[]{:S(2)}) collective-permute-start(f32[320,128]{1,0:T(8,128)S(1)} %slice_add_fusion.11), channel_id=1, source_target_pairs={{0,1},{1,0},{2,3},{3,2},{4,5},{5,4},{6,7},{7,6},{8,9},{9,8},{10,11... | collective-permute-start | bytes 491528 | tf_op jit(solution)/shard_map/ppermute | solution.py:179
  49.9 3.5 %collective-permute-done.7 = f32[704,128]{1,0:T(8,128)S(1)} collective-permute-done((f32[704,128]{1,0:T(8,128)S(1)}, f32[704,128]{1,0:T(8,128)S(1)}, u32[]{:S(2)}, u32[]{:S(2)}) %collective-permute-start.7) | collective-permute-done | bytes 360480 | tf_op jit(solution)/shard_map/ppermute | solution.py:179
  53.4 0.7 collective-permute-start.8
  54.2 1.2 %collective-permute-done.10 = f32[704,128]{1,0:T(8,128)S(1)} collective-permute-done((f32[704,128]{1,0:T(8,128)S(1)}, f32[704,128]{1,0:T(8,128)S(1)}, u32[]{:S(2)}, u32[]{:S(2)}) %collective-permute-start.10) | collective-permute-done | bytes 360480 | tf_op jit(solution)/shard_map/ppermute | solution.py:179
  55.4 0.6 collective-permute-start.11
  56.0 0.0 collective-permute-done.14
  56.0 4.6 %collective-permute-done.8 = f32[352,128]{1,0:T(8,128)S(1)} collective-permute-done((f32[352,128]{1,0:T(8,128)S(1)}, f32[352,128]{1,0:T(8,128)S(1)}, u32[]{:S(2)}, u32[]{:S(2)}) %collective-permute-start.8) | collective-permute-done | bytes 180256 | tf_op jit(solution)/shard_map/ppermute | solution.py:179
  60.7 0.2 collective-permute-done.11
  61.0 0.7 collective-permute-start.15
  61.8 9.4 %collective-permute-done.15 = f32[1,512,128]{2,1,0:T(8,128)S(1)} collective-permute-done((f32[1,512,128]{2,1,0:T(8,128)S(1)}, f32[1,512,128]{2,1,0:T(8,128)S(1)}, u32[]{:S(2)}, u32[]{:S(2)}) %collective-permute-start.15) | collective-permute-done | bytes 262176 | tf_op jit(solution)/shard_map/ppermute | solution.py:179
  71.2 0.1 collective-permute-start.16
  71.3 1.5 %collective-permute-done.16.refs_1_ = f32[512,128]{1,0:T(8,128)S(1)} collective-permute-done((f32[512,128]{1,0:T(8,128)S(1)}, f32[512,128]{1,0:T(8,128)S(1)}, u32[]{:S(2)}, u32[]{:S(2)}) %collective-permute-start.16) | collective-permute-done | bytes 262176 | tf_op jit(solution)/shard_map/ppermute | solution.py:179
  72.8 1.4 %shard_map.53 = (f32[128,512]{1,0:T(8,128)}, f32[256,512]{1,0:T(8,128)S(1)}) custom-call(s32[1]{0:T(128)} %bitcast.core_ref, f32[512,128]{1,0:T(8,128)S(1)} %fusion.refs_0_, f32[512,128]{1,0:T(8,128)S(1)} %collective-permute-done.16.refs_1_), custom_call_target="tpu_custom_call" | custom-call | flops 201326592 | bytes 1048576 | tf_op jit(solution)/shard_map/pallas_call | solution.py:294
  74.2 0.1 slice_select_fusion.3
  74.4 1.6 %collective-permute-start.17 = (f32[4,16,512]{2,1,0:T(8,128)S(1)}, f32[4,16,512]{2,1,0:T(8,128)S(1)}, u32[]{:S(2)}, u32[]{:S(2)}) collective-permute-start(f32[4,16,512]{2,1,0:T(8,128)S(1)} %fusion.6), channel_id=1, source_target_pairs={{0,17},{1,16},{16,1},{17,0},{2,19},{3,18},{18,3},{19,2},{4,21},{5,... | collective-permute-start | bytes 393224 | tf_op jit(solution)/shard_map/ppermute | solution.py:196
  76.0 1.2 %collective-permute-start.18 = (f32[4,16,512]{2,1,0:T(8,128)S(1)}, f32[4,16,512]{2,1,0:T(8,128)S(1)}, u32[]{:S(2)}, u32[]{:S(2)}) collective-permute-start(f32[4,16,512]{2,1,0:T(8,128)S(1)} %fusion.5), channel_id=1, source_target_pairs={{0,16},{1,17},{16,0},{17,1},{2,18},{3,19},{18,2},{19,3},{4,20},{5,... | collective-permute-start | bytes 393224 | tf_op jit(solution)/shard_map/ppermute | solution.py:196
  77.1 1.0 %collective-permute-start.19 = (f32[4,16,512]{2,1,0:T(8,128)S(1)}, f32[4,16,512]{2,1,0:T(8,128)S(1)}, u32[]{:S(2)}, u32[]{:S(2)}) collective-permute-start(f32[4,16,512]{2,1,0:T(8,128)S(1)} %fusion.4), channel_id=1, source_target_pairs={{0,1},{1,0},{16,17},{17,16},{2,3},{3,2},{18,19},{19,18},{4,5},{5,4... | collective-permute-start | bytes 393224 | tf_op jit(solution)/shard_map/ppermute | solution.py:196
  78.1 3.6 %collective-permute-done.17 = f32[4,16,512]{2,1,0:T(8,128)S(1)} collective-permute-done((f32[4,16,512]{2,1,0:T(8,128)S(1)}, f32[4,16,512]{2,1,0:T(8,128)S(1)}, u32[]{:S(2)}, u32[]{:S(2)}) %collective-permute-start.17) | collective-permute-done | bytes 131104 | tf_op jit(solution)/shard_map/ppermute | solution.py:196
  81.7 1.7 %collective-permute-done.18 = f32[4,16,512]{2,1,0:T(8,128)S(1)} collective-permute-done((f32[4,16,512]{2,1,0:T(8,128)S(1)}, f32[4,16,512]{2,1,0:T(8,128)S(1)}, u32[]{:S(2)}, u32[]{:S(2)}) %collective-permute-start.18) | collective-permute-done | bytes 131104 | tf_op jit(solution)/shard_map/ppermute | solution.py:196
  83.4 0.3 collective-permute-done.19
  83.8 0.3 collective-permute-start.20
  84.1 0.0 collective-permute-start.21
  84.1 4.1 %collective-permute-start.22 = (f32[1,16,512]{2,1,0:T(8,128)S(1)}, f32[1,16,512]{2,1,0:T(8,128)S(1)}, u32[]{:S(2)}, u32[]{:S(2)}) collective-permute-start(f32[1,16,512]{2,1,0:T(8,128)S(1)} %slice_select_fusion.12), channel_id=1, source_target_pairs={{0,2},{2,0},{4,6},{6,4},{1,3},{3,1},{5,7},{7,5},{8,10},{10,8},{12,... | collective-permute-start | bytes 98312 | tf_op jit(solution)/shard_map/ppermute | solution.py:196
  88.3 1.3 %collective-permute-done.20 = f32[1,16,512]{2,1,0:T(8,128)S(1)} collective-permute-done((f32[1,16,512]{2,1,0:T(8,128)S(1)}, f32[1,16,512]{2,1,0:T(8,128)S(1)}, u32[]{:S(2)}, u32[]{:S(2)}) %collective-permute-start.20) | collective-permute-done | bytes 32800 | tf_op jit(solution)/shard_map/ppermute | solution.py:196
  89.6 0.0 collective-permute-done.21
  89.6 0.6 collective-permute-done.22
  90.2 0.6 fusion.14
  (27 shorter events, 0.5 us)
Async XLA Ops:
  0.6 12.0 %collective-permute-start.3 = (f32[2048,512]{1,0:T(8,128)}, f32[2048,512]{1,0:T(8,128)}, u32[]{:S(2)}, u32[]{:S(2)}) collective-permute-start(f32[2048,512]{1,0:T(8,128)} %own_ref.1), channel_id=1, source_target_pairs={{0,8},{8,0},{1,9},{9,1},{2,10},{10,2},{3,11},{11,3},{4,12},{12,4},... | collective-permute-start | bytes 12582920 | tf_op jit(solution)/shard_map/ppermute | solution.py:179
  1.1 4.2 %collective-permute-start = (s32[128]{0:T(128)}, s32[128]{0:T(128)S(1)}, u32[]{:S(2)}, u32[]{:S(2)}) collective-permute-start(s32[128]{0:T(128)} %param.5), channel_id=1, source_target_pairs={{0,16},{16,0},{1,17},{17,1},{2,18},{18,2},{3,19},{19,3},{4,20},{20... | collective-permute-start | bytes 1544 | tf_op jit(solution)/shard_map/ppermute | solution.py:179
  5.4 3.6 %collective-permute-start.1 = (s32[256]{0:T(256)S(1)}, s32[256]{0:T(256)S(1)}, u32[]{:S(2)}, u32[]{:S(2)}) collective-permute-start(s32[256]{0:T(256)S(1)} %pad_add_fusion.2), channel_id=1, source_target_pairs={{0,1},{1,0},{2,3},{3,2},{4,5},{5,4},{6,7},{7,6},{8,9},{9,8},{10,11... | collective-permute-start | bytes 3080 | tf_op jit(solution)/shard_map/ppermute | solution.py:179
  7.4 5.2 %collective-permute-start.5 = (s32[2048]{0:T(1024)}, s32[2048]{0:T(1024)S(1)}, u32[]{:S(2)}, u32[]{:S(2)}) collective-permute-start(s32[2048]{0:T(1024)} %param.4), channel_id=1, source_target_pairs={{0,8},{8,0},{1,9},{9,1},{2,10},{10,2},{3,11},{11,3},{4,12},{12,4},... | collective-permute-start | bytes 24584 | tf_op jit(solution)/shard_map/ppermute | solution.py:179
  9.0 3.6 %collective-permute-start.2 = (s32[512]{0:T(512)S(1)}, s32[512]{0:T(512)S(1)}, u32[]{:S(2)}, u32[]{:S(2)}) collective-permute-start(s32[512]{0:T(512)S(1)} %pad_add_fusion.1), channel_id=1, source_target_pairs={{0,2},{2,0},{1,3},{3,1},{4,6},{6,4},{5,7},{7,5},{8,10},{10,8},{9,1... | collective-permute-start | bytes 6152 | tf_op jit(solution)/shard_map/ppermute | solution.py:179
  12.7 9.7 %collective-permute-start.4 = (s32[1024]{0:T(1024)S(1)}, s32[1024]{0:T(1024)S(1)}, u32[]{:S(2)}, u32[]{:S(2)}) collective-permute-start(s32[1024]{0:T(1024)S(1)} %pad_add_fusion), channel_id=1, source_target_pairs={{0,4},{4,0},{1,5},{5,1},{2,6},{6,2},{3,7},{7,3},{8,12},{12,8},{9,1... | collective-permute-start | bytes 12296 | tf_op jit(solution)/shard_map/ppermute | solution.py:179
  25.2 13.8 %collective-permute-start.12 = (f32[1280,128]{1,0:T(8,128)S(1)}, f32[1280,128]{1,0:T(8,128)S(1)}, u32[]{:S(2)}, u32[]{:S(2)}) collective-permute-start(f32[1280,128]{1,0:T(8,128)S(1)} %get-tuple-element.19), channel_id=1, source_target_pairs={{0,2},{2,0},{1,3},{3,1},{4,6},{6,4},{5,7},{7,5},{8,10},{10,8},{9,1... | collective-permute-start | bytes 1966088 | tf_op jit(solution)/shard_map/ppermute | solution.py:179
  26.8 18.4 %collective-permute-start.6 = (f32[1408,128]{1,0:T(8,128)S(1)}, f32[1408,128]{1,0:T(8,128)S(1)}, u32[]{:S(2)}, u32[]{:S(2)}) collective-permute-start(f32[1408,128]{1,0:T(8,128)S(1)} %get-tuple-element.15), channel_id=1, source_target_pairs={{0,16},{16,0},{1,17},{17,1},{2,18},{18,2},{3,19},{19,3},{4,20},{20... | collective-permute-start | bytes 2162696 | tf_op jit(solution)/shard_map/ppermute | solution.py:179
  28.3 18.2 %collective-permute-start.9 = (f32[1408,128]{1,0:T(8,128)S(1)}, f32[1408,128]{1,0:T(8,128)S(1)}, u32[]{:S(2)}, u32[]{:S(2)}) collective-permute-start(f32[1408,128]{1,0:T(8,128)S(1)} %get-tuple-element.17), channel_id=1, source_target_pairs={{0,1},{1,0},{2,3},{3,2},{4,5},{5,4},{6,7},{7,6},{8,9},{9,8},{10,11... | collective-permute-start | bytes 2162696 | tf_op jit(solution)/shard_map/ppermute | solution.py:179
  39.1 9.6 %collective-permute-start.13 = (f32[640,128]{1,0:T(8,128)S(1)}, f32[640,128]{1,0:T(8,128)S(1)}, u32[]{:S(2)}, u32[]{:S(2)}) collective-permute-start(f32[640,128]{1,0:T(8,128)S(1)} %get-tuple-element.27), channel_id=1, source_target_pairs={{0,16},{16,0},{1,17},{17,1},{2,18},{18,2},{3,19},{19,3},{4,20},{20... | collective-permute-start | bytes 983048 | tf_op jit(solution)/shard_map/ppermute | solution.py:179
  45.3 8.1 %collective-permute-start.7 = (f32[704,128]{1,0:T(8,128)S(1)}, f32[704,128]{1,0:T(8,128)S(1)}, u32[]{:S(2)}, u32[]{:S(2)}) collective-permute-start(f32[704,128]{1,0:T(8,128)S(1)} %get-tuple-element.23), channel_id=1, source_target_pairs={{0,1},{1,0},{2,3},{3,2},{4,5},{5,4},{6,7},{7,6},{8,9},{9,8},{10,11... | collective-permute-start | bytes 1081352 | tf_op jit(solution)/shard_map/ppermute | solution.py:179
  46.6 8.8 %collective-permute-start.10 = (f32[704,128]{1,0:T(8,128)S(1)}, f32[704,128]{1,0:T(8,128)S(1)}, u32[]{:S(2)}, u32[]{:S(2)}) collective-permute-start(f32[704,128]{1,0:T(8,128)S(1)} %get-tuple-element.25), channel_id=1, source_target_pairs={{0,2},{2,0},{1,3},{3,1},{4,6},{6,4},{5,7},{7,5},{8,10},{10,8},{9,1... | collective-permute-start | bytes 1081352 | tf_op jit(solution)/shard_map/ppermute | solution.py:179
  48.7 7.2 %collective-permute-start.14 = (f32[320,128]{1,0:T(8,128)S(1)}, f32[320,128]{1,0:T(8,128)S(1)}, u32[]{:S(2)}, u32[]{:S(2)}) collective-permute-start(f32[320,128]{1,0:T(8,128)S(1)} %slice_add_fusion.11), channel_id=1, source_target_pairs={{0,1},{1,0},{2,3},{3,2},{4,5},{5,4},{6,7},{7,6},{8,9},{9,8},{10,11... | collective-permute-start | bytes 491528 | tf_op jit(solution)/shard_map/ppermute | solution.py:179
  53.4 7.2 %collective-permute-start.8 = (f32[352,128]{1,0:T(8,128)S(1)}, f32[352,128]{1,0:T(8,128)S(1)}, u32[]{:S(2)}, u32[]{:S(2)}) collective-permute-start(f32[352,128]{1,0:T(8,128)S(1)} %slice_add_fusion.9), channel_id=1, source_target_pairs={{0,2},{2,0},{1,3},{3,1},{4,6},{6,4},{5,7},{7,5},{8,10},{10,8},{9,1... | collective-permute-start | bytes 540680 | tf_op jit(solution)/shard_map/ppermute | solution.py:179
  55.4 5.6 %collective-permute-start.11 = (f32[352,128]{1,0:T(8,128)S(1)}, f32[352,128]{1,0:T(8,128)S(1)}, u32[]{:S(2)}, u32[]{:S(2)}) collective-permute-start(f32[352,128]{1,0:T(8,128)S(1)} %slice_add_fusion.7), channel_id=1, source_target_pairs={{0,16},{16,0},{1,17},{17,1},{2,18},{18,2},{3,19},{19,3},{4,20},{20... | collective-permute-start | bytes 540680 | tf_op jit(solution)/shard_map/ppermute | solution.py:179
  61.0 10.1 %collective-permute-start.15 = (f32[1,512,128]{2,1,0:T(8,128)S(1)}, f32[1,512,128]{2,1,0:T(8,128)S(1)}, u32[]{:S(2)}, u32[]{:S(2)}) collective-permute-start(f32[1,512,128]{2,1,0:T(8,128)S(1)} %slice.235), channel_id=1, source_target_pairs={{0,4},{4,0},{1,5},{5,1},{2,6},{6,2},{3,7},{7,3},{8,12},{12,8},{9,1... | collective-permute-start | bytes 786440 | tf_op jit(solution)/shard_map/ppermute | solution.py:179
  71.2 1.6 %collective-permute-start.16 = (f32[512,128]{1,0:T(8,128)S(1)}, f32[512,128]{1,0:T(8,128)S(1)}, u32[]{:S(2)}, u32[]{:S(2)}) collective-permute-start(f32[512,128]{1,0:T(8,128)S(1)} %fusion.refs_0_), channel_id=1, source_target_pairs={{0,8},{8,0},{1,9},{9,1},{2,10},{10,2},{3,11},{11,3},{4,12},{12,4},... | collective-permute-start | bytes 786440 | tf_op jit(solution)/shard_map/ppermute | solution.py:179
  74.4 7.3 %collective-permute-start.17 = (f32[4,16,512]{2,1,0:T(8,128)S(1)}, f32[4,16,512]{2,1,0:T(8,128)S(1)}, u32[]{:S(2)}, u32[]{:S(2)}) collective-permute-start(f32[4,16,512]{2,1,0:T(8,128)S(1)} %fusion.6), channel_id=1, source_target_pairs={{0,17},{1,16},{16,1},{17,0},{2,19},{3,18},{18,3},{19,2},{4,21},{5,... | collective-permute-start | bytes 393224 | tf_op jit(solution)/shard_map/ppermute | solution.py:196
  76.0 7.4 %collective-permute-start.18 = (f32[4,16,512]{2,1,0:T(8,128)S(1)}, f32[4,16,512]{2,1,0:T(8,128)S(1)}, u32[]{:S(2)}, u32[]{:S(2)}) collective-permute-start(f32[4,16,512]{2,1,0:T(8,128)S(1)} %fusion.5), channel_id=1, source_target_pairs={{0,16},{1,17},{16,0},{17,1},{2,18},{3,19},{18,2},{19,3},{4,20},{5,... | collective-permute-start | bytes 393224 | tf_op jit(solution)/shard_map/ppermute | solution.py:196
  77.1 6.5 %collective-permute-start.19 = (f32[4,16,512]{2,1,0:T(8,128)S(1)}, f32[4,16,512]{2,1,0:T(8,128)S(1)}, u32[]{:S(2)}, u32[]{:S(2)}) collective-permute-start(f32[4,16,512]{2,1,0:T(8,128)S(1)} %fusion.4), channel_id=1, source_target_pairs={{0,1},{1,0},{16,17},{17,16},{2,3},{3,2},{18,19},{19,18},{4,5},{5,4... | collective-permute-start | bytes 393224 | tf_op jit(solution)/shard_map/ppermute | solution.py:196
  83.8 5.8 %collective-permute-start.20 = (f32[1,16,512]{2,1,0:T(8,128)S(1)}, f32[1,16,512]{2,1,0:T(8,128)S(1)}, u32[]{:S(2)}, u32[]{:S(2)}) collective-permute-start(f32[1,16,512]{2,1,0:T(8,128)S(1)} %slice_select_fusion.14), channel_id=1, source_target_pairs={{0,6},{2,4},{4,2},{6,0},{1,7},{3,5},{5,3},{7,1},{8,14},{10,12},{12... | collective-permute-start | bytes 98312 | tf_op jit(solution)/shard_map/ppermute | solution.py:196
  84.1 5.5 %collective-permute-start.21 = (f32[1,16,512]{2,1,0:T(8,128)S(1)}, f32[1,16,512]{2,1,0:T(8,128)S(1)}, u32[]{:S(2)}, u32[]{:S(2)}) collective-permute-start(f32[1,16,512]{2,1,0:T(8,128)S(1)} %slice_select_fusion.13), channel_id=1, source_target_pairs={{0,4},{2,6},{4,0},{6,2},{1,5},{3,7},{5,1},{7,3},{8,12},{10,14},{12... | collective-permute-start | bytes 98312 | tf_op jit(solution)/shard_map/ppermute | solution.py:196
  84.1 6.0 %collective-permute-start.22 = (f32[1,16,512]{2,1,0:T(8,128)S(1)}, f32[1,16,512]{2,1,0:T(8,128)S(1)}, u32[]{:S(2)}, u32[]{:S(2)}) collective-permute-start(f32[1,16,512]{2,1,0:T(8,128)S(1)} %slice_select_fusion.12), channel_id=1, source_target_pairs={{0,2},{2,0},{4,6},{6,4},{1,3},{3,1},{5,7},{7,5},{8,10},{10,8},{12,... | collective-permute-start | bytes 98312 | tf_op jit(solution)/shard_map/ppermute | solution.py:196

commit v4 on v2

v4 whole, which is shorter than its diff:
```python
import functools
import math

import jax
import jax.numpy as jnp
from jax import lax
from jax.experimental import pallas as pl
from jax.experimental.pallas import tpu as pltpu
from jax.sharding import Mesh, PartitionSpec as P

HBM = pl.BlockSpec(memory_space=pltpu.HBM)
VMEM = pl.BlockSpec(memory_space=pltpu.VMEM)
SMEM = pl.BlockSpec(memory_space=pltpu.SMEM)
BLOCK = 256
LANES = 128
CHUNKS = 2


def limit(mib):
    return pltpu.CompilerParams(vmem_limit_bytes=mib * 1024 * 1024)


def cost(flops, moved):
    return pl.CostEstimate(flops=flops, bytes_accessed=moved, transcendentals=0)


def walsh(values):
    half = 1
    while half < len(values):
        out = list(values)
        for i in range(len(values)):
            if not i & half:
                out[i] = values[i] + values[i | half]
                out[i | half] = values[i] - values[i | half]
        values = out
        half *= 2
    return values


def blocks_kernel(rows_ref, sign_ref, part_ref, zero_ref, held_ref, sems):
    zero_ref[...] = jnp.zeros_like(zero_ref)
    blocks = part_ref.shape[0]
    chunk = blocks // CHUNKS
    copies = []
    for i in range(CHUNKS):
        window = pl.ds(i * chunk * BLOCK, chunk * BLOCK)
        copies.append(pltpu.make_async_copy(rows_ref.at[window], held_ref.at[window], sems.at[i]))
        copies[i].start()
    common = lax.broadcasted_iota(jnp.int32, (BLOCK, BLOCK), 0) & lax.broadcasted_iota(
        jnp.int32, (BLOCK, BLOCK), 1
    )
    for shift in (4, 2, 1):
        common = common ^ (common >> shift)
    had = (1 - 2 * (common & 1)).astype(jnp.float32)
    for b in range(blocks):
        if b % chunk == 0:
            copies[b // chunk].wait()
        left = (had * sign_ref[b : b + 1, :]).astype(jnp.bfloat16)
        full = held_ref[b * BLOCK : (b + 1) * BLOCK, :]
        high = full.astype(jnp.bfloat16)
        low = (full - high.astype(jnp.float32)).astype(jnp.bfloat16)
        part_ref[b] = jnp.dot(
            jnp.concatenate([left, left], axis=1),
            jnp.concatenate([high, low], axis=0),
            preferred_element_type=jnp.float32,
        )


def transform_blocks(rows, sign, length):
    count, cols = rows.shape
    blocks = count // BLOCK
    return pl.pallas_call(
        blocks_kernel,
        out_shape=[
            jax.ShapeDtypeStruct((blocks, BLOCK, cols), jnp.float32),
            jax.ShapeDtypeStruct((length,), jnp.int32),
        ],
        in_specs=[HBM, VMEM],
        out_specs=[VMEM, VMEM],
        scratch_shapes=[pltpu.VMEM((count, cols), jnp.float32), pltpu.SemaphoreType.DMA((CHUNKS,))],
        compiler_params=limit(8),
        cost_estimate=cost(4 * count * BLOCK * cols, 8 * count * cols),
    )(pltpu.with_memory_space_constraint(rows, pltpu.HBM), sign)


def merge_kernel(own_ref, oth_ref, table_ref):
    blocks, _, cols = own_ref.shape
    tiles = cols // LANES

    def one_chunk(step, carry):
        start = pl.multiple_of(step * 8, 8)
        for tile in range(tiles):
            lanes = slice(tile * LANES, (tile + 1) * LANES)
            own = walsh([own_ref[b, pl.ds(start, 8), lanes] for b in range(blocks)])
            oth = walsh([oth_ref[b, pl.ds(start, 8), lanes] for b in range(blocks)])
            for b in range(blocks):
                for core, value in enumerate((own[b] + oth[b], own[b] - oth[b])):
                    row = (core * blocks + b) * BLOCK + start
                    table_ref[pl.ds(row * tiles + tile, 8, stride=tiles), :] = value
        return carry

    lax.fori_loop(0, BLOCK // 8, one_chunk, 0)


def merge(own, oth):
    blocks, _, cols = own.shape
    return pl.pallas_call(
        merge_kernel,
        out_shape=jax.ShapeDtypeStruct((2 * blocks * BLOCK * cols // LANES, LANES), jnp.float32),
        in_specs=[VMEM, VMEM],
        out_specs=VMEM,
        compiler_params=limit(4),
        cost_estimate=cost(10 * blocks * BLOCK * cols, 16 * blocks * BLOCK * cols),
    )(own, oth)


def gather_kernel(plans, tiles, at_ref, sign_ref, table_ref, *out_refs):
    for out_ref, (fixed, places, skip, count) in zip(out_refs, plans):

        def one_owner(place, carry, out_ref=out_ref, fixed=fixed, places=places, skip=skip, count=count):
            owner = fixed
            for i, bit in enumerate(places):
                owner = owner + ((place >> i & 1) << bit)
            first = owner * count[0] + skip
            rows = []
            for i in range(count[1]):
                at = pl.multiple_of(at_ref[first + i], tiles)
                rows.append(table_ref[pl.ds(at, tiles), :] * sign_ref[first + i])
            for i, row in enumerate(rows):
                to = pl.multiple_of((place * count[1] + i) * tiles, tiles)
                out_ref[pl.ds(to, tiles), :] = row
            return carry

        lax.fori_loop(0, 2 ** len(places), one_owner, 0)


def gather(plans, tiles, at, sign, table):
    total = [2 ** len(places) * count[1] for _, places, _, count in plans]
    return pl.pallas_call(
        functools.partial(gather_kernel, plans, tiles),
        out_shape=[jax.ShapeDtypeStruct((rows * tiles, LANES), jnp.float32) for rows in total],
        in_specs=[SMEM, SMEM, VMEM],
        out_specs=[VMEM] * len(plans),
        compiler_params=limit(4),
        cost_estimate=cost(0, 8 * sum(total) * tiles * LANES),
    )(at, sign, table)


def gram_kernel(scale, inverse_total, core_ref, own_ref, oth_ref, sketch_ref, gram_ref, high_ref, low_ref):
    samp, cols = sketch_ref.shape
    tiles = cols // LANES
    for which, ref in enumerate((own_ref, oth_ref)):
        for tile in range(tiles):
            lanes = slice(tile * LANES, (tile + 1) * LANES)
            value = ref[pl.ds(tile, samp, stride=tiles), :] * scale
            if not which:
                sketch_ref[:, lanes] = value
            high = value.astype(jnp.bfloat16)
            high_ref[which * samp : (which + 1) * samp, lanes] = high
            low_ref[which * samp : (which + 1) * samp, lanes] = (
                value - high.astype(jnp.float32)
            ).astype(jnp.bfloat16)
    width = gram_ref.shape[0] // 2
    for upper in range(2):
        start = pl.multiple_of(upper * (cols // 2) + core_ref[0] * width, LANES)
        total = None
        for left_ref, right_ref in ((high_ref, high_ref), (high_ref, low_ref), (low_ref, high_ref)):
            term = lax.dot_general(
                left_ref[:, pl.ds(start, width)],
                right_ref[...],
                (((0,), (0,)), ((), ())),
                preferred_element_type=jnp.float32,
            )
            total = term if total is None else total + term
        gram_ref[upper * width : (upper + 1) * width, :] = total * inverse_total


def swap(block, bit):
    return lax.ppermute(block, bit, [(0, 1), (1, 0)])


def exclusive(block, place, axis):
    while block.shape[axis] > 1:
        half = block.shape[axis] // 2
        upper = lax.slice_in_dim(block, half, 2 * half, axis=axis)
        lower = lax.slice_in_dim(block, 0, half, axis=axis)
        block = jnp.where(place & half == half, upper, lower)
    return jnp.squeeze(block, axis)


def reduce_pairs(block, axes):
    own = lax.axis_index(axes)
    total = exclusive(block, own, 0)
    for flip in (3, 2, 1):
        route = [(i, i ^ flip) for i in range(4)]
        total += lax.ppermute(exclusive(block, own ^ flip, 0), axes, route)
    return total


def reduce_gram(block, high, low):
    first, rest = low[0], low[1:]
    block = block.reshape(2, -1, 2, *block.shape[2:])
    block = jnp.moveaxis(block, 2, 1).reshape(4, -1, *block.shape[3:])
    block = reduce_pairs(block, (high, first))
    while rest:
        if len(rest) >= 2:
            block = reduce_pairs(block.reshape(4, -1, *block.shape[1:]), (rest[-1], rest[-2]))
            rest = rest[:-2]
        else:
            last = rest[-1]
            own = lax.axis_index(last)
            block = block.reshape(2, -1, *block.shape[1:])
            block = exclusive(block, own, 0) + swap(exclusive(block, 1 - own, 0), last)
            rest = rest[:-1]
    return block[0]


def per_device(bits, design, signs, samples):
    rows, cols = design.shape
    samp = samples.shape[0]
    tiles = cols // LANES
    devices = 2 ** len(bits)
    high, core, low = bits[0], bits[1], bits[:1:-1]
    steps = [high, *low]
    own_index = lax.axis_index(tuple(bits))
    core_bit = len(low)

    own_sign = (2 * signs - 1).astype(jnp.float32).reshape(rows // BLOCK, BLOCK)
    oth_design = swap(design, core)
    oth_sign = swap(own_sign, core)
    listing = steps
    listed = lax.optimization_barrier(samples ^ (own_index >> len(bits)))
    listed = jnp.concatenate([listed, swap(samples, listing[0])])
    for i, bit in enumerate(listing[1:], 1):
        listed = jnp.concatenate([listed, swap(listed, bit)])
        if i == 1:
            own_blocks, zeros = transform_blocks(design, own_sign, listed.shape[0])
            listed = listed + zeros
        if i == len(steps) - 2:
            oth_blocks, zeros = transform_blocks(oth_design, oth_sign, listed.shape[0])
            listed = listed + zeros
    mixed = merge(own_blocks, oth_blocks)

    source = listed // rows
    parity = source & own_index
    shift = 1
    while shift < devices:
        parity = parity ^ (parity >> shift)
        shift *= 2
    at = ((source >> core_bit & 1) * rows + listed % rows) * tiles
    sign = (1 - 2 * (parity & 1)).astype(jnp.float32)

    third = (samp // 3 + 2) // 2 * 2
    counts = [third, third, samp - 2 * third]
    orders = []
    for part in range(3):
        order = [(part + i) % 3 for i in range(3)]
        orders.append(order + list(range(3, len(steps))))

    def plan(part, first):
        places = [listing.index(steps[bit]) for bit in orders[part]]
        return first << places[0], places[:0:-1], sum(counts[:part]), (samp, counts[part])

    parts = range(3)
    sent = gather([plan(part, 1) for part in parts], tiles, at, sign, mixed)
    arrived = [swap(sent[part], steps[part]) for part in parts]
    held = list(gather([plan(part, 0) for part in parts], tiles, at, sign, mixed))
    for level in range(1, 3):
        for part in parts:
            half = held[part].shape[0] // 2
            send = held[part][half:] + arrived[part][half:]
            held[part] = held[part][:half] + arrived[part][:half]
            arrived[part] = swap(send, steps[orders[part][level]])
    done = []
    for members in ((2,), (0, 1)):
        whole = jnp.concatenate(
            [(held[part] + arrived[part]).reshape(-1, counts[part] * tiles, LANES) for part in members], axis=1
        )
        for level in range(3, len(steps)):
            half = whole.shape[0] // 2
            whole = whole[:half] + swap(whole[half:], steps[level])
        done.append(whole[0])
    own_sum = jnp.concatenate([done[1], done[0]])
    oth_sum = swap(own_sum, core)

    half_rows = cols // 2
    sketch, product = pl.pallas_call(
        functools.partial(gram_kernel, 1.0 / math.sqrt(rows * devices), 1.0 / (samp * devices)),
        out_shape=[
            jax.ShapeDtypeStruct((samp, cols), jnp.float32),
            jax.ShapeDtypeStruct((half_rows, cols), jnp.float32),
        ],
        in_specs=[SMEM] + [VMEM] * 2,
        out_specs=[VMEM, VMEM],
        scratch_shapes=[pltpu.VMEM((2 * samp, cols), jnp.bfloat16)] * 2,
        compiler_params=limit(8),
        cost_estimate=cost(24 * samp * samp * cols, 16 * samp * cols),
    )(lax.axis_index(core).astype(jnp.int32).reshape(1), own_sum, oth_sum)

    gram = reduce_gram(product.reshape(2, 2 ** len(low), -1, cols), high, low)
    return sketch, gram


def solution(mesh):
    width = [size.bit_length() - 1 for size in mesh.devices.shape]
    bits = [f"{axis}{i}" for axis, w in zip(mesh.axis_names, width) for i in reversed(range(w))]
    split = Mesh(mesh.devices.reshape((2,) * len(bits)), tuple(bits))
    every = tuple(bits)
    return jax.shard_map(
        functools.partial(per_device, bits),
        mesh=split,
        in_specs=(P(every, None), P(every), P(every)),
        out_specs=(P(every, None), P(every, None)),
        check_vma=False,
    )
```

time: 95.7 us -> 87.6 us (0.915)
  waiting for transfers between devices: 44.3 us -> 34.9 us
  starting transfers between devices: 29.8 us -> 35.7 us
  Pallas kernels: 15.4 us -> 13 us
  local copies, waits for them, and re-layouts: 2.26 us -> 0.05 us
    ppermute x17 -> x18, waiting for transfers between devices: 36.9 us -> 25.4 us  [swap(): return lax.ppermute(block, bit, [(0, 1), (1, 0)])]
    ppermute x17 -> x18, starting transfers between devices: 21.7 us -> 27.6 us  [swap(): return lax.ppermute(block, bit, [(0, 1), (1, 0)])]
    pallas_call x4 -> x2, Pallas kernels: 6.87 us -> 4.17 us  [gather(): pl.pallas_call(functools.partial(gather_kernel, plans, tiles), out_shape=...]
    unnamed x3 -> x0, local copies, waits for them, and re-layouts: 2.19 us -> none
    ppermute x6, waiting for transfers between devices: 7.48 us -> 9.5 us  [reduce_pairs(): total += lax.ppermute(exclusive(block, own ^ flip, 0), axes, route)]
    pallas_call x1 -> x3, Pallas kernels: 7.22 us -> 7.9 us  [the longest x2 6.12 us: transform_blocks(): pl.pallas_call(blocks_kernel, out_shape=[jax.ShapeDtypeStruct((blocks, BL...]
  transfers between devices with their start and end apart: 23 -> 24, of which waited for: 17 -> 16; matrix products, arithmetic and copies ran while one was open for 2% -> 2% of each run, Pallas kernels for 13% -> 11%
where the time goes in v4:
time: 87.6 us; the launch traced here: 87.4 us
  starting transfers between devices  35.7 us (41%)
  waiting for transfers between devices  34.9 us (40%)
  Pallas kernels  13 us (15%)
  other arithmetic  2.73 us (3%)
  between operations  0.89 us (1%)
    ppermute x18, starting transfers between devices, swap(): return lax.ppermute(block, bit, [(0, 1), (1, 0)])  27.6 us
    ppermute x18, waiting for transfers between devices, swap(): return lax.ppermute(block, bit, [(0, 1), (1, 0)])  25.4 us
    ppermute x6, waiting for transfers between devices, reduce_pairs(): total += lax.ppermute(exclusive(block, own ^ flip, 0), axes, route)  9.5 us
    ppermute x6, starting transfers between devices, reduce_pairs(): total += lax.ppermute(exclusive(block, own ^ flip, 0), axes, route)  8.11 us
    pallas_call x2, Pallas kernels, transform_blocks(): pl.pallas_call(blocks_kernel, out_shape=[jax.ShapeDtypeStruct((blocks, BL...  6.12 us
    pallas_call x2, Pallas kernels, gather(): pl.pallas_call(functools.partial(gather_kernel, plans, tiles), out_shape=...  4.17 us
    pallas_call x1, Pallas kernels, merge(): pl.pallas_call(merge_kernel, out_shape=jax.ShapeDtypeStruct((2 * blocks *...  1.78 us
  transfers between devices with their start and end apart: 24, of which 16 were waited for; matrix products, arithmetic and copies ran while one was open for 2% of the time, Pallas kernels for 11%

profile of v4, /device:TPU:0, one launch (start us, length us, event | category | flops | bytes accessed | tf_op | source)
XLA Modules:
  0.0 87.4 jit_solution(3650710142398617667)
XLA Ops:
  0.6 0.5 collective-permute-start.3
  1.1 2.6 %collective-permute-start = (s32[128]{0:T(128)}, s32[128]{0:T(128)S(1)}, u32[]{:S(2)}, u32[]{:S(2)}) collective-permute-start(s32[128]{0:T(128)} %param.5), channel_id=1, source_target_pairs={{0,16},{16,0},{1,17},{17,1},{2,18},{18,2},{3,19},{19,3},{4,20},{20... | collective-permute-start | bytes 1544 | tf_op jit(solution)/shard_map/ppermute | solution.py:179
  3.7 0.7 add_convert_fusion
  4.4 0.2 collective-permute-start.4
  4.6 0.7 broadcast_xor_fusion
  5.2 0.1 collective-permute-done
  5.4 2.0 %collective-permute-start.1 = (s32[256]{0:T(256)S(1)}, s32[256]{0:T(256)S(1)}, u32[]{:S(2)}, u32[]{:S(2)}) collective-permute-start(s32[256]{0:T(256)S(1)} %pad_add_fusion.1), channel_id=1, source_target_pairs={{0,1},{1,0},{2,3},{3,2},{4,5},{5,4},{6,7},{7,6},{8,9},{9,8},{10,11... | collective-permute-start | bytes 3080 | tf_op jit(solution)/shard_map/ppermute | solution.py:179
  7.4 3.1 %shard_map.50 = (f32[8,256,512]{2,1,0:T(8,128)S(1)}, s32[512]{0:T(512)S(1)}) custom-call(f32[2048,512]{1,0:T(8,128)} %rows_ref.1, f32[8,256]{1,0:T(8,128)S(1)} %reshape.86.sign_ref), custom_call_target="tpu_custom_call" | custom-call | flops 1073741824 | bytes 8388608 | tf_op jit(solution)/shard_map/pallas_call | solution.py:72
  10.5 0.0 collective-permute-done.1
  10.5 1.6 %collective-permute-start.2 = (s32[512]{0:T(512)S(1)}, s32[512]{0:T(512)S(1)}, u32[]{:S(2)}, u32[]{:S(2)}) collective-permute-start(s32[512]{0:T(512)S(1)} %add_add_fusion.1), channel_id=1, source_target_pairs={{0,2},{2,0},{1,3},{3,1},{4,6},{6,4},{5,7},{7,5},{8,10},{10,8},{9,1... | collective-permute-start | bytes 6152 | tf_op jit(solution)/shard_map/ppermute | solution.py:179
  12.2 0.0 collective-permute-done.4.sign_ref
  12.2 0.0 collective-permute-done.3.rows_ref
  12.2 3.1 %shard_map.51 = (f32[8,256,512]{2,1,0:T(8,128)S(1)}, s32[1024]{0:T(1024)S(1)}) custom-call(f32[2048,512]{1,0:T(8,128)} %collective-permute-done.3.rows_ref, f32[8,256]{1,0:T(8,128)S(1)} %collective-permute-done.4.sign_ref), custom_call_target="tpu_custom_call" | custom-call | flops 1073741824 | bytes 8388608 | tf_op jit(solution)/shard_map/pallas_call | solution.py:72
  15.2 0.0 collective-permute-done.2
  15.3 2.7 %collective-permute-start.5 = (s32[1024]{0:T(1024)S(1)}, s32[1024]{0:T(1024)S(1)}, u32[]{:S(2)}, u32[]{:S(2)}) collective-permute-start(s32[1024]{0:T(1024)S(1)} %add_add_fusion), channel_id=1, source_target_pairs={{0,4},{4,0},{1,5},{5,1},{2,6},{6,2},{3,7},{7,3},{8,12},{12,8},{9,1... | collective-permute-start | bytes 12296 | tf_op jit(solution)/shard_map/ppermute | solution.py:179
  17.9 1.8 %shard_map.52.table_ref = f32[16384,128]{1,0:T(8,128)S(1)} custom-call(f32[8,256,512]{2,1,0:T(8,128)S(1)} %get-tuple-element.16.own_ref, f32[8,256,512]{2,1,0:T(8,128)S(1)} %get-tuple-element.17.oth_ref), custom_call_target="tpu_custom_call" | custom-call | flops 10485760 | bytes 16777216 | tf_op jit(solution)/shard_map/pallas_call | solution.py:107
  19.7 0.1 collective-permute-done.5
  19.9 2.1 %shard_map.54 = (f32[1408,128]{1,0:T(8,128)S(1)}, f32[1408,128]{1,0:T(8,128)S(1)}, f32[1280,128]{1,0:T(8,128)S(1)}) custom-call(s32[2048]{0:T(1024)S(1)} %get-tuple-element.41.at_ref, f32[2048]{0:T(1024)S(1)} %get-tuple-element.40.sign_ref, f32[16384,128]{1,0:T(8,128)S(1)} %shard_map.52.table_ref), custom_call_target="tpu_custom_call" | custom-call | bytes 4194304 | tf_op jit(solution)/shard_map/pallas_call | solution.py:139
  22.0 0.5 collective-permute-start.13
  22.5 1.5 %collective-permute-start.6 = (f32[1408,128]{1,0:T(8,128)S(1)}, f32[1408,128]{1,0:T(8,128)S(1)}, u32[]{:S(2)}, u32[]{:S(2)}) collective-permute-start(f32[1408,128]{1,0:T(8,128)S(1)} %get-tuple-element.19), channel_id=1, source_target_pairs={{0,16},{16,0},{1,17},{17,1},{2,18},{18,2},{3,19},{19,3},{4,20},{20... | collective-permute-start | bytes 2162696 | tf_op jit(solution)/shard_map/ppermute | solution.py:179
  24.0 0.5 collective-permute-start.9
  24.5 2.1 %shard_map.53 = (f32[1408,128]{1,0:T(8,128)S(1)}, f32[1408,128]{1,0:T(8,128)S(1)}, f32[1280,128]{1,0:T(8,128)S(1)}) custom-call(s32[2048]{0:T(1024)S(1)} %get-tuple-element.41.at_ref, f32[2048]{0:T(1024)S(1)} %get-tuple-element.40.sign_ref, f32[16384,128]{1,0:T(8,128)S(1)} %shard_map.52.table_ref), custom_call_target="tpu_custom_call" | custom-call | bytes 4194304 | tf_op jit(solution)/shard_map/pallas_call | solution.py:139
  26.6 10.9 %collective-permute-done.13 = f32[1280,128]{1,0:T(8,128)S(1)} collective-permute-done((f32[1280,128]{1,0:T(8,128)S(1)}, f32[1280,128]{1,0:T(8,128)S(1)}, u32[]{:S(2)}, u32[]{:S(2)}) %collective-permute-start.13) | collective-permute-done | bytes 655392 | tf_op jit(solution)/shard_map/ppermute | solution.py:179
  37.5 0.1 slice_add_fusion.5
  37.6 1.1 %collective-permute-start.14 = (f32[640,128]{1,0:T(8,128)S(1)}, f32[640,128]{1,0:T(8,128)S(1)}, u32[]{:S(2)}, u32[]{:S(2)}) collective-permute-start(f32[640,128]{1,0:T(8,128)S(1)} %get-tuple-element.31), channel_id=1, source_target_pairs={{0,16},{16,0},{1,17},{17,1},{2,18},{18,2},{3,19},{19,3},{4,20},{20... | collective-permute-start | bytes 983048 | tf_op jit(solution)/shard_map/ppermute | solution.py:179
  38.6 1.3 %collective-permute-done.6 = f32[1408,128]{1,0:T(8,128)S(1)} collective-permute-done((f32[1408,128]{1,0:T(8,128)S(1)}, f32[1408,128]{1,0:T(8,128)S(1)}, u32[]{:S(2)}, u32[]{:S(2)}) %collective-permute-start.6) | collective-permute-done | bytes 720928 | tf_op jit(solution)/shard_map/ppermute | solution.py:179
  39.9 0.1 slice_add_fusion.3
  40.0 1.7 %collective-permute-start.7 = (f32[704,128]{1,0:T(8,128)S(1)}, f32[704,128]{1,0:T(8,128)S(1)}, u32[]{:S(2)}, u32[]{:S(2)}) collective-permute-start(f32[704,128]{1,0:T(8,128)S(1)} %get-tuple-element.27), channel_id=1, source_target_pairs={{0,1},{1,0},{2,3},{3,2},{4,5},{5,4},{6,7},{7,6},{8,9},{9,8},{10,11... | collective-permute-start | bytes 1081352 | tf_op jit(solution)/shard_map/ppermute | solution.py:179
  41.7 0.0 collective-permute-done.9
  41.7 0.1 slice_add_fusion.1
  41.8 1.2 %collective-permute-start.10 = (f32[704,128]{1,0:T(8,128)S(1)}, f32[704,128]{1,0:T(8,128)S(1)}, u32[]{:S(2)}, u32[]{:S(2)}) collective-permute-start(f32[704,128]{1,0:T(8,128)S(1)} %get-tuple-element.29), channel_id=1, source_target_pairs={{0,2},{2,0},{1,3},{3,1},{4,6},{6,4},{5,7},{7,5},{8,10},{10,8},{9,1... | collective-permute-start | bytes 1081352 | tf_op jit(solution)/shard_map/ppermute | solution.py:179
  43.0 3.1 %collective-permute-done.14 = f32[640,128]{1,0:T(8,128)S(1)} collective-permute-done((f32[640,128]{1,0:T(8,128)S(1)}, f32[640,128]{1,0:T(8,128)S(1)}, u32[]{:S(2)}, u32[]{:S(2)}) %collective-permute-start.14) | collective-permute-done | bytes 327712 | tf_op jit(solution)/shard_map/ppermute | solution.py:179
  46.1 1.1 %collective-permute-start.15 = (f32[320,128]{1,0:T(8,128)S(1)}, f32[320,128]{1,0:T(8,128)S(1)}, u32[]{:S(2)}, u32[]{:S(2)}) collective-permute-start(f32[320,128]{1,0:T(8,128)S(1)} %slice_add_fusion.10), channel_id=1, source_target_pairs={{0,1},{1,0},{2,3},{3,2},{4,5},{5,4},{6,7},{7,6},{8,9},{9,8},{10,11... | collective-permute-start | bytes 491528 | tf_op jit(solution)/shard_map/ppermute | solution.py:179
  47.2 1.1 %collective-permute-done.7 = f32[704,128]{1,0:T(8,128)S(1)} collective-permute-done((f32[704,128]{1,0:T(8,128)S(1)}, f32[704,128]{1,0:T(8,128)S(1)}, u32[]{:S(2)}, u32[]{:S(2)}) %collective-permute-start.7) | collective-permute-done | bytes 360480 | tf_op jit(solution)/shard_map/ppermute | solution.py:179
  48.3 3.8 %collective-permute-start.8 = (f32[352,128]{1,0:T(8,128)S(1)}, f32[352,128]{1,0:T(8,128)S(1)}, u32[]{:S(2)}, u32[]{:S(2)}) collective-permute-start(f32[352,128]{1,0:T(8,128)S(1)} %slice_add_fusion.8), channel_id=1, source_target_pairs={{0,2},{2,0},{1,3},{3,1},{4,6},{6,4},{5,7},{7,5},{8,10},{10,8},{9,1... | collective-permute-start | bytes 540680 | tf_op jit(solution)/shard_map/ppermute | solution.py:179
  52.1 0.0 collective-permute-done.10
  52.1 1.5 %collective-permute-start.11 = (f32[352,128]{1,0:T(8,128)S(1)}, f32[352,128]{1,0:T(8,128)S(1)}, u32[]{:S(2)}, u32[]{:S(2)}) collective-permute-start(f32[352,128]{1,0:T(8,128)S(1)} %slice_add_fusion.6), channel_id=1, source_target_pairs={{0,16},{16,0},{1,17},{17,1},{2,18},{18,2},{3,19},{19,3},{4,20},{20... | collective-permute-start | bytes 540680 | tf_op jit(solution)/shard_map/ppermute | solution.py:179
  53.7 0.0 collective-permute-done.15
  53.7 2.3 %collective-permute-start.16 = (f32[1,160,128]{2,1,0:T(8,128)S(1)}, f32[1,160,128]{2,1,0:T(8,128)S(1)}, u32[]{:S(2)}, u32[]{:S(2)}) collective-permute-start(f32[1,160,128]{2,1,0:T(8,128)S(1)} %slice_bitcast_fusion), channel_id=1, source_target_pairs={{0,4},{4,0},{1,5},{5,1},{2,6},{6,2},{3,7},{7,3},{8,12},{12,8},{9,1... | collective-permute-start | bytes 245768 | tf_op jit(solution)/shard_map/ppermute | solution.py:179
  56.0 0.8 collective-permute-done.8
  56.9 0.8 collective-permute-done.11
  57.7 2.7 %collective-permute-start.12 = (f32[1,352,128]{2,1,0:T(8,128)S(1)}, f32[1,352,128]{2,1,0:T(8,128)S(1)}, u32[]{:S(2)}, u32[]{:S(2)}) collective-permute-start(f32[1,352,128]{2,1,0:T(8,128)S(1)} %pad_maximum_fusion.1), channel_id=1, source_target_pairs={{0,4},{4,0},{1,5},{5,1},{2,6},{6,2},{3,7},{7,3},{8,12},{12,8},{9,1... | collective-permute-start | bytes 540680 | tf_op jit(solution)/shard_map/ppermute | solution.py:179
  60.4 1.2 %collective-permute-done.16 = f32[1,160,128]{2,1,0:T(8,128)S(1)} collective-permute-done((f32[1,160,128]{2,1,0:T(8,128)S(1)}, f32[1,160,128]{2,1,0:T(8,128)S(1)}, u32[]{:S(2)}, u32[]{:S(2)}) %collective-permute-start.16) | collective-permute-done | bytes 81952 | tf_op jit(solution)/shard_map/ppermute | solution.py:179
  61.6 4.5 %collective-permute-done.12 = f32[1,352,128]{2,1,0:T(8,128)S(1)} collective-permute-done((f32[1,352,128]{2,1,0:T(8,128)S(1)}, f32[1,352,128]{2,1,0:T(8,128)S(1)}, u32[]{:S(2)}, u32[]{:S(2)}) %collective-permute-start.12) | collective-permute-done | bytes 180256 | tf_op jit(solution)/shard_map/ppermute | solution.py:179
  66.2 0.1 collective-permute-start.17
  66.3 1.5 %collective-permute-done.17.oth_ref = f32[512,128]{1,0:T(8,128)S(1)} collective-permute-done((f32[512,128]{1,0:T(8,128)S(1)}, f32[512,128]{1,0:T(8,128)S(1)}, u32[]{:S(2)}, u32[]{:S(2)}) %collective-permute-start.17) | collective-permute-done | bytes 262176 | tf_op jit(solution)/shard_map/ppermute | solution.py:179
  67.8 1.0 %shard_map.55 = (f32[128,512]{1,0:T(8,128)}, f32[256,512]{1,0:T(8,128)S(1)}) custom-call(s32[1]{0:T(128)} %bitcast.core_ref, f32[512,128]{1,0:T(8,128)S(1)} %pad_maximum_fusion.own_ref, f32[512,128]{1,0:T(8,128)S(1)} %collective-permute-done.17.oth_ref), custom_call_target="tpu_custom_call" | custom-call | flops 201326592 | bytes 1048576 | tf_op jit(solution)/shard_map/pallas_call | solution.py:287
  68.8 0.1 slice_select_fusion.3
  68.9 1.9 %collective-permute-start.18 = (f32[4,16,512]{2,1,0:T(8,128)S(1)}, f32[4,16,512]{2,1,0:T(8,128)S(1)}, u32[]{:S(2)}, u32[]{:S(2)}) collective-permute-start(f32[4,16,512]{2,1,0:T(8,128)S(1)} %fusion.8), channel_id=1, source_target_pairs={{0,17},{1,16},{16,1},{17,0},{2,19},{3,18},{18,3},{19,2},{4,21},{5,... | collective-permute-start | bytes 393224 | tf_op jit(solution)/shard_map/ppermute | solution.py:196
  70.8 0.1 collective-permute-start.19
  71.0 1.7 %collective-permute-start.20 = (f32[4,16,512]{2,1,0:T(8,128)S(1)}, f32[4,16,512]{2,1,0:T(8,128)S(1)}, u32[]{:S(2)}, u32[]{:S(2)}) collective-permute-start(f32[4,16,512]{2,1,0:T(8,128)S(1)} %fusion.6), channel_id=1, source_target_pairs={{0,1},{1,0},{16,17},{17,16},{2,3},{3,2},{18,19},{19,18},{4,5},{5,4... | collective-permute-start | bytes 393224 | tf_op jit(solution)/shard_map/ppermute | solution.py:196
  72.7 3.6 %collective-permute-done.18 = f32[4,16,512]{2,1,0:T(8,128)S(1)} collective-permute-done((f32[4,16,512]{2,1,0:T(8,128)S(1)}, f32[4,16,512]{2,1,0:T(8,128)S(1)}, u32[]{:S(2)}, u32[]{:S(2)}) %collective-permute-start.18) | collective-permute-done | bytes 131104 | tf_op jit(solution)/shard_map/ppermute | solution.py:196
  76.3 0.8 collective-permute-done.19
  77.1 1.2 %collective-permute-done.20 = f32[4,16,512]{2,1,0:T(8,128)S(1)} collective-permute-done((f32[4,16,512]{2,1,0:T(8,128)S(1)}, f32[4,16,512]{2,1,0:T(8,128)S(1)}, u32[]{:S(2)}, u32[]{:S(2)}) %collective-permute-start.20) | collective-permute-done | bytes 131104 | tf_op jit(solution)/shard_map/ppermute | solution.py:196
  78.4 3.6 %collective-permute-start.21 = (f32[1,16,512]{2,1,0:T(8,128)S(1)}, f32[1,16,512]{2,1,0:T(8,128)S(1)}, u32[]{:S(2)}, u32[]{:S(2)}) collective-permute-start(f32[1,16,512]{2,1,0:T(8,128)S(1)} %slice_select_fusion.14), channel_id=1, source_target_pairs={{0,6},{2,4},{4,2},{6,0},{1,7},{3,5},{5,3},{7,1},{8,14},{10,12},{12... | collective-permute-start | bytes 98312 | tf_op jit(solution)/shard_map/ppermute | solution.py:196
  81.9 0.0 collective-permute-start.22
  81.9 0.9 %collective-permute-start.23 = (f32[1,16,512]{2,1,0:T(8,128)S(1)}, f32[1,16,512]{2,1,0:T(8,128)S(1)}, u32[]{:S(2)}, u32[]{:S(2)}) collective-permute-start(f32[1,16,512]{2,1,0:T(8,128)S(1)} %slice_select_fusion.12), channel_id=1, source_target_pairs={{0,2},{2,0},{4,6},{6,4},{1,3},{3,1},{5,7},{7,5},{8,10},{10,8},{12,... | collective-permute-start | bytes 98312 | tf_op jit(solution)/shard_map/ppermute | solution.py:196
  82.8 1.3 %collective-permute-done.21 = f32[1,16,512]{2,1,0:T(8,128)S(1)} collective-permute-done((f32[1,16,512]{2,1,0:T(8,128)S(1)}, f32[1,16,512]{2,1,0:T(8,128)S(1)}, u32[]{:S(2)}, u32[]{:S(2)}) %collective-permute-start.21) | collective-permute-done | bytes 32800 | tf_op jit(solution)/shard_map/ppermute | solution.py:196
  84.1 2.6 %collective-permute-done.22 = f32[1,16,512]{2,1,0:T(8,128)S(1)} collective-permute-done((f32[1,16,512]{2,1,0:T(8,128)S(1)}, f32[1,16,512]{2,1,0:T(8,128)S(1)}, u32[]{:S(2)}, u32[]{:S(2)}) %collective-permute-start.22) | collective-permute-done | bytes 32800 | tf_op jit(solution)/shard_map/ppermute | solution.py:196
  86.7 0.0 collective-permute-done.23
  86.7 0.6 fusion.18
  (25 shorter events, 0.5 us)
Async XLA Ops:
  0.6 11.5 %collective-permute-start.3 = (f32[2048,512]{1,0:T(8,128)}, f32[2048,512]{1,0:T(8,128)}, u32[]{:S(2)}, u32[]{:S(2)}) collective-permute-start(f32[2048,512]{1,0:T(8,128)} %rows_ref.1), channel_id=1, source_target_pairs={{0,8},{8,0},{1,9},{9,1},{2,10},{10,2},{3,11},{11,3},{4,12},{12,4},... | collective-permute-start | bytes 12582920 | tf_op jit(solution)/shard_map/ppermute | solution.py:179
  1.1 4.2 %collective-permute-start = (s32[128]{0:T(128)}, s32[128]{0:T(128)S(1)}, u32[]{:S(2)}, u32[]{:S(2)}) collective-permute-start(s32[128]{0:T(128)} %param.5), channel_id=1, source_target_pairs={{0,16},{16,0},{1,17},{17,1},{2,18},{18,2},{3,19},{19,3},{4,20},{20... | collective-permute-start | bytes 1544 | tf_op jit(solution)/shard_map/ppermute | solution.py:179
  4.4 7.7 %collective-permute-start.4 = (f32[8,256]{1,0:T(8,128)S(1)}, f32[8,256]{1,0:T(8,128)S(1)}, u32[]{:S(2)}, u32[]{:S(2)}) collective-permute-start(f32[8,256]{1,0:T(8,128)S(1)} %reshape.86.sign_ref), channel_id=1, source_target_pairs={{0,8},{8,0},{1,9},{9,1},{2,10},{10,2},{3,11},{11,3},{4,12},{12,4},... | collective-permute-start | bytes 24584 | tf_op jit(solution)/shard_map/ppermute | solution.py:179
  5.4 5.1 %collective-permute-start.1 = (s32[256]{0:T(256)S(1)}, s32[256]{0:T(256)S(1)}, u32[]{:S(2)}, u32[]{:S(2)}) collective-permute-start(s32[256]{0:T(256)S(1)} %pad_add_fusion.1), channel_id=1, source_target_pairs={{0,1},{1,0},{2,3},{3,2},{4,5},{5,4},{6,7},{7,6},{8,9},{9,8},{10,11... | collective-permute-start | bytes 3080 | tf_op jit(solution)/shard_map/ppermute | solution.py:179
  10.5 4.7 %collective-permute-start.2 = (s32[512]{0:T(512)S(1)}, s32[512]{0:T(512)S(1)}, u32[]{:S(2)}, u32[]{:S(2)}) collective-permute-start(s32[512]{0:T(512)S(1)} %add_add_fusion.1), channel_id=1, source_target_pairs={{0,2},{2,0},{1,3},{3,1},{4,6},{6,4},{5,7},{7,5},{8,10},{10,8},{9,1... | collective-permute-start | bytes 6152 | tf_op jit(solution)/shard_map/ppermute | solution.py:179
  15.3 4.6 %collective-permute-start.5 = (s32[1024]{0:T(1024)S(1)}, s32[1024]{0:T(1024)S(1)}, u32[]{:S(2)}, u32[]{:S(2)}) collective-permute-start(s32[1024]{0:T(1024)S(1)} %add_add_fusion), channel_id=1, source_target_pairs={{0,4},{4,0},{1,5},{5,1},{2,6},{6,2},{3,7},{7,3},{8,12},{12,8},{9,1... | collective-permute-start | bytes 12296 | tf_op jit(solution)/shard_map/ppermute | solution.py:179
  22.0 15.5 %collective-permute-start.13 = (f32[1280,128]{1,0:T(8,128)S(1)}, f32[1280,128]{1,0:T(8,128)S(1)}, u32[]{:S(2)}, u32[]{:S(2)}) collective-permute-start(f32[1280,128]{1,0:T(8,128)S(1)} %get-tuple-element.23), channel_id=1, source_target_pairs={{0,2},{2,0},{1,3},{3,1},{4,6},{6,4},{5,7},{7,5},{8,10},{10,8},{9,1... | collective-permute-start | bytes 1966088 | tf_op jit(solution)/shard_map/ppermute | solution.py:179
  22.5 17.4 %collective-permute-start.6 = (f32[1408,128]{1,0:T(8,128)S(1)}, f32[1408,128]{1,0:T(8,128)S(1)}, u32[]{:S(2)}, u32[]{:S(2)}) collective-permute-start(f32[1408,128]{1,0:T(8,128)S(1)} %get-tuple-element.19), channel_id=1, source_target_pairs={{0,16},{16,0},{1,17},{17,1},{2,18},{18,2},{3,19},{19,3},{4,20},{20... | collective-permute-start | bytes 2162696 | tf_op jit(solution)/shard_map/ppermute | solution.py:179
  24.0 17.7 %collective-permute-start.9 = (f32[1408,128]{1,0:T(8,128)S(1)}, f32[1408,128]{1,0:T(8,128)S(1)}, u32[]{:S(2)}, u32[]{:S(2)}) collective-permute-start(f32[1408,128]{1,0:T(8,128)S(1)} %get-tuple-element.21), channel_id=1, source_target_pairs={{0,1},{1,0},{2,3},{3,2},{4,5},{5,4},{6,7},{7,6},{8,9},{9,8},{10,11... | collective-permute-start | bytes 2162696 | tf_op jit(solution)/shard_map/ppermute | solution.py:179
  37.6 8.5 %collective-permute-start.14 = (f32[640,128]{1,0:T(8,128)S(1)}, f32[640,128]{1,0:T(8,128)S(1)}, u32[]{:S(2)}, u32[]{:S(2)}) collective-permute-start(f32[640,128]{1,0:T(8,128)S(1)} %get-tuple-element.31), channel_id=1, source_target_pairs={{0,16},{16,0},{1,17},{17,1},{2,18},{18,2},{3,19},{19,3},{4,20},{20... | collective-permute-start | bytes 983048 | tf_op jit(solution)/shard_map/ppermute | solution.py:179
  40.0 8.3 %collective-permute-start.7 = (f32[704,128]{1,0:T(8,128)S(1)}, f32[704,128]{1,0:T(8,128)S(1)}, u32[]{:S(2)}, u32[]{:S(2)}) collective-permute-start(f32[704,128]{1,0:T(8,128)S(1)} %get-tuple-element.27), channel_id=1, source_target_pairs={{0,1},{1,0},{2,3},{3,2},{4,5},{5,4},{6,7},{7,6},{8,9},{9,8},{10,11... | collective-permute-start | bytes 1081352 | tf_op jit(solution)/shard_map/ppermute | solution.py:179
  41.8 10.3 %collective-permute-start.10 = (f32[704,128]{1,0:T(8,128)S(1)}, f32[704,128]{1,0:T(8,128)S(1)}, u32[]{:S(2)}, u32[]{:S(2)}) collective-permute-start(f32[704,128]{1,0:T(8,128)S(1)} %get-tuple-element.29), channel_id=1, source_target_pairs={{0,2},{2,0},{1,3},{3,1},{4,6},{6,4},{5,7},{7,5},{8,10},{10,8},{9,1... | collective-permute-start | bytes 1081352 | tf_op jit(solution)/shard_map/ppermute | solution.py:179
  46.1 7.6 %collective-permute-start.15 = (f32[320,128]{1,0:T(8,128)S(1)}, f32[320,128]{1,0:T(8,128)S(1)}, u32[]{:S(2)}, u32[]{:S(2)}) collective-permute-start(f32[320,128]{1,0:T(8,128)S(1)} %slice_add_fusion.10), channel_id=1, source_target_pairs={{0,1},{1,0},{2,3},{3,2},{4,5},{5,4},{6,7},{7,6},{8,9},{9,8},{10,11... | collective-permute-start | bytes 491528 | tf_op jit(solution)/shard_map/ppermute | solution.py:179
  48.3 8.5 %collective-permute-start.8 = (f32[352,128]{1,0:T(8,128)S(1)}, f32[352,128]{1,0:T(8,128)S(1)}, u32[]{:S(2)}, u32[]{:S(2)}) collective-permute-start(f32[352,128]{1,0:T(8,128)S(1)} %slice_add_fusion.8), channel_id=1, source_target_pairs={{0,2},{2,0},{1,3},{3,1},{4,6},{6,4},{5,7},{7,5},{8,10},{10,8},{9,1... | collective-permute-start | bytes 540680 | tf_op jit(solution)/shard_map/ppermute | solution.py:179
  52.1 5.6 %collective-permute-start.11 = (f32[352,128]{1,0:T(8,128)S(1)}, f32[352,128]{1,0:T(8,128)S(1)}, u32[]{:S(2)}, u32[]{:S(2)}) collective-permute-start(f32[352,128]{1,0:T(8,128)S(1)} %slice_add_fusion.6), channel_id=1, source_target_pairs={{0,16},{16,0},{1,17},{17,1},{2,18},{18,2},{3,19},{19,3},{4,20},{20... | collective-permute-start | bytes 540680 | tf_op jit(solution)/shard_map/ppermute | solution.py:179
  53.7 7.9 %collective-permute-start.16 = (f32[1,160,128]{2,1,0:T(8,128)S(1)}, f32[1,160,128]{2,1,0:T(8,128)S(1)}, u32[]{:S(2)}, u32[]{:S(2)}) collective-permute-start(f32[1,160,128]{2,1,0:T(8,128)S(1)} %slice_bitcast_fusion), channel_id=1, source_target_pairs={{0,4},{4,0},{1,5},{5,1},{2,6},{6,2},{3,7},{7,3},{8,12},{12,8},{9,1... | collective-permute-start | bytes 245768 | tf_op jit(solution)/shard_map/ppermute | solution.py:179
  57.7 8.4 %collective-permute-start.12 = (f32[1,352,128]{2,1,0:T(8,128)S(1)}, f32[1,352,128]{2,1,0:T(8,128)S(1)}, u32[]{:S(2)}, u32[]{:S(2)}) collective-permute-start(f32[1,352,128]{2,1,0:T(8,128)S(1)} %pad_maximum_fusion.1), channel_id=1, source_target_pairs={{0,4},{4,0},{1,5},{5,1},{2,6},{6,2},{3,7},{7,3},{8,12},{12,8},{9,1... | collective-permute-start | bytes 540680 | tf_op jit(solution)/shard_map/ppermute | solution.py:179
  66.2 1.6 %collective-permute-start.17 = (f32[512,128]{1,0:T(8,128)S(1)}, f32[512,128]{1,0:T(8,128)S(1)}, u32[]{:S(2)}, u32[]{:S(2)}) collective-permute-start(f32[512,128]{1,0:T(8,128)S(1)} %pad_maximum_fusion.own_ref), channel_id=1, source_target_pairs={{0,8},{8,0},{1,9},{9,1},{2,10},{10,2},{3,11},{11,3},{4,12},{12,4},... | collective-permute-start | bytes 786440 | tf_op jit(solution)/shard_map/ppermute | solution.py:179
  68.9 7.3 %collective-permute-start.18 = (f32[4,16,512]{2,1,0:T(8,128)S(1)}, f32[4,16,512]{2,1,0:T(8,128)S(1)}, u32[]{:S(2)}, u32[]{:S(2)}) collective-permute-start(f32[4,16,512]{2,1,0:T(8,128)S(1)} %fusion.8), channel_id=1, source_target_pairs={{0,17},{1,16},{16,1},{17,0},{2,19},{3,18},{18,3},{19,2},{4,21},{5,... | collective-permute-start | bytes 393224 | tf_op jit(solution)/shard_map/ppermute | solution.py:196
  70.8 6.3 %collective-permute-start.19 = (f32[4,16,512]{2,1,0:T(8,128)S(1)}, f32[4,16,512]{2,1,0:T(8,128)S(1)}, u32[]{:S(2)}, u32[]{:S(2)}) collective-permute-start(f32[4,16,512]{2,1,0:T(8,128)S(1)} %fusion.7), channel_id=1, source_target_pairs={{0,16},{1,17},{16,0},{17,1},{2,18},{3,19},{18,2},{19,3},{4,20},{5,... | collective-permute-start | bytes 393224 | tf_op jit(solution)/shard_map/ppermute | solution.py:196
  71.0 7.3 %collective-permute-start.20 = (f32[4,16,512]{2,1,0:T(8,128)S(1)}, f32[4,16,512]{2,1,0:T(8,128)S(1)}, u32[]{:S(2)}, u32[]{:S(2)}) collective-permute-start(f32[4,16,512]{2,1,0:T(8,128)S(1)} %fusion.6), channel_id=1, source_target_pairs={{0,1},{1,0},{16,17},{17,16},{2,3},{3,2},{18,19},{19,18},{4,5},{5,4... | collective-permute-start | bytes 393224 | tf_op jit(solution)/shard_map/ppermute | solution.py:196
  78.4 5.8 %collective-permute-start.21 = (f32[1,16,512]{2,1,0:T(8,128)S(1)}, f32[1,16,512]{2,1,0:T(8,128)S(1)}, u32[]{:S(2)}, u32[]{:S(2)}) collective-permute-start(f32[1,16,512]{2,1,0:T(8,128)S(1)} %slice_select_fusion.14), channel_id=1, source_target_pairs={{0,6},{2,4},{4,2},{6,0},{1,7},{3,5},{5,3},{7,1},{8,14},{10,12},{12... | collective-permute-start | bytes 98312 | tf_op jit(solution)/shard_map/ppermute | solution.py:196
  81.9 4.8 %collective-permute-start.22 = (f32[1,16,512]{2,1,0:T(8,128)S(1)}, f32[1,16,512]{2,1,0:T(8,128)S(1)}, u32[]{:S(2)}, u32[]{:S(2)}) collective-permute-start(f32[1,16,512]{2,1,0:T(8,128)S(1)} %slice_select_fusion.13), channel_id=1, source_target_pairs={{0,4},{2,6},{4,0},{6,2},{1,5},{3,7},{5,1},{7,3},{8,12},{10,14},{12... | collective-permute-start | bytes 98312 | tf_op jit(solution)/shard_map/ppermute | solution.py:196
  81.9 4.8 %collective-permute-start.23 = (f32[1,16,512]{2,1,0:T(8,128)S(1)}, f32[1,16,512]{2,1,0:T(8,128)S(1)}, u32[]{:S(2)}, u32[]{:S(2)}) collective-permute-start(f32[1,16,512]{2,1,0:T(8,128)S(1)} %slice_select_fusion.12), channel_id=1, source_target_pairs={{0,2},{2,0},{4,6},{6,4},{1,3},{3,1},{5,7},{7,5},{8,10},{10,8},{12,... | collective-permute-start | bytes 98312 | tf_op jit(solution)/shard_map/ppermute | solution.py:196

commit v5 on v4

--- a/solution.py
+++ b/solution.py
@@ -250,8 +250,9 @@
     at = ((source >> core_bit & 1) * rows + listed % rows) * tiles
     sign = (1 - 2 * (parity & 1)).astype(jnp.float32)
 
-    third = (samp // 3 + 2) // 2 * 2
-    counts = [third, third, samp - 2 * third]
+    third = samp // 6 * 2
+    counts = [third + 0, third + 0]
+    counts.append(samp - sum(counts))
     orders = []
     for part in range(3):
         order = [(part + i) % 3 for i in range(3)]
@@ -272,7 +273,7 @@
             held[part] = held[part][:half] + arrived[part][:half]
             arrived[part] = swap(send, steps[orders[part][level]])
     done = []
-    for members in ((2,), (0, 1)):
+    for members in ((2,), (0,), (1,)):
         whole = jnp.concatenate(
             [(held[part] + arrived[part]).reshape(-1, counts[part] * tiles, LANES) for part in members], axis=1
         )
@@ -280,7 +281,7 @@
             half = whole.shape[0] // 2
             whole = whole[:half] + swap(whole[half:], steps[level])
         done.append(whole[0])
-    own_sum = jnp.concatenate([done[1], done[0]])
+    own_sum = jnp.concatenate([done[1], done[2], done[0]])
     oth_sum = swap(own_sum, core)
 
     half_rows = cols // 2

time: 87.6 us -> 84.4 us (0.963)
  starting transfers between devices: 35.7 us -> 32.8 us
    ppermute x18 -> x19, starting transfers between devices: 27.6 us -> 24.7 us  [swap(): return lax.ppermute(block, bit, [(0, 1), (1, 0)])]
    ppermute x6, waiting for transfers between devices: 9.5 us -> 8.46 us  [reduce_pairs(): total += lax.ppermute(exclusive(block, own ^ flip, 0), axes, route)]
    ppermute x18 -> x19, waiting for transfers between devices: 25.4 us -> 26.3 us  [swap(): return lax.ppermute(block, bit, [(0, 1), (1, 0)])]
  transfers between devices with their start and end apart: 24 -> 25, of which waited for: 16 -> 17; matrix products, arithmetic and copies ran while one was open for 2% -> 2% of each run, Pallas kernels for 11% -> 12%
where the time goes in v5:
time: 84.4 us; the launch traced here: 84.2 us
  waiting for transfers between devices  34.7 us (41%)
  starting transfers between devices  32.8 us (39%)
  Pallas kernels  13 us (15%)
  other arithmetic  2.73 us (3%)
  between operations  0.88 us (1%)
    ppermute x19, waiting for transfers between devices, swap(): return lax.ppermute(block, bit, [(0, 1), (1, 0)])  26.3 us
    ppermute x19, starting transfers between devices, swap(): return lax.ppermute(block, bit, [(0, 1), (1, 0)])  24.7 us
    ppermute x6, waiting for transfers between devices, reduce_pairs(): total += lax.ppermute(exclusive(block, own ^ flip, 0), axes, route)  8.46 us
    ppermute x6, starting transfers between devices, reduce_pairs(): total += lax.ppermute(exclusive(block, own ^ flip, 0), axes, route)  8.12 us
    pallas_call x2, Pallas kernels, transform_blocks(): pl.pallas_call(blocks_kernel, out_shape=[jax.ShapeDtypeStruct((blocks, BL...  6.12 us
    pallas_call x2, Pallas kernels, gather(): pl.pallas_call(functools.partial(gather_kernel, plans, tiles), out_shape=...  4.17 us
    pallas_call x1, Pallas kernels, merge(): pl.pallas_call(merge_kernel, out_shape=jax.ShapeDtypeStruct((2 * blocks *...  1.78 us
  transfers between devices with their start and end apart: 25, of which 17 were waited for; matrix products, arithmetic and copies ran while one was open for 2% of the time, Pallas kernels for 12%

profile of v5, /device:TPU:0, one launch (start us, length us, event | category | flops | bytes accessed | tf_op | source)
XLA Modules:
  0.0 84.2 jit_solution(4585340686584670258)
XLA Ops:
  0.6 0.5 collective-permute-start.3
  1.1 2.6 %collective-permute-start = (s32[128]{0:T(128)}, s32[128]{0:T(128)S(1)}, u32[]{:S(2)}, u32[]{:S(2)}) collective-permute-start(s32[128]{0:T(128)} %param.5), channel_id=1, source_target_pairs={{0,16},{16,0},{1,17},{17,1},{2,18},{18,2},{3,19},{19,3},{4,20},{20... | collective-permute-start | bytes 1544 | tf_op jit(solution)/shard_map/ppermute | solution.py:179
  3.7 0.7 add_convert_fusion
  4.4 0.2 collective-permute-start.4
  4.6 0.7 broadcast_xor_fusion
  5.2 0.1 collective-permute-done
  5.4 2.0 %collective-permute-start.1 = (s32[256]{0:T(256)S(1)}, s32[256]{0:T(256)S(1)}, u32[]{:S(2)}, u32[]{:S(2)}) collective-permute-start(s32[256]{0:T(256)S(1)} %pad_add_fusion.1), channel_id=1, source_target_pairs={{0,1},{1,0},{2,3},{3,2},{4,5},{5,4},{6,7},{7,6},{8,9},{9,8},{10,11... | collective-permute-start | bytes 3080 | tf_op jit(solution)/shard_map/ppermute | solution.py:179
  7.4 3.1 %shard_map.50 = (f32[8,256,512]{2,1,0:T(8,128)S(1)}, s32[512]{0:T(512)S(1)}) custom-call(f32[2048,512]{1,0:T(8,128)} %rows_ref.1, f32[8,256]{1,0:T(8,128)S(1)} %reshape.86.sign_ref), custom_call_target="tpu_custom_call" | custom-call | flops 1073741824 | bytes 8388608 | tf_op jit(solution)/shard_map/pallas_call | solution.py:72
  10.5 0.0 collective-permute-done.1
  10.5 1.6 %collective-permute-start.2 = (s32[512]{0:T(512)S(1)}, s32[512]{0:T(512)S(1)}, u32[]{:S(2)}, u32[]{:S(2)}) collective-permute-start(s32[512]{0:T(512)S(1)} %add_add_fusion.1), channel_id=1, source_target_pairs={{0,2},{2,0},{1,3},{3,1},{4,6},{6,4},{5,7},{7,5},{8,10},{10,8},{9,1... | collective-permute-start | bytes 6152 | tf_op jit(solution)/shard_map/ppermute | solution.py:179
  12.2 0.0 collective-permute-done.4.sign_ref
  12.2 0.0 collective-permute-done.3.rows_ref
  12.2 3.1 %shard_map.51 = (f32[8,256,512]{2,1,0:T(8,128)S(1)}, s32[1024]{0:T(1024)S(1)}) custom-call(f32[2048,512]{1,0:T(8,128)} %collective-permute-done.3.rows_ref, f32[8,256]{1,0:T(8,128)S(1)} %collective-permute-done.4.sign_ref), custom_call_target="tpu_custom_call" | custom-call | flops 1073741824 | bytes 8388608 | tf_op jit(solution)/shard_map/pallas_call | solution.py:72
  15.2 0.0 collective-permute-done.2
  15.3 2.7 %collective-permute-start.5 = (s32[1024]{0:T(1024)S(1)}, s32[1024]{0:T(1024)S(1)}, u32[]{:S(2)}, u32[]{:S(2)}) collective-permute-start(s32[1024]{0:T(1024)S(1)} %add_add_fusion), channel_id=1, source_target_pairs={{0,4},{4,0},{1,5},{5,1},{2,6},{6,2},{3,7},{7,3},{8,12},{12,8},{9,1... | collective-permute-start | bytes 12296 | tf_op jit(solution)/shard_map/ppermute | solution.py:179
  17.9 1.8 %shard_map.52.table_ref = f32[16384,128]{1,0:T(8,128)S(1)} custom-call(f32[8,256,512]{2,1,0:T(8,128)S(1)} %get-tuple-element.16.own_ref, f32[8,256,512]{2,1,0:T(8,128)S(1)} %get-tuple-element.17.oth_ref), custom_call_target="tpu_custom_call" | custom-call | flops 10485760 | bytes 16777216 | tf_op jit(solution)/shard_map/pallas_call | solution.py:107
  19.7 0.1 collective-permute-done.5
  19.9 2.1 %shard_map.54 = (f32[1344,128]{1,0:T(8,128)S(1)}, f32[1344,128]{1,0:T(8,128)S(1)}, f32[1408,128]{1,0:T(8,128)S(1)}) custom-call(s32[2048]{0:T(1024)S(1)} %get-tuple-element.41.at_ref, f32[2048]{0:T(1024)S(1)} %get-tuple-element.40.sign_ref, f32[16384,128]{1,0:T(8,128)S(1)} %shard_map.52.table_ref), custom_call_target="tpu_custom_call" | custom-call | bytes 4194304 | tf_op jit(solution)/shard_map/pallas_call | solution.py:139
  22.0 1.6 %collective-permute-start.6 = (f32[1344,128]{1,0:T(8,128)S(1)}, f32[1344,128]{1,0:T(8,128)S(1)}, u32[]{:S(2)}, u32[]{:S(2)}) collective-permute-start(f32[1344,128]{1,0:T(8,128)S(1)} %get-tuple-element.19), channel_id=1, source_target_pairs={{0,16},{16,0},{1,17},{17,1},{2,18},{18,2},{3,19},{19,3},{4,20},{20... | collective-permute-start | bytes 2064392 | tf_op jit(solution)/shard_map/ppermute | solution.py:179
  23.5 0.5 collective-permute-start.10
  24.0 0.5 collective-permute-start.14
  24.5 2.1 %shard_map.53 = (f32[1344,128]{1,0:T(8,128)S(1)}, f32[1344,128]{1,0:T(8,128)S(1)}, f32[1408,128]{1,0:T(8,128)S(1)}) custom-call(s32[2048]{0:T(1024)S(1)} %get-tuple-element.41.at_ref, f32[2048]{0:T(1024)S(1)} %get-tuple-element.40.sign_ref, f32[16384,128]{1,0:T(8,128)S(1)} %shard_map.52.table_ref), custom_call_target="tpu_custom_call" | custom-call | bytes 4194304 | tf_op jit(solution)/shard_map/pallas_call | solution.py:139
  26.6 11.6 %collective-permute-done.6 = f32[1344,128]{1,0:T(8,128)S(1)} collective-permute-done((f32[1344,128]{1,0:T(8,128)S(1)}, f32[1344,128]{1,0:T(8,128)S(1)}, u32[]{:S(2)}, u32[]{:S(2)}) %collective-permute-start.6) | collective-permute-done | bytes 688160 | tf_op jit(solution)/shard_map/ppermute | solution.py:179
  38.2 0.1 slice_add_fusion.5
  38.3 0.6 collective-permute-start.7
  38.8 0.1 collective-permute-done.10
  39.0 0.1 slice_add_fusion.3
  39.0 0.9 %collective-permute-start.11 = (f32[672,128]{1,0:T(8,128)S(1)}, f32[672,128]{1,0:T(8,128)S(1)}, u32[]{:S(2)}, u32[]{:S(2)}) collective-permute-start(f32[672,128]{1,0:T(8,128)S(1)} %get-tuple-element.31), channel_id=1, source_target_pairs={{0,2},{2,0},{1,3},{3,1},{4,6},{6,4},{5,7},{7,5},{8,10},{10,8},{9,1... | collective-permute-start | bytes 1032200 | tf_op jit(solution)/shard_map/ppermute | solution.py:179
  40.0 0.5 collective-permute-done.14
  40.5 0.1 slice_add_fusion.1
  40.6 1.0 %collective-permute-start.15 = (f32[704,128]{1,0:T(8,128)S(1)}, f32[704,128]{1,0:T(8,128)S(1)}, u32[]{:S(2)}, u32[]{:S(2)}) collective-permute-start(f32[704,128]{1,0:T(8,128)S(1)} %get-tuple-element.27), channel_id=1, source_target_pairs={{0,16},{16,0},{1,17},{17,1},{2,18},{18,2},{3,19},{19,3},{4,20},{20... | collective-permute-start | bytes 1081352 | tf_op jit(solution)/shard_map/ppermute | solution.py:179
  41.6 4.7 %collective-permute-done.7 = f32[672,128]{1,0:T(8,128)S(1)} collective-permute-done((f32[672,128]{1,0:T(8,128)S(1)}, f32[672,128]{1,0:T(8,128)S(1)}, u32[]{:S(2)}, u32[]{:S(2)}) %collective-permute-start.7) | collective-permute-done | bytes 344096 | tf_op jit(solution)/shard_map/ppermute | solution.py:179
  46.3 0.5 collective-permute-start.8
  46.8 1.5 %collective-permute-done.11 = f32[672,128]{1,0:T(8,128)S(1)} collective-permute-done((f32[672,128]{1,0:T(8,128)S(1)}, f32[672,128]{1,0:T(8,128)S(1)}, u32[]{:S(2)}, u32[]{:S(2)}) %collective-permute-start.11) | collective-permute-done | bytes 344096 | tf_op jit(solution)/shard_map/ppermute | solution.py:179
  48.4 1.0 %collective-permute-start.12 = (f32[336,128]{1,0:T(8,128)S(1)}, f32[336,128]{1,0:T(8,128)S(1)}, u32[]{:S(2)}, u32[]{:S(2)}) collective-permute-start(f32[336,128]{1,0:T(8,128)S(1)} %slice_add_fusion.8), channel_id=1, source_target_pairs={{0,16},{16,0},{1,17},{17,1},{2,18},{18,2},{3,19},{19,3},{4,20},{20... | collective-permute-start | bytes 516104 | tf_op jit(solution)/shard_map/ppermute | solution.py:179
  49.4 0.0 collective-permute-done.15
  49.4 2.1 %collective-permute-start.16 = (f32[352,128]{1,0:T(8,128)S(1)}, f32[352,128]{1,0:T(8,128)S(1)}, u32[]{:S(2)}, u32[]{:S(2)}) collective-permute-start(f32[352,128]{1,0:T(8,128)S(1)} %slice_add_fusion.6), channel_id=1, source_target_pairs={{0,1},{1,0},{2,3},{3,2},{4,5},{5,4},{6,7},{7,6},{8,9},{9,8},{10,11... | collective-permute-start | bytes 540680 | tf_op jit(solution)/shard_map/ppermute | solution.py:179
  51.5 0.3 collective-permute-done.8
  51.8 2.0 %collective-permute-start.9 = (f32[1,168,128]{2,1,0:T(8,128)S(1)}, f32[1,168,128]{2,1,0:T(8,128)S(1)}, u32[]{:S(2)}, u32[]{:S(2)}) collective-permute-start(f32[1,168,128]{2,1,0:T(8,128)S(1)} %slice_bitcast_fusion.4), channel_id=1, source_target_pairs={{0,4},{4,0},{1,5},{5,1},{2,6},{6,2},{3,7},{7,3},{8,12},{12,8},{9,1... | collective-permute-start | bytes 258056 | tf_op jit(solution)/shard_map/ppermute | solution.py:179
  53.8 0.0 collective-permute-done.12
  53.9 2.0 %collective-permute-start.13 = (f32[1,168,128]{2,1,0:T(8,128)S(1)}, f32[1,168,128]{2,1,0:T(8,128)S(1)}, u32[]{:S(2)}, u32[]{:S(2)}) collective-permute-start(f32[1,168,128]{2,1,0:T(8,128)S(1)} %slice_bitcast_fusion.2), channel_id=1, source_target_pairs={{0,4},{4,0},{1,5},{5,1},{2,6},{6,2},{3,7},{7,3},{8,12},{12,8},{9,1... | collective-permute-start | bytes 258056 | tf_op jit(solution)/shard_map/ppermute | solution.py:179
  55.8 0.0 collective-permute-done.16
  55.9 2.4 %collective-permute-start.17 = (f32[1,176,128]{2,1,0:T(8,128)S(1)}, f32[1,176,128]{2,1,0:T(8,128)S(1)}, u32[]{:S(2)}, u32[]{:S(2)}) collective-permute-start(f32[1,176,128]{2,1,0:T(8,128)S(1)} %slice_bitcast_fusion), channel_id=1, source_target_pairs={{0,4},{4,0},{1,5},{5,1},{2,6},{6,2},{3,7},{7,3},{8,12},{12,8},{9,1... | collective-permute-start | bytes 270344 | tf_op jit(solution)/shard_map/ppermute | solution.py:179
  58.3 2.8 %collective-permute-done.9 = f32[1,168,128]{2,1,0:T(8,128)S(1)} collective-permute-done((f32[1,168,128]{2,1,0:T(8,128)S(1)}, f32[1,168,128]{2,1,0:T(8,128)S(1)}, u32[]{:S(2)}, u32[]{:S(2)}) %collective-permute-start.9) | collective-permute-done | bytes 86048 | tf_op jit(solution)/shard_map/ppermute | solution.py:179
  61.1 1.0 %collective-permute-done.13 = f32[1,168,128]{2,1,0:T(8,128)S(1)} collective-permute-done((f32[1,168,128]{2,1,0:T(8,128)S(1)}, f32[1,168,128]{2,1,0:T(8,128)S(1)}, u32[]{:S(2)}, u32[]{:S(2)}) %collective-permute-start.13) | collective-permute-done | bytes 86048 | tf_op jit(solution)/shard_map/ppermute | solution.py:179
  62.1 1.9 %collective-permute-done.17 = f32[1,176,128]{2,1,0:T(8,128)S(1)} collective-permute-done((f32[1,176,128]{2,1,0:T(8,128)S(1)}, f32[1,176,128]{2,1,0:T(8,128)S(1)}, u32[]{:S(2)}, u32[]{:S(2)}) %collective-permute-start.17) | collective-permute-done | bytes 90144 | tf_op jit(solution)/shard_map/ppermute | solution.py:179
  64.1 0.1 collective-permute-start.18
  64.2 1.5 %collective-permute-done.18.oth_ref = f32[512,128]{1,0:T(8,128)S(1)} collective-permute-done((f32[512,128]{1,0:T(8,128)S(1)}, f32[512,128]{1,0:T(8,128)S(1)}, u32[]{:S(2)}, u32[]{:S(2)}) %collective-permute-start.18) | collective-permute-done | bytes 262176 | tf_op jit(solution)/shard_map/ppermute | solution.py:179
  65.7 1.0 %shard_map.55 = (f32[128,512]{1,0:T(8,128)}, f32[256,512]{1,0:T(8,128)S(1)}) custom-call(s32[1]{0:T(128)} %bitcast.core_ref, f32[512,128]{1,0:T(8,128)S(1)} %pad_maximum_fusion.own_ref, f32[512,128]{1,0:T(8,128)S(1)} %collective-permute-done.18.oth_ref), custom_call_target="tpu_custom_call" | custom-call | flops 201326592 | bytes 1048576 | tf_op jit(solution)/shard_map/pallas_call | solution.py:288
  66.7 0.1 slice_select_fusion.3
  66.8 1.8 %collective-permute-start.19 = (f32[4,16,512]{2,1,0:T(8,128)S(1)}, f32[4,16,512]{2,1,0:T(8,128)S(1)}, u32[]{:S(2)}, u32[]{:S(2)}) collective-permute-start(f32[4,16,512]{2,1,0:T(8,128)S(1)} %fusion.5), channel_id=1, source_target_pairs={{0,17},{1,16},{16,1},{17,0},{2,19},{3,18},{18,3},{19,2},{4,21},{5,... | collective-permute-start | bytes 393224 | tf_op jit(solution)/shard_map/ppermute | solution.py:196
  68.7 1.2 %collective-permute-start.20 = (f32[4,16,512]{2,1,0:T(8,128)S(1)}, f32[4,16,512]{2,1,0:T(8,128)S(1)}, u32[]{:S(2)}, u32[]{:S(2)}) collective-permute-start(f32[4,16,512]{2,1,0:T(8,128)S(1)} %fusion.4), channel_id=1, source_target_pairs={{0,16},{1,17},{16,0},{17,1},{2,18},{3,19},{18,2},{19,3},{4,20},{5,... | collective-permute-start | bytes 393224 | tf_op jit(solution)/shard_map/ppermute | solution.py:196
  69.9 0.7 collective-permute-start.21
  70.6 3.6 %collective-permute-done.19 = f32[4,16,512]{2,1,0:T(8,128)S(1)} collective-permute-done((f32[4,16,512]{2,1,0:T(8,128)S(1)}, f32[4,16,512]{2,1,0:T(8,128)S(1)}, u32[]{:S(2)}, u32[]{:S(2)}) %collective-permute-start.19) | collective-permute-done | bytes 131104 | tf_op jit(solution)/shard_map/ppermute | solution.py:196
  74.1 1.9 %collective-permute-done.20 = f32[4,16,512]{2,1,0:T(8,128)S(1)} collective-permute-done((f32[4,16,512]{2,1,0:T(8,128)S(1)}, f32[4,16,512]{2,1,0:T(8,128)S(1)}, u32[]{:S(2)}, u32[]{:S(2)}) %collective-permute-start.20) | collective-permute-done | bytes 131104 | tf_op jit(solution)/shard_map/ppermute | solution.py:196
  76.1 0.1 collective-permute-done.21
  76.2 2.5 %collective-permute-start.22 = (f32[1,16,512]{2,1,0:T(8,128)S(1)}, f32[1,16,512]{2,1,0:T(8,128)S(1)}, u32[]{:S(2)}, u32[]{:S(2)}) collective-permute-start(f32[1,16,512]{2,1,0:T(8,128)S(1)} %slice_select_fusion.14), channel_id=1, source_target_pairs={{0,6},{2,4},{4,2},{6,0},{1,7},{3,5},{5,3},{7,1},{8,14},{10,12},{12... | collective-permute-start | bytes 98312 | tf_op jit(solution)/shard_map/ppermute | solution.py:196
  78.8 0.0 collective-permute-start.23
  78.8 1.9 %collective-permute-start.24 = (f32[1,16,512]{2,1,0:T(8,128)S(1)}, f32[1,16,512]{2,1,0:T(8,128)S(1)}, u32[]{:S(2)}, u32[]{:S(2)}) collective-permute-start(f32[1,16,512]{2,1,0:T(8,128)S(1)} %slice_select_fusion.12), channel_id=1, source_target_pairs={{0,2},{2,0},{4,6},{6,4},{1,3},{3,1},{5,7},{7,5},{8,10},{10,8},{12,... | collective-permute-start | bytes 98312 | tf_op jit(solution)/shard_map/ppermute | solution.py:196
  80.7 1.3 %collective-permute-done.22 = f32[1,16,512]{2,1,0:T(8,128)S(1)} collective-permute-done((f32[1,16,512]{2,1,0:T(8,128)S(1)}, f32[1,16,512]{2,1,0:T(8,128)S(1)}, u32[]{:S(2)}, u32[]{:S(2)}) %collective-permute-start.22) | collective-permute-done | bytes 32800 | tf_op jit(solution)/shard_map/ppermute | solution.py:196
  82.0 1.6 %collective-permute-done.23 = f32[1,16,512]{2,1,0:T(8,128)S(1)} collective-permute-done((f32[1,16,512]{2,1,0:T(8,128)S(1)}, f32[1,16,512]{2,1,0:T(8,128)S(1)}, u32[]{:S(2)}, u32[]{:S(2)}) %collective-permute-start.23) | collective-permute-done | bytes 32800 | tf_op jit(solution)/shard_map/ppermute | solution.py:196
  83.6 0.0 collective-permute-done.24
  83.6 0.6 fusion.19
  (27 shorter events, 0.5 us)
Async XLA Ops:
  0.6 11.5 %collective-permute-start.3 = (f32[2048,512]{1,0:T(8,128)}, f32[2048,512]{1,0:T(8,128)}, u32[]{:S(2)}, u32[]{:S(2)}) collective-permute-start(f32[2048,512]{1,0:T(8,128)} %rows_ref.1), channel_id=1, source_target_pairs={{0,8},{8,0},{1,9},{9,1},{2,10},{10,2},{3,11},{11,3},{4,12},{12,4},... | collective-permute-start | bytes 12582920 | tf_op jit(solution)/shard_map/ppermute | solution.py:179
  1.1 4.2 %collective-permute-start = (s32[128]{0:T(128)}, s32[128]{0:T(128)S(1)}, u32[]{:S(2)}, u32[]{:S(2)}) collective-permute-start(s32[128]{0:T(128)} %param.5), channel_id=1, source_target_pairs={{0,16},{16,0},{1,17},{17,1},{2,18},{18,2},{3,19},{19,3},{4,20},{20... | collective-permute-start | bytes 1544 | tf_op jit(solution)/shard_map/ppermute | solution.py:179
  4.4 7.7 %collective-permute-start.4 = (f32[8,256]{1,0:T(8,128)S(1)}, f32[8,256]{1,0:T(8,128)S(1)}, u32[]{:S(2)}, u32[]{:S(2)}) collective-permute-start(f32[8,256]{1,0:T(8,128)S(1)} %reshape.86.sign_ref), channel_id=1, source_target_pairs={{0,8},{8,0},{1,9},{9,1},{2,10},{10,2},{3,11},{11,3},{4,12},{12,4},... | collective-permute-start | bytes 24584 | tf_op jit(solution)/shard_map/ppermute | solution.py:179
  5.4 5.1 %collective-permute-start.1 = (s32[256]{0:T(256)S(1)}, s32[256]{0:T(256)S(1)}, u32[]{:S(2)}, u32[]{:S(2)}) collective-permute-start(s32[256]{0:T(256)S(1)} %pad_add_fusion.1), channel_id=1, source_target_pairs={{0,1},{1,0},{2,3},{3,2},{4,5},{5,4},{6,7},{7,6},{8,9},{9,8},{10,11... | collective-permute-start | bytes 3080 | tf_op jit(solution)/shard_map/ppermute | solution.py:179
  10.5 4.7 %collective-permute-start.2 = (s32[512]{0:T(512)S(1)}, s32[512]{0:T(512)S(1)}, u32[]{:S(2)}, u32[]{:S(2)}) collective-permute-start(s32[512]{0:T(512)S(1)} %add_add_fusion.1), channel_id=1, source_target_pairs={{0,2},{2,0},{1,3},{3,1},{4,6},{6,4},{5,7},{7,5},{8,10},{10,8},{9,1... | collective-permute-start | bytes 6152 | tf_op jit(solution)/shard_map/ppermute | solution.py:179
  15.3 4.6 %collective-permute-start.5 = (s32[1024]{0:T(1024)S(1)}, s32[1024]{0:T(1024)S(1)}, u32[]{:S(2)}, u32[]{:S(2)}) collective-permute-start(s32[1024]{0:T(1024)S(1)} %add_add_fusion), channel_id=1, source_target_pairs={{0,4},{4,0},{1,5},{5,1},{2,6},{6,2},{3,7},{7,3},{8,12},{12,8},{9,1... | collective-permute-start | bytes 12296 | tf_op jit(solution)/shard_map/ppermute | solution.py:179
  22.0 16.2 %collective-permute-start.6 = (f32[1344,128]{1,0:T(8,128)S(1)}, f32[1344,128]{1,0:T(8,128)S(1)}, u32[]{:S(2)}, u32[]{:S(2)}) collective-permute-start(f32[1344,128]{1,0:T(8,128)S(1)} %get-tuple-element.19), channel_id=1, source_target_pairs={{0,16},{16,0},{1,17},{17,1},{2,18},{18,2},{3,19},{19,3},{4,20},{20... | collective-permute-start | bytes 2064392 | tf_op jit(solution)/shard_map/ppermute | solution.py:179
  23.5 15.4 %collective-permute-start.10 = (f32[1344,128]{1,0:T(8,128)S(1)}, f32[1344,128]{1,0:T(8,128)S(1)}, u32[]{:S(2)}, u32[]{:S(2)}) collective-permute-start(f32[1344,128]{1,0:T(8,128)S(1)} %get-tuple-element.21), channel_id=1, source_target_pairs={{0,1},{1,0},{2,3},{3,2},{4,5},{5,4},{6,7},{7,6},{8,9},{9,8},{10,11... | collective-permute-start | bytes 2064392 | tf_op jit(solution)/shard_map/ppermute | solution.py:179
  24.0 16.5 %collective-permute-start.14 = (f32[1408,128]{1,0:T(8,128)S(1)}, f32[1408,128]{1,0:T(8,128)S(1)}, u32[]{:S(2)}, u32[]{:S(2)}) collective-permute-start(f32[1408,128]{1,0:T(8,128)S(1)} %get-tuple-element.23), channel_id=1, source_target_pairs={{0,2},{2,0},{1,3},{3,1},{4,6},{6,4},{5,7},{7,5},{8,10},{10,8},{9,1... | collective-permute-start | bytes 2162696 | tf_op jit(solution)/shard_map/ppermute | solution.py:179
  38.3 8.0 %collective-permute-start.7 = (f32[672,128]{1,0:T(8,128)S(1)}, f32[672,128]{1,0:T(8,128)S(1)}, u32[]{:S(2)}, u32[]{:S(2)}) collective-permute-start(f32[672,128]{1,0:T(8,128)S(1)} %get-tuple-element.29), channel_id=1, source_target_pairs={{0,1},{1,0},{2,3},{3,2},{4,5},{5,4},{6,7},{7,6},{8,9},{9,8},{10,11... | collective-permute-start | bytes 1032200 | tf_op jit(solution)/shard_map/ppermute | solution.py:179
  39.0 9.3 %collective-permute-start.11 = (f32[672,128]{1,0:T(8,128)S(1)}, f32[672,128]{1,0:T(8,128)S(1)}, u32[]{:S(2)}, u32[]{:S(2)}) collective-permute-start(f32[672,128]{1,0:T(8,128)S(1)} %get-tuple-element.31), channel_id=1, source_target_pairs={{0,2},{2,0},{1,3},{3,1},{4,6},{6,4},{5,7},{7,5},{8,10},{10,8},{9,1... | collective-permute-start | bytes 1032200 | tf_op jit(solution)/shard_map/ppermute | solution.py:179
  40.6 8.8 %collective-permute-start.15 = (f32[704,128]{1,0:T(8,128)S(1)}, f32[704,128]{1,0:T(8,128)S(1)}, u32[]{:S(2)}, u32[]{:S(2)}) collective-permute-start(f32[704,128]{1,0:T(8,128)S(1)} %get-tuple-element.27), channel_id=1, source_target_pairs={{0,16},{16,0},{1,17},{17,1},{2,18},{18,2},{3,19},{19,3},{4,20},{20... | collective-permute-start | bytes 1081352 | tf_op jit(solution)/shard_map/ppermute | solution.py:179
  46.3 5.5 %collective-permute-start.8 = (f32[336,128]{1,0:T(8,128)S(1)}, f32[336,128]{1,0:T(8,128)S(1)}, u32[]{:S(2)}, u32[]{:S(2)}) collective-permute-start(f32[336,128]{1,0:T(8,128)S(1)} %slice_add_fusion.10), channel_id=1, source_target_pairs={{0,2},{2,0},{1,3},{3,1},{4,6},{6,4},{5,7},{7,5},{8,10},{10,8},{9,1... | collective-permute-start | bytes 516104 | tf_op jit(solution)/shard_map/ppermute | solution.py:179
  48.4 5.5 %collective-permute-start.12 = (f32[336,128]{1,0:T(8,128)S(1)}, f32[336,128]{1,0:T(8,128)S(1)}, u32[]{:S(2)}, u32[]{:S(2)}) collective-permute-start(f32[336,128]{1,0:T(8,128)S(1)} %slice_add_fusion.8), channel_id=1, source_target_pairs={{0,16},{16,0},{1,17},{17,1},{2,18},{18,2},{3,19},{19,3},{4,20},{20... | collective-permute-start | bytes 516104 | tf_op jit(solution)/shard_map/ppermute | solution.py:179
  49.4 6.4 %collective-permute-start.16 = (f32[352,128]{1,0:T(8,128)S(1)}, f32[352,128]{1,0:T(8,128)S(1)}, u32[]{:S(2)}, u32[]{:S(2)}) collective-permute-start(f32[352,128]{1,0:T(8,128)S(1)} %slice_add_fusion.6), channel_id=1, source_target_pairs={{0,1},{1,0},{2,3},{3,2},{4,5},{5,4},{6,7},{7,6},{8,9},{9,8},{10,11... | collective-permute-start | bytes 540680 | tf_op jit(solution)/shard_map/ppermute | solution.py:179
  51.8 9.2 %collective-permute-start.9 = (f32[1,168,128]{2,1,0:T(8,128)S(1)}, f32[1,168,128]{2,1,0:T(8,128)S(1)}, u32[]{:S(2)}, u32[]{:S(2)}) collective-permute-start(f32[1,168,128]{2,1,0:T(8,128)S(1)} %slice_bitcast_fusion.4), channel_id=1, source_target_pairs={{0,4},{4,0},{1,5},{5,1},{2,6},{6,2},{3,7},{7,3},{8,12},{12,8},{9,1... | collective-permute-start | bytes 258056 | tf_op jit(solution)/shard_map/ppermute | solution.py:179
  53.9 8.2 %collective-permute-start.13 = (f32[1,168,128]{2,1,0:T(8,128)S(1)}, f32[1,168,128]{2,1,0:T(8,128)S(1)}, u32[]{:S(2)}, u32[]{:S(2)}) collective-permute-start(f32[1,168,128]{2,1,0:T(8,128)S(1)} %slice_bitcast_fusion.2), channel_id=1, source_target_pairs={{0,4},{4,0},{1,5},{5,1},{2,6},{6,2},{3,7},{7,3},{8,12},{12,8},{9,1... | collective-permute-start | bytes 258056 | tf_op jit(solution)/shard_map/ppermute | solution.py:179
  55.9 8.1 %collective-permute-start.17 = (f32[1,176,128]{2,1,0:T(8,128)S(1)}, f32[1,176,128]{2,1,0:T(8,128)S(1)}, u32[]{:S(2)}, u32[]{:S(2)}) collective-permute-start(f32[1,176,128]{2,1,0:T(8,128)S(1)} %slice_bitcast_fusion), channel_id=1, source_target_pairs={{0,4},{4,0},{1,5},{5,1},{2,6},{6,2},{3,7},{7,3},{8,12},{12,8},{9,1... | collective-permute-start | bytes 270344 | tf_op jit(solution)/shard_map/ppermute | solution.py:179
  64.1 1.6 %collective-permute-start.18 = (f32[512,128]{1,0:T(8,128)S(1)}, f32[512,128]{1,0:T(8,128)S(1)}, u32[]{:S(2)}, u32[]{:S(2)}) collective-permute-start(f32[512,128]{1,0:T(8,128)S(1)} %pad_maximum_fusion.own_ref), channel_id=1, source_target_pairs={{0,8},{8,0},{1,9},{9,1},{2,10},{10,2},{3,11},{11,3},{4,12},{12,4},... | collective-permute-start | bytes 786440 | tf_op jit(solution)/shard_map/ppermute | solution.py:179
  66.8 7.3 %collective-permute-start.19 = (f32[4,16,512]{2,1,0:T(8,128)S(1)}, f32[4,16,512]{2,1,0:T(8,128)S(1)}, u32[]{:S(2)}, u32[]{:S(2)}) collective-permute-start(f32[4,16,512]{2,1,0:T(8,128)S(1)} %fusion.5), channel_id=1, source_target_pairs={{0,17},{1,16},{16,1},{17,0},{2,19},{3,18},{18,3},{19,2},{4,21},{5,... | collective-permute-start | bytes 393224 | tf_op jit(solution)/shard_map/ppermute | solution.py:196
  68.7 7.4 %collective-permute-start.20 = (f32[4,16,512]{2,1,0:T(8,128)S(1)}, f32[4,16,512]{2,1,0:T(8,128)S(1)}, u32[]{:S(2)}, u32[]{:S(2)}) collective-permute-start(f32[4,16,512]{2,1,0:T(8,128)S(1)} %fusion.4), channel_id=1, source_target_pairs={{0,16},{1,17},{16,0},{17,1},{2,18},{3,19},{18,2},{19,3},{4,20},{5,... | collective-permute-start | bytes 393224 | tf_op jit(solution)/shard_map/ppermute | solution.py:196
  69.9 6.3 %collective-permute-start.21 = (f32[4,16,512]{2,1,0:T(8,128)S(1)}, f32[4,16,512]{2,1,0:T(8,128)S(1)}, u32[]{:S(2)}, u32[]{:S(2)}) collective-permute-start(f32[4,16,512]{2,1,0:T(8,128)S(1)} %fusion.3), channel_id=1, source_target_pairs={{0,1},{1,0},{16,17},{17,16},{2,3},{3,2},{18,19},{19,18},{4,5},{5,4... | collective-permute-start | bytes 393224 | tf_op jit(solution)/shard_map/ppermute | solution.py:196
  76.2 5.8 %collective-permute-start.22 = (f32[1,16,512]{2,1,0:T(8,128)S(1)}, f32[1,16,512]{2,1,0:T(8,128)S(1)}, u32[]{:S(2)}, u32[]{:S(2)}) collective-permute-start(f32[1,16,512]{2,1,0:T(8,128)S(1)} %slice_select_fusion.14), channel_id=1, source_target_pairs={{0,6},{2,4},{4,2},{6,0},{1,7},{3,5},{5,3},{7,1},{8,14},{10,12},{12... | collective-permute-start | bytes 98312 | tf_op jit(solution)/shard_map/ppermute | solution.py:196
  78.8 4.8 %collective-permute-start.23 = (f32[1,16,512]{2,1,0:T(8,128)S(1)}, f32[1,16,512]{2,1,0:T(8,128)S(1)}, u32[]{:S(2)}, u32[]{:S(2)}) collective-permute-start(f32[1,16,512]{2,1,0:T(8,128)S(1)} %slice_select_fusion.13), channel_id=1, source_target_pairs={{0,4},{2,6},{4,0},{6,2},{1,5},{3,7},{5,1},{7,3},{8,12},{10,14},{12... | collective-permute-start | bytes 98312 | tf_op jit(solution)/shard_map/ppermute | solution.py:196
  78.8 4.8 %collective-permute-start.24 = (f32[1,16,512]{2,1,0:T(8,128)S(1)}, f32[1,16,512]{2,1,0:T(8,128)S(1)}, u32[]{:S(2)}, u32[]{:S(2)}) collective-permute-start(f32[1,16,512]{2,1,0:T(8,128)S(1)} %slice_select_fusion.12), channel_id=1, source_target_pairs={{0,2},{2,0},{4,6},{6,4},{1,3},{3,1},{5,7},{7,5},{8,10},{10,8},{12,... | collective-permute-start | bytes 98312 | tf_op jit(solution)/shard_map/ppermute | solution.py:196

commit v6 on v5

--- a/solution.py
+++ b/solution.py
@@ -104,9 +104,10 @@
 
 def merge(own, oth):
     blocks, _, cols = own.shape
+    tiles = cols // LANES
     return pl.pallas_call(
         merge_kernel,
-        out_shape=jax.ShapeDtypeStruct((2 * blocks * BLOCK * cols // LANES, LANES), jnp.float32),
+        out_shape=jax.ShapeDtypeStruct((2 * blocks * BLOCK * tiles + 8, LANES), jnp.float32),
         in_specs=[VMEM, VMEM],
         out_specs=VMEM,
         compiler_params=limit(4),
@@ -228,7 +229,7 @@
     own_sign = (2 * signs - 1).astype(jnp.float32).reshape(rows // BLOCK, BLOCK)
     oth_design = swap(design, core)
     oth_sign = swap(own_sign, core)
-    listing = steps
+    listing = [steps[-1], *steps[:-1]]
     listed = lax.optimization_barrier(samples ^ (own_index >> len(bits)))
     listed = jnp.concatenate([listed, swap(samples, listing[0])])
     for i, bit in enumerate(listing[1:], 1):

time: 84.4 us -> 83.8 us (level)
  waiting for transfers between devices: 34.7 us -> 32.4 us
  starting transfers between devices: 32.8 us -> 34.5 us
    ppermute x19, waiting for transfers between devices: 26.3 us -> 24.1 us  [swap(): return lax.ppermute(block, bit, [(0, 1), (1, 0)])]
    ppermute x19, starting transfers between devices: 24.7 us -> 26.4 us  [swap(): return lax.ppermute(block, bit, [(0, 1), (1, 0)])]
  transfers between devices with their start and end apart: 25 -> 25, of which waited for: 17 -> 15; matrix products, arithmetic and copies ran while one was open for 2% -> 2% of each run, Pallas kernels for 12% -> 12%
where the time goes in v6:
time: 83.8 us; the launch traced here: 83.6 us
  starting transfers between devices  34.5 us (41%)
  waiting for transfers between devices  32.4 us (39%)
  Pallas kernels  13 us (16%)
  other arithmetic  2.74 us (3%)
  between operations  0.89 us (1%)
    ppermute x19, starting transfers between devices, swap(): return lax.ppermute(block, bit, [(0, 1), (1, 0)])  26.4 us
    ppermute x19, waiting for transfers between devices, swap(): return lax.ppermute(block, bit, [(0, 1), (1, 0)])  24.1 us
    ppermute x6, waiting for transfers between devices, reduce_pairs(): total += lax.ppermute(exclusive(block, own ^ flip, 0), axes, route)  8.35 us
    ppermute x6, starting transfers between devices, reduce_pairs(): total += lax.ppermute(exclusive(block, own ^ flip, 0), axes, route)  8.12 us
    pallas_call x2, Pallas kernels, transform_blocks(): pl.pallas_call(blocks_kernel, out_shape=[jax.ShapeDtypeStruct((blocks, BL...  6.11 us
    pallas_call x2, Pallas kernels, gather(): pl.pallas_call(functools.partial(gather_kernel, plans, tiles), out_shape=...  4.16 us
    pallas_call x1, Pallas kernels, merge(): pl.pallas_call(merge_kernel, out_shape=jax.ShapeDtypeStruct((2 * blocks *...  1.75 us
  transfers between devices with their start and end apart: 25, of which 15 were waited for; matrix products, arithmetic and copies ran while one was open for 2% of the time, Pallas kernels for 12%

profile of v6, /device:TPU:0, one launch (start us, length us, event | category | flops | bytes accessed | tf_op | source)
XLA Modules:
  0.0 83.6 jit_solution(16632654502144406094)
XLA Ops:
  0.6 0.5 collective-permute-start.3
  1.1 3.7 %collective-permute-start = (s32[128]{0:T(128)}, s32[128]{0:T(128)S(1)}, u32[]{:S(2)}, u32[]{:S(2)}) collective-permute-start(s32[128]{0:T(128)} %param.5), channel_id=1, source_target_pairs={{0,4},{4,0},{1,5},{5,1},{2,6},{6,2},{3,7},{7,3},{8,12},{12,8},{9,1... | collective-permute-start | bytes 1544 | tf_op jit(solution)/shard_map/ppermute | solution.py:180
  4.8 0.7 add_convert_fusion
  5.5 0.2 collective-permute-start.4
  5.7 0.7 broadcast_xor_fusion
  6.3 0.1 collective-permute-done
  6.5 1.8 %collective-permute-start.1 = (s32[256]{0:T(256)S(1)}, s32[256]{0:T(256)S(1)}, u32[]{:S(2)}, u32[]{:S(2)}) collective-permute-start(s32[256]{0:T(256)S(1)} %pad_add_fusion.1), channel_id=1, source_target_pairs={{0,16},{16,0},{1,17},{17,1},{2,18},{18,2},{3,19},{19,3},{4,20},{20... | collective-permute-start | bytes 3080 | tf_op jit(solution)/shard_map/ppermute | solution.py:180
  8.3 3.1 %shard_map.50 = (f32[8,256,512]{2,1,0:T(8,128)S(1)}, s32[512]{0:T(512)S(1)}) custom-call(f32[2048,512]{1,0:T(8,128)} %rows_ref.1, f32[8,256]{1,0:T(8,128)S(1)} %reshape.86.sign_ref), custom_call_target="tpu_custom_call" | custom-call | flops 1073741824 | bytes 8388608 | tf_op jit(solution)/shard_map/pallas_call | solution.py:72
  11.4 0.0 collective-permute-done.1
  11.4 1.6 %collective-permute-start.2 = (s32[512]{0:T(512)S(1)}, s32[512]{0:T(512)S(1)}, u32[]{:S(2)}, u32[]{:S(2)}) collective-permute-start(s32[512]{0:T(512)S(1)} %add_add_fusion.1), channel_id=1, source_target_pairs={{0,1},{1,0},{2,3},{3,2},{4,5},{5,4},{6,7},{7,6},{8,9},{9,8},{10,11... | collective-permute-start | bytes 6152 | tf_op jit(solution)/shard_map/ppermute | solution.py:180
  13.0 0.0 collective-permute-done.4.sign_ref
  13.0 0.0 collective-permute-done.3.rows_ref
  13.0 3.1 %shard_map.51 = (f32[8,256,512]{2,1,0:T(8,128)S(1)}, s32[1024]{0:T(1024)S(1)}) custom-call(f32[2048,512]{1,0:T(8,128)} %collective-permute-done.3.rows_ref, f32[8,256]{1,0:T(8,128)S(1)} %collective-permute-done.4.sign_ref), custom_call_target="tpu_custom_call" | custom-call | flops 1073741824 | bytes 8388608 | tf_op jit(solution)/shard_map/pallas_call | solution.py:72
  16.0 0.0 collective-permute-done.2
  16.1 1.6 %collective-permute-start.5 = (s32[1024]{0:T(1024)S(1)}, s32[1024]{0:T(1024)S(1)}, u32[]{:S(2)}, u32[]{:S(2)}) collective-permute-start(s32[1024]{0:T(1024)S(1)} %add_add_fusion), channel_id=1, source_target_pairs={{0,2},{2,0},{1,3},{3,1},{4,6},{6,4},{5,7},{7,5},{8,10},{10,8},{9,1... | collective-permute-start | bytes 12296 | tf_op jit(solution)/shard_map/ppermute | solution.py:180
  17.7 1.7 %shard_map.52.table_ref = f32[16392,128]{1,0:T(8,128)S(1)} custom-call(f32[8,256,512]{2,1,0:T(8,128)S(1)} %get-tuple-element.16.own_ref, f32[8,256,512]{2,1,0:T(8,128)S(1)} %get-tuple-element.17.oth_ref), custom_call_target="tpu_custom_call" | custom-call | flops 10485760 | bytes 16777216 | tf_op jit(solution)/shard_map/pallas_call | solution.py:108
  19.5 0.3 collective-permute-done.5
  19.8 2.1 %shard_map.54 = (f32[1344,128]{1,0:T(8,128)S(1)}, f32[1344,128]{1,0:T(8,128)S(1)}, f32[1408,128]{1,0:T(8,128)S(1)}) custom-call(s32[2048]{0:T(1024)S(1)} %get-tuple-element.41.at_ref, f32[2048]{0:T(1024)S(1)} %get-tuple-element.40.sign_ref, f32[16392,128]{1,0:T(8,128)S(1)} %shard_map.52.table_ref), custom_call_target="tpu_custom_call" | custom-call | bytes 4194304 | tf_op jit(solution)/shard_map/pallas_call | solution.py:140
  21.9 0.6 collective-permute-start.6
  22.5 0.5 collective-permute-start.10
  22.9 1.6 %collective-permute-start.14 = (f32[1408,128]{1,0:T(8,128)S(1)}, f32[1408,128]{1,0:T(8,128)S(1)}, u32[]{:S(2)}, u32[]{:S(2)}) collective-permute-start(f32[1408,128]{1,0:T(8,128)S(1)} %get-tuple-element.23), channel_id=1, source_target_pairs={{0,2},{2,0},{1,3},{3,1},{4,6},{6,4},{5,7},{7,5},{8,10},{10,8},{9,1... | collective-permute-start | bytes 2162696 | tf_op jit(solution)/shard_map/ppermute | solution.py:180
  24.6 2.1 %shard_map.53 = (f32[1344,128]{1,0:T(8,128)S(1)}, f32[1344,128]{1,0:T(8,128)S(1)}, f32[1408,128]{1,0:T(8,128)S(1)}) custom-call(s32[2048]{0:T(1024)S(1)} %get-tuple-element.41.at_ref, f32[2048]{0:T(1024)S(1)} %get-tuple-element.40.sign_ref, f32[16392,128]{1,0:T(8,128)S(1)} %shard_map.52.table_ref), custom_call_target="tpu_custom_call" | custom-call | bytes 4194304 | tf_op jit(solution)/shard_map/pallas_call | solution.py:140
  26.6 11.5 %collective-permute-done.6 = f32[1344,128]{1,0:T(8,128)S(1)} collective-permute-done((f32[1344,128]{1,0:T(8,128)S(1)}, f32[1344,128]{1,0:T(8,128)S(1)}, u32[]{:S(2)}, u32[]{:S(2)}) %collective-permute-start.6) | collective-permute-done | bytes 688160 | tf_op jit(solution)/shard_map/ppermute | solution.py:180
  38.1 0.1 slice_add_fusion.5
  38.2 0.6 collective-permute-start.7
  38.8 0.0 collective-permute-done.10
  38.8 0.1 slice_add_fusion.3
  38.9 1.0 %collective-permute-start.11 = (f32[672,128]{1,0:T(8,128)S(1)}, f32[672,128]{1,0:T(8,128)S(1)}, u32[]{:S(2)}, u32[]{:S(2)}) collective-permute-start(f32[672,128]{1,0:T(8,128)S(1)} %get-tuple-element.31), channel_id=1, source_target_pairs={{0,2},{2,0},{1,3},{3,1},{4,6},{6,4},{5,7},{7,5},{8,10},{10,8},{9,1... | collective-permute-start | bytes 1032200 | tf_op jit(solution)/shard_map/ppermute | solution.py:180
  39.9 0.0 collective-permute-done.14
  39.9 0.1 slice_add_fusion.1
  40.0 2.3 %collective-permute-start.15 = (f32[704,128]{1,0:T(8,128)S(1)}, f32[704,128]{1,0:T(8,128)S(1)}, u32[]{:S(2)}, u32[]{:S(2)}) collective-permute-start(f32[704,128]{1,0:T(8,128)S(1)} %get-tuple-element.27), channel_id=1, source_target_pairs={{0,16},{16,0},{1,17},{17,1},{2,18},{18,2},{3,19},{19,3},{4,20},{20... | collective-permute-start | bytes 1081352 | tf_op jit(solution)/shard_map/ppermute | solution.py:180
  42.2 4.0 %collective-permute-done.7 = f32[672,128]{1,0:T(8,128)S(1)} collective-permute-done((f32[672,128]{1,0:T(8,128)S(1)}, f32[672,128]{1,0:T(8,128)S(1)}, u32[]{:S(2)}, u32[]{:S(2)}) %collective-permute-start.7) | collective-permute-done | bytes 344096 | tf_op jit(solution)/shard_map/ppermute | solution.py:180
  46.2 0.6 collective-permute-start.8
  46.8 0.6 collective-permute-done.11
  47.5 1.4 %collective-permute-start.12 = (f32[336,128]{1,0:T(8,128)S(1)}, f32[336,128]{1,0:T(8,128)S(1)}, u32[]{:S(2)}, u32[]{:S(2)}) collective-permute-start(f32[336,128]{1,0:T(8,128)S(1)} %slice_add_fusion.8), channel_id=1, source_target_pairs={{0,16},{16,0},{1,17},{17,1},{2,18},{18,2},{3,19},{19,3},{4,20},{20... | collective-permute-start | bytes 516104 | tf_op jit(solution)/shard_map/ppermute | solution.py:180
  48.9 0.0 collective-permute-done.15
  48.9 2.6 %collective-permute-start.16 = (f32[352,128]{1,0:T(8,128)S(1)}, f32[352,128]{1,0:T(8,128)S(1)}, u32[]{:S(2)}, u32[]{:S(2)}) collective-permute-start(f32[352,128]{1,0:T(8,128)S(1)} %slice_add_fusion.6), channel_id=1, source_target_pairs={{0,1},{1,0},{2,3},{3,2},{4,5},{5,4},{6,7},{7,6},{8,9},{9,8},{10,11... | collective-permute-start | bytes 540680 | tf_op jit(solution)/shard_map/ppermute | solution.py:180
  51.5 0.1 collective-permute-done.8
  51.7 1.9 %collective-permute-start.9 = (f32[1,168,128]{2,1,0:T(8,128)S(1)}, f32[1,168,128]{2,1,0:T(8,128)S(1)}, u32[]{:S(2)}, u32[]{:S(2)}) collective-permute-start(f32[1,168,128]{2,1,0:T(8,128)S(1)} %slice_bitcast_fusion.4), channel_id=1, source_target_pairs={{0,4},{4,0},{1,5},{5,1},{2,6},{6,2},{3,7},{7,3},{8,12},{12,8},{9,1... | collective-permute-start | bytes 258056 | tf_op jit(solution)/shard_map/ppermute | solution.py:180
  53.6 0.0 collective-permute-done.12
  53.6 2.2 %collective-permute-start.13 = (f32[1,168,128]{2,1,0:T(8,128)S(1)}, f32[1,168,128]{2,1,0:T(8,128)S(1)}, u32[]{:S(2)}, u32[]{:S(2)}) collective-permute-start(f32[1,168,128]{2,1,0:T(8,128)S(1)} %slice_bitcast_fusion.2), channel_id=1, source_target_pairs={{0,4},{4,0},{1,5},{5,1},{2,6},{6,2},{3,7},{7,3},{8,12},{12,8},{9,1... | collective-permute-start | bytes 258056 | tf_op jit(solution)/shard_map/ppermute | solution.py:180
  55.8 0.0 collective-permute-done.16
  55.9 1.7 %collective-permute-start.17 = (f32[1,176,128]{2,1,0:T(8,128)S(1)}, f32[1,176,128]{2,1,0:T(8,128)S(1)}, u32[]{:S(2)}, u32[]{:S(2)}) collective-permute-start(f32[1,176,128]{2,1,0:T(8,128)S(1)} %slice_bitcast_fusion), channel_id=1, source_target_pairs={{0,4},{4,0},{1,5},{5,1},{2,6},{6,2},{3,7},{7,3},{8,12},{12,8},{9,1... | collective-permute-start | bytes 270344 | tf_op jit(solution)/shard_map/ppermute | solution.py:180
  57.6 3.1 %collective-permute-done.9 = f32[1,168,128]{2,1,0:T(8,128)S(1)} collective-permute-done((f32[1,168,128]{2,1,0:T(8,128)S(1)}, f32[1,168,128]{2,1,0:T(8,128)S(1)}, u32[]{:S(2)}, u32[]{:S(2)}) %collective-permute-start.9) | collective-permute-done | bytes 86048 | tf_op jit(solution)/shard_map/ppermute | solution.py:180
  60.7 1.9 %collective-permute-done.13 = f32[1,168,128]{2,1,0:T(8,128)S(1)} collective-permute-done((f32[1,168,128]{2,1,0:T(8,128)S(1)}, f32[1,168,128]{2,1,0:T(8,128)S(1)}, u32[]{:S(2)}, u32[]{:S(2)}) %collective-permute-start.13) | collective-permute-done | bytes 86048 | tf_op jit(solution)/shard_map/ppermute | solution.py:180
  62.6 1.0 %collective-permute-done.17 = f32[1,176,128]{2,1,0:T(8,128)S(1)} collective-permute-done((f32[1,176,128]{2,1,0:T(8,128)S(1)}, f32[1,176,128]{2,1,0:T(8,128)S(1)}, u32[]{:S(2)}, u32[]{:S(2)}) %collective-permute-start.17) | collective-permute-done | bytes 90144 | tf_op jit(solution)/shard_map/ppermute | solution.py:180
  63.6 0.1 collective-permute-start.18
  63.7 1.5 %collective-permute-done.18.oth_ref = f32[512,128]{1,0:T(8,128)S(1)} collective-permute-done((f32[512,128]{1,0:T(8,128)S(1)}, f32[512,128]{1,0:T(8,128)S(1)}, u32[]{:S(2)}, u32[]{:S(2)}) %collective-permute-start.18) | collective-permute-done | bytes 262176 | tf_op jit(solution)/shard_map/ppermute | solution.py:180
  65.2 1.0 %shard_map.55 = (f32[128,512]{1,0:T(8,128)}, f32[256,512]{1,0:T(8,128)S(1)}) custom-call(s32[1]{0:T(128)} %bitcast.core_ref, f32[512,128]{1,0:T(8,128)S(1)} %pad_maximum_fusion.own_ref, f32[512,128]{1,0:T(8,128)S(1)} %collective-permute-done.18.oth_ref), custom_call_target="tpu_custom_call" | custom-call | flops 201326592 | bytes 1048576 | tf_op jit(solution)/shard_map/pallas_call | solution.py:289
  66.2 0.1 slice_select_fusion.3
  66.3 2.6 %collective-permute-start.19 = (f32[4,16,512]{2,1,0:T(8,128)S(1)}, f32[4,16,512]{2,1,0:T(8,128)S(1)}, u32[]{:S(2)}, u32[]{:S(2)}) collective-permute-start(f32[4,16,512]{2,1,0:T(8,128)S(1)} %fusion.5), channel_id=1, source_target_pairs={{0,17},{1,16},{16,1},{17,0},{2,19},{3,18},{18,3},{19,2},{4,21},{5,... | collective-permute-start | bytes 393224 | tf_op jit(solution)/shard_map/ppermute | solution.py:197
  68.9 0.3 collective-permute-start.20
  69.3 0.8 collective-permute-start.21
  70.0 3.6 %collective-permute-done.19 = f32[4,16,512]{2,1,0:T(8,128)S(1)} collective-permute-done((f32[4,16,512]{2,1,0:T(8,128)S(1)}, f32[4,16,512]{2,1,0:T(8,128)S(1)}, u32[]{:S(2)}, u32[]{:S(2)}) %collective-permute-start.19) | collective-permute-done | bytes 131104 | tf_op jit(solution)/shard_map/ppermute | solution.py:197
  73.6 1.9 %collective-permute-done.20 = f32[4,16,512]{2,1,0:T(8,128)S(1)} collective-permute-done((f32[4,16,512]{2,1,0:T(8,128)S(1)}, f32[4,16,512]{2,1,0:T(8,128)S(1)}, u32[]{:S(2)}, u32[]{:S(2)}) %collective-permute-start.20) | collective-permute-done | bytes 131104 | tf_op jit(solution)/shard_map/ppermute | solution.py:197
  75.5 0.1 collective-permute-done.21
  75.7 2.4 %collective-permute-start.22 = (f32[1,16,512]{2,1,0:T(8,128)S(1)}, f32[1,16,512]{2,1,0:T(8,128)S(1)}, u32[]{:S(2)}, u32[]{:S(2)}) collective-permute-start(f32[1,16,512]{2,1,0:T(8,128)S(1)} %slice_select_fusion.14), channel_id=1, source_target_pairs={{0,6},{2,4},{4,2},{6,0},{1,7},{3,5},{5,3},{7,1},{8,14},{10,12},{12... | collective-permute-start | bytes 98312 | tf_op jit(solution)/shard_map/ppermute | solution.py:197
  78.1 0.0 collective-permute-start.23
  78.2 2.0 %collective-permute-start.24 = (f32[1,16,512]{2,1,0:T(8,128)S(1)}, f32[1,16,512]{2,1,0:T(8,128)S(1)}, u32[]{:S(2)}, u32[]{:S(2)}) collective-permute-start(f32[1,16,512]{2,1,0:T(8,128)S(1)} %slice_select_fusion.12), channel_id=1, source_target_pairs={{0,2},{2,0},{4,6},{6,4},{1,3},{3,1},{5,7},{7,5},{8,10},{10,8},{12,... | collective-permute-start | bytes 98312 | tf_op jit(solution)/shard_map/ppermute | solution.py:197
  80.2 1.4 %collective-permute-done.22 = f32[1,16,512]{2,1,0:T(8,128)S(1)} collective-permute-done((f32[1,16,512]{2,1,0:T(8,128)S(1)}, f32[1,16,512]{2,1,0:T(8,128)S(1)}, u32[]{:S(2)}, u32[]{:S(2)}) %collective-permute-start.22) | collective-permute-done | bytes 32800 | tf_op jit(solution)/shard_map/ppermute | solution.py:197
  81.6 1.4 %collective-permute-done.23 = f32[1,16,512]{2,1,0:T(8,128)S(1)} collective-permute-done((f32[1,16,512]{2,1,0:T(8,128)S(1)}, f32[1,16,512]{2,1,0:T(8,128)S(1)}, u32[]{:S(2)}, u32[]{:S(2)}) %collective-permute-start.23) | collective-permute-done | bytes 32800 | tf_op jit(solution)/shard_map/ppermute | solution.py:197
  83.0 0.0 collective-permute-done.24
  83.0 0.6 fusion.19
  (27 shorter events, 0.5 us)
Async XLA Ops:
  0.6 12.3 %collective-permute-start.3 = (f32[2048,512]{1,0:T(8,128)}, f32[2048,512]{1,0:T(8,128)}, u32[]{:S(2)}, u32[]{:S(2)}) collective-permute-start(f32[2048,512]{1,0:T(8,128)} %rows_ref.1), channel_id=1, source_target_pairs={{0,8},{8,0},{1,9},{9,1},{2,10},{10,2},{3,11},{11,3},{4,12},{12,4},... | collective-permute-start | bytes 12582920 | tf_op jit(solution)/shard_map/ppermute | solution.py:180
  1.1 5.3 %collective-permute-start = (s32[128]{0:T(128)}, s32[128]{0:T(128)S(1)}, u32[]{:S(2)}, u32[]{:S(2)}) collective-permute-start(s32[128]{0:T(128)} %param.5), channel_id=1, source_target_pairs={{0,4},{4,0},{1,5},{5,1},{2,6},{6,2},{3,7},{7,3},{8,12},{12,8},{9,1... | collective-permute-start | bytes 1544 | tf_op jit(solution)/shard_map/ppermute | solution.py:180
  5.5 7.5 %collective-permute-start.4 = (f32[8,256]{1,0:T(8,128)S(1)}, f32[8,256]{1,0:T(8,128)S(1)}, u32[]{:S(2)}, u32[]{:S(2)}) collective-permute-start(f32[8,256]{1,0:T(8,128)S(1)} %reshape.86.sign_ref), channel_id=1, source_target_pairs={{0,8},{8,0},{1,9},{9,1},{2,10},{10,2},{3,11},{11,3},{4,12},{12,4},... | collective-permute-start | bytes 24584 | tf_op jit(solution)/shard_map/ppermute | solution.py:180
  6.5 4.9 %collective-permute-start.1 = (s32[256]{0:T(256)S(1)}, s32[256]{0:T(256)S(1)}, u32[]{:S(2)}, u32[]{:S(2)}) collective-permute-start(s32[256]{0:T(256)S(1)} %pad_add_fusion.1), channel_id=1, source_target_pairs={{0,16},{16,0},{1,17},{17,1},{2,18},{18,2},{3,19},{19,3},{4,20},{20... | collective-permute-start | bytes 3080 | tf_op jit(solution)/shard_map/ppermute | solution.py:180
  11.4 4.7 %collective-permute-start.2 = (s32[512]{0:T(512)S(1)}, s32[512]{0:T(512)S(1)}, u32[]{:S(2)}, u32[]{:S(2)}) collective-permute-start(s32[512]{0:T(512)S(1)} %add_add_fusion.1), channel_id=1, source_target_pairs={{0,1},{1,0},{2,3},{3,2},{4,5},{5,4},{6,7},{7,6},{8,9},{9,8},{10,11... | collective-permute-start | bytes 6152 | tf_op jit(solution)/shard_map/ppermute | solution.py:180
  16.1 3.7 %collective-permute-start.5 = (s32[1024]{0:T(1024)S(1)}, s32[1024]{0:T(1024)S(1)}, u32[]{:S(2)}, u32[]{:S(2)}) collective-permute-start(s32[1024]{0:T(1024)S(1)} %add_add_fusion), channel_id=1, source_target_pairs={{0,2},{2,0},{1,3},{3,1},{4,6},{6,4},{5,7},{7,5},{8,10},{10,8},{9,1... | collective-permute-start | bytes 12296 | tf_op jit(solution)/shard_map/ppermute | solution.py:180
  21.9 16.3 %collective-permute-start.6 = (f32[1344,128]{1,0:T(8,128)S(1)}, f32[1344,128]{1,0:T(8,128)S(1)}, u32[]{:S(2)}, u32[]{:S(2)}) collective-permute-start(f32[1344,128]{1,0:T(8,128)S(1)} %get-tuple-element.19), channel_id=1, source_target_pairs={{0,16},{16,0},{1,17},{17,1},{2,18},{18,2},{3,19},{19,3},{4,20},{20... | collective-permute-start | bytes 2064392 | tf_op jit(solution)/shard_map/ppermute | solution.py:180
  22.5 16.3 %collective-permute-start.10 = (f32[1344,128]{1,0:T(8,128)S(1)}, f32[1344,128]{1,0:T(8,128)S(1)}, u32[]{:S(2)}, u32[]{:S(2)}) collective-permute-start(f32[1344,128]{1,0:T(8,128)S(1)} %get-tuple-element.21), channel_id=1, source_target_pairs={{0,1},{1,0},{2,3},{3,2},{4,5},{5,4},{6,7},{7,6},{8,9},{9,8},{10,11... | collective-permute-start | bytes 2064392 | tf_op jit(solution)/shard_map/ppermute | solution.py:180
  22.9 16.9 %collective-permute-start.14 = (f32[1408,128]{1,0:T(8,128)S(1)}, f32[1408,128]{1,0:T(8,128)S(1)}, u32[]{:S(2)}, u32[]{:S(2)}) collective-permute-start(f32[1408,128]{1,0:T(8,128)S(1)} %get-tuple-element.23), channel_id=1, source_target_pairs={{0,2},{2,0},{1,3},{3,1},{4,6},{6,4},{5,7},{7,5},{8,10},{10,8},{9,1... | collective-permute-start | bytes 2162696 | tf_op jit(solution)/shard_map/ppermute | solution.py:180
  38.2 8.0 %collective-permute-start.7 = (f32[672,128]{1,0:T(8,128)S(1)}, f32[672,128]{1,0:T(8,128)S(1)}, u32[]{:S(2)}, u32[]{:S(2)}) collective-permute-start(f32[672,128]{1,0:T(8,128)S(1)} %get-tuple-element.29), channel_id=1, source_target_pairs={{0,1},{1,0},{2,3},{3,2},{4,5},{5,4},{6,7},{7,6},{8,9},{9,8},{10,11... | collective-permute-start | bytes 1032200 | tf_op jit(solution)/shard_map/ppermute | solution.py:180
  38.9 8.6 %collective-permute-start.11 = (f32[672,128]{1,0:T(8,128)S(1)}, f32[672,128]{1,0:T(8,128)S(1)}, u32[]{:S(2)}, u32[]{:S(2)}) collective-permute-start(f32[672,128]{1,0:T(8,128)S(1)} %get-tuple-element.31), channel_id=1, source_target_pairs={{0,2},{2,0},{1,3},{3,1},{4,6},{6,4},{5,7},{7,5},{8,10},{10,8},{9,1... | collective-permute-start | bytes 1032200 | tf_op jit(solution)/shard_map/ppermute | solution.py:180
  40.0 8.9 %collective-permute-start.15 = (f32[704,128]{1,0:T(8,128)S(1)}, f32[704,128]{1,0:T(8,128)S(1)}, u32[]{:S(2)}, u32[]{:S(2)}) collective-permute-start(f32[704,128]{1,0:T(8,128)S(1)} %get-tuple-element.27), channel_id=1, source_target_pairs={{0,16},{16,0},{1,17},{17,1},{2,18},{18,2},{3,19},{19,3},{4,20},{20... | collective-permute-start | bytes 1081352 | tf_op jit(solution)/shard_map/ppermute | solution.py:180
  46.2 5.5 %collective-permute-start.8 = (f32[336,128]{1,0:T(8,128)S(1)}, f32[336,128]{1,0:T(8,128)S(1)}, u32[]{:S(2)}, u32[]{:S(2)}) collective-permute-start(f32[336,128]{1,0:T(8,128)S(1)} %slice_add_fusion.10), channel_id=1, source_target_pairs={{0,2},{2,0},{1,3},{3,1},{4,6},{6,4},{5,7},{7,5},{8,10},{10,8},{9,1... | collective-permute-start | bytes 516104 | tf_op jit(solution)/shard_map/ppermute | solution.py:180
  47.5 6.1 %collective-permute-start.12 = (f32[336,128]{1,0:T(8,128)S(1)}, f32[336,128]{1,0:T(8,128)S(1)}, u32[]{:S(2)}, u32[]{:S(2)}) collective-permute-start(f32[336,128]{1,0:T(8,128)S(1)} %slice_add_fusion.8), channel_id=1, source_target_pairs={{0,16},{16,0},{1,17},{17,1},{2,18},{18,2},{3,19},{19,3},{4,20},{20... | collective-permute-start | bytes 516104 | tf_op jit(solution)/shard_map/ppermute | solution.py:180
  48.9 6.9 %collective-permute-start.16 = (f32[352,128]{1,0:T(8,128)S(1)}, f32[352,128]{1,0:T(8,128)S(1)}, u32[]{:S(2)}, u32[]{:S(2)}) collective-permute-start(f32[352,128]{1,0:T(8,128)S(1)} %slice_add_fusion.6), channel_id=1, source_target_pairs={{0,1},{1,0},{2,3},{3,2},{4,5},{5,4},{6,7},{7,6},{8,9},{9,8},{10,11... | collective-permute-start | bytes 540680 | tf_op jit(solution)/shard_map/ppermute | solution.py:180
  51.7 8.9 %collective-permute-start.9 = (f32[1,168,128]{2,1,0:T(8,128)S(1)}, f32[1,168,128]{2,1,0:T(8,128)S(1)}, u32[]{:S(2)}, u32[]{:S(2)}) collective-permute-start(f32[1,168,128]{2,1,0:T(8,128)S(1)} %slice_bitcast_fusion.4), channel_id=1, source_target_pairs={{0,4},{4,0},{1,5},{5,1},{2,6},{6,2},{3,7},{7,3},{8,12},{12,8},{9,1... | collective-permute-start | bytes 258056 | tf_op jit(solution)/shard_map/ppermute | solution.py:180
  53.6 8.9 %collective-permute-start.13 = (f32[1,168,128]{2,1,0:T(8,128)S(1)}, f32[1,168,128]{2,1,0:T(8,128)S(1)}, u32[]{:S(2)}, u32[]{:S(2)}) collective-permute-start(f32[1,168,128]{2,1,0:T(8,128)S(1)} %slice_bitcast_fusion.2), channel_id=1, source_target_pairs={{0,4},{4,0},{1,5},{5,1},{2,6},{6,2},{3,7},{7,3},{8,12},{12,8},{9,1... | collective-permute-start | bytes 258056 | tf_op jit(solution)/shard_map/ppermute | solution.py:180
  55.9 7.6 %collective-permute-start.17 = (f32[1,176,128]{2,1,0:T(8,128)S(1)}, f32[1,176,128]{2,1,0:T(8,128)S(1)}, u32[]{:S(2)}, u32[]{:S(2)}) collective-permute-start(f32[1,176,128]{2,1,0:T(8,128)S(1)} %slice_bitcast_fusion), channel_id=1, source_target_pairs={{0,4},{4,0},{1,5},{5,1},{2,6},{6,2},{3,7},{7,3},{8,12},{12,8},{9,1... | collective-permute-start | bytes 270344 | tf_op jit(solution)/shard_map/ppermute | solution.py:180
  63.6 1.6 %collective-permute-start.18 = (f32[512,128]{1,0:T(8,128)S(1)}, f32[512,128]{1,0:T(8,128)S(1)}, u32[]{:S(2)}, u32[]{:S(2)}) collective-permute-start(f32[512,128]{1,0:T(8,128)S(1)} %pad_maximum_fusion.own_ref), channel_id=1, source_target_pairs={{0,8},{8,0},{1,9},{9,1},{2,10},{10,2},{3,11},{11,3},{4,12},{12,4},... | collective-permute-start | bytes 786440 | tf_op jit(solution)/shard_map/ppermute | solution.py:180
  66.3 7.3 %collective-permute-start.19 = (f32[4,16,512]{2,1,0:T(8,128)S(1)}, f32[4,16,512]{2,1,0:T(8,128)S(1)}, u32[]{:S(2)}, u32[]{:S(2)}) collective-permute-start(f32[4,16,512]{2,1,0:T(8,128)S(1)} %fusion.5), channel_id=1, source_target_pairs={{0,17},{1,16},{16,1},{17,0},{2,19},{3,18},{18,3},{19,2},{4,21},{5,... | collective-permute-start | bytes 393224 | tf_op jit(solution)/shard_map/ppermute | solution.py:197
  68.9 6.6 %collective-permute-start.20 = (f32[4,16,512]{2,1,0:T(8,128)S(1)}, f32[4,16,512]{2,1,0:T(8,128)S(1)}, u32[]{:S(2)}, u32[]{:S(2)}) collective-permute-start(f32[4,16,512]{2,1,0:T(8,128)S(1)} %fusion.4), channel_id=1, source_target_pairs={{0,16},{1,17},{16,0},{17,1},{2,18},{3,19},{18,2},{19,3},{4,20},{5,... | collective-permute-start | bytes 393224 | tf_op jit(solution)/shard_map/ppermute | solution.py:197
  69.3 6.4 %collective-permute-start.21 = (f32[4,16,512]{2,1,0:T(8,128)S(1)}, f32[4,16,512]{2,1,0:T(8,128)S(1)}, u32[]{:S(2)}, u32[]{:S(2)}) collective-permute-start(f32[4,16,512]{2,1,0:T(8,128)S(1)} %fusion.3), channel_id=1, source_target_pairs={{0,1},{1,0},{16,17},{17,16},{2,3},{3,2},{18,19},{19,18},{4,5},{5,4... | collective-permute-start | bytes 393224 | tf_op jit(solution)/shard_map/ppermute | solution.py:197
  75.7 5.9 %collective-permute-start.22 = (f32[1,16,512]{2,1,0:T(8,128)S(1)}, f32[1,16,512]{2,1,0:T(8,128)S(1)}, u32[]{:S(2)}, u32[]{:S(2)}) collective-permute-start(f32[1,16,512]{2,1,0:T(8,128)S(1)} %slice_select_fusion.14), channel_id=1, source_target_pairs={{0,6},{2,4},{4,2},{6,0},{1,7},{3,5},{5,3},{7,1},{8,14},{10,12},{12... | collective-permute-start | bytes 98312 | tf_op jit(solution)/shard_map/ppermute | solution.py:197
  78.1 4.8 %collective-permute-start.23 = (f32[1,16,512]{2,1,0:T(8,128)S(1)}, f32[1,16,512]{2,1,0:T(8,128)S(1)}, u32[]{:S(2)}, u32[]{:S(2)}) collective-permute-start(f32[1,16,512]{2,1,0:T(8,128)S(1)} %slice_select_fusion.13), channel_id=1, source_target_pairs={{0,4},{2,6},{4,0},{6,2},{1,5},{3,7},{5,1},{7,3},{8,12},{10,14},{12... | collective-permute-start | bytes 98312 | tf_op jit(solution)/shard_map/ppermute | solution.py:197
  78.2 4.8 %collective-permute-start.24 = (f32[1,16,512]{2,1,0:T(8,128)S(1)}, f32[1,16,512]{2,1,0:T(8,128)S(1)}, u32[]{:S(2)}, u32[]{:S(2)}) collective-permute-start(f32[1,16,512]{2,1,0:T(8,128)S(1)} %slice_select_fusion.12), channel_id=1, source_target_pairs={{0,2},{2,0},{4,6},{6,4},{1,3},{3,1},{5,7},{7,5},{8,10},{10,8},{12,... | collective-permute-start | bytes 98312 | tf_op jit(solution)/shard_map/ppermute | solution.py:197
